TPU v7x, 32 devices: a whole 2x2x4 slice. The times are simulated.
32 devices in a mesh: dp: 8 (over z, y), mp: 4 (over x, core).
Axes of the slice: x: 2, y: 2, z: 4, core: 2. Of those that a mesh axis runs over, the one named last changes fastest.
Arguments:
- tokens: bfloat16 [8192, 768], P(('dp', 'mp')), may hold values from -6 to 6
- memory: bfloat16 [6272, 768], P(('dp', 'mp')), may hold values from -6 to 6
- split_point: int32 [32], P('dp'), may hold values from 0 to 32
- text_length: int32 [32], P('dp'), may hold values from 128 to 256
- patch_mask: int32 [32, 196], P('dp'), may hold values 0 or 1
- query_weight: bfloat16 [768, 768], P('dp', 'mp'), may hold values from -0.21875 to 0.21875
- query_bias: bfloat16 [768], P('mp'), may hold values from -3 to 3
- key_weight: bfloat16 [768, 768], P('dp', 'mp'), may hold values from -0.21875 to 0.21875
- value_weight: bfloat16 [768, 768], P('dp', 'mp'), may hold values from -0.21875 to 0.21875
- value_bias: bfloat16 [768], P('mp'), may hold values from -3 to 3
- out_weight: bfloat16 [768, 768], P('mp', 'dp'), may hold values from -1.75 to 1.75
- out_bias: bfloat16 [768], replicated, may hold values from -2 to 2
- attn_gain: bfloat16 [768], replicated, may hold values from 0.099609375 to 1.8984375
- attn_shift: bfloat16 [768], replicated, may hold values from -2 to 2
- mlp_gain: bfloat16 [768], replicated, may hold values from 0.099609375 to 1.8984375
- mlp_shift: bfloat16 [768], replicated, may hold values from -2 to 2
- up_weight: bfloat16 [768, 3072], P('dp', 'mp'), may hold values from -0.21875 to 0.21875
- up_bias: bfloat16 [3072], P('mp'), may hold values from -3 to 3
- down_weight: bfloat16 [3072, 768], P('mp', 'dp'), may hold values from -0.109375 to 0.109375
- down_bias: bfloat16 [768], replicated, may hold values from -2 to 2
- cotangent: bfloat16 [8192, 768], P(('dp', 'mp')), may hold values from -6 to 6
Outputs:
- layer_out: bfloat16 [8192, 768], P(('dp', 'mp'))
- input_grad: float32 [8192, 768], P(('dp', 'mp'))
- memory_grad: float32 [6272, 768], P(('dp', 'mp'))
- query_weight_grad: float32 [768, 768], P('dp', 'mp')
- key_weight_grad: float32 [768, 768], P('dp', 'mp')
- value_weight_grad: float32 [768, 768], P('dp', 'mp')
- out_weight_grad: float32 [768, 768], P('mp', 'dp')
- up_weight_grad: float32 [768, 3072], P('dp', 'mp')
- down_weight_grad: float32 [3072, 768], P('mp', 'dp')
- query_bias_grad: float32 [768], P(('dp', 'mp'))
- value_bias_grad: float32 [768], P(('dp', 'mp'))
- up_bias_grad: float32 [3072], P(('dp', 'mp'))
- out_bias_grad: float32 [768], P(('dp', 'mp'))
- down_bias_grad: float32 [768], P(('dp', 'mp'))
- attn_gain_grad: float32 [768], P(('dp', 'mp'))
- attn_shift_grad: float32 [768], P(('dp', 'mp'))
- mlp_gain_grad: float32 [768], P(('dp', 'mp'))
- mlp_shift_grad: float32 [768], P(('dp', 'mp'))
Inputs may be any that keep to these rules, and one draw needn't show every extreme that they name: `split_point`: never exceeds the same example's text_length.
All inputs are finite; a program needn't handle non-finite values. No bound on the sum of `patch_mask` on one device may be relied on, other than what follows from the above.
Results may differ from a plain program's by a relative error of at most 0.02.
Values may be sent and summed in bfloat16 or wider, within the bound.
No kernel may reach another device: no remote copies, remote signals or barrier semaphores. Data moves between devices by JAX's collectives and lax.ppermute only.
A program may use at most 128 MiB of HBM per device.

v0:
```python
import math

import jax
import jax.numpy as jnp
from jax import lax
from jax.sharding import PartitionSpec as P

HEAD = 64
TEXT = 256
PATCHES = 196


epsilon = 1e-06
neg_fill = -1000000000.0


def normalize(matrix):
    average = jnp.mean(matrix, axis=-1, keepdims=True)
    centered = matrix - average
    inverse = lax.rsqrt(jnp.mean(centered * centered, axis=-1, keepdims=True) + epsilon)
    return (centered * inverse, inverse)


def normalize_back(normed, inverse, grad_out, gain):
    scaled = grad_out * gain
    return inverse * (
        scaled
        - jnp.mean(scaled, axis=-1, keepdims=True)
        - normed * jnp.mean(scaled * normed, axis=-1, keepdims=True)
    )


def build_mask(split_block, length_block, patch_block, text_len):
    places = jnp.arange(text_len, dtype=jnp.int32)
    key_place = places[None, None, :]
    query_place = places[None, :, None]
    text_ok = ((key_place < split_block[:, None, None]) | (key_place <= query_place)) & (
        key_place < length_block[:, None, None]
    )
    patch_ok = jnp.broadcast_to(
        patch_block[:, None, :] > 0, (patch_block.shape[0], text_len, patch_block.shape[1])
    )
    return jnp.concatenate([patch_ok, text_ok], axis=2)


def masked_scores(query_blk, key_blk, allowed, score_scale):
    scores = (
        jnp.einsum("glhe,gshe->ghls", query_blk, key_blk, preferred_element_type=jnp.float32)
        * score_scale
    )
    return jnp.where(allowed[:, None], scores, neg_fill)


def per_device(
    tokens,
    memory,
    split_point,
    text_length,
    patch_mask,
    query_weight,
    query_bias,
    key_weight,
    value_weight,
    value_bias,
    out_weight,
    out_bias,
    attn_gain,
    attn_shift,
    mlp_gain,
    mlp_shift,
    up_weight,
    up_bias,
    down_weight,
    down_bias,
    cotangent,
):
    examples = split_point.shape[0]
    features = tokens.shape[1]
    local_width = query_weight.shape[1]
    heads_here = local_width // HEAD
    score_scale = HEAD ** (-0.5)
    group_size = math.gcd(examples, max(1, 512 // TEXT))
    group_count = examples // group_size
    key_span = PATCHES + TEXT
    group_rows = examples * TEXT
    mp_count = lax.axis_size("mp")
    full_query, full_key, full_value, full_out, full_up, full_down = (
        lax.all_gather(query_weight, "dp", axis=0, tiled=True),
        lax.all_gather(key_weight, "dp", axis=0, tiled=True),
        lax.all_gather(value_weight, "dp", axis=0, tiled=True),
        lax.all_gather(out_weight, "dp", axis=1, tiled=True),
        lax.all_gather(up_weight, "dp", axis=0, tiled=True),
        lax.all_gather(down_weight, "dp", axis=1, tiled=True),
    )
    gain_one = attn_gain.astype(jnp.float32)
    shift_one = attn_shift.astype(jnp.float32)
    gain_two = mlp_gain.astype(jnp.float32)
    shift_two = mlp_shift.astype(jnp.float32)
    text_in = tokens.astype(jnp.float32)
    memory_in = memory.astype(jnp.float32)
    text_normed, text_inverse = normalize(text_in)
    memory_normed, memory_inverse = normalize(memory_in)
    text_low = (text_normed * gain_one + shift_one).astype(jnp.bfloat16)
    memory_low = (memory_normed * gain_one + shift_one).astype(jnp.bfloat16)
    text_all, memory_all = (
        lax.all_gather(text_low, "mp", axis=0, tiled=True),
        lax.all_gather(memory_low, "mp", axis=0, tiled=True),
    )
    query_rows = (
        jnp.dot(text_all, full_query, preferred_element_type=jnp.float32)
        + query_bias.astype(jnp.float32)
    ).astype(jnp.bfloat16)
    joined = jnp.concatenate(
        [
            memory_all.reshape(examples, PATCHES, features),
            text_all.reshape(examples, TEXT, features),
        ],
        axis=1,
    )
    key_rows = jnp.einsum(
        "gsd,df->gsf", joined, full_key, preferred_element_type=jnp.float32
    ).astype(jnp.bfloat16)
    value_rows = (
        jnp.einsum("gsd,df->gsf", joined, full_value, preferred_element_type=jnp.float32)
        + value_bias.astype(jnp.float32)
    ).astype(jnp.bfloat16)
    query_blocks = query_rows.reshape(group_count, group_size, TEXT, heads_here, HEAD)
    key_blocks = key_rows.reshape(group_count, group_size, key_span, heads_here, HEAD)
    value_blocks = value_rows.reshape(group_count, group_size, key_span, heads_here, HEAD)
    split_blocks = split_point.reshape(group_count, group_size)
    length_blocks = text_length.reshape(group_count, group_size)
    patch_blocks = patch_mask.reshape(group_count, group_size, PATCHES)

    def attend(bundle):
        query_blk, key_blk, value_blk, split_blk, length_blk, patch_blk = bundle
        allowed = build_mask(split_blk, length_blk, patch_blk, TEXT)
        scores = masked_scores(query_blk, key_blk, allowed, score_scale)
        largest = jnp.max(scores, axis=-1, keepdims=True)
        log_total = largest + jnp.log(jnp.sum(jnp.exp(scores - largest), axis=-1, keepdims=True))
        weights_low = jnp.exp(scores - log_total).astype(jnp.bfloat16)
        context_blk = jnp.einsum(
            "ghls,gshe->glhe", weights_low, value_blk, preferred_element_type=jnp.float32
        ).astype(jnp.bfloat16)
        return (context_blk, log_total)

    context_blocks, log_totals = lax.map(
        attend, (query_blocks, key_blocks, value_blocks, split_blocks, length_blocks, patch_blocks)
    )
    context = context_blocks.reshape(group_rows, local_width)
    picked = context
    attn_sum = lax.psum_scatter(
        jnp.dot(picked, full_out, preferred_element_type=jnp.float32).astype(jnp.bfloat16),
        "mp",
        scatter_dimension=0,
        tiled=True,
    ).astype(jnp.float32)
    residual = text_in + attn_sum + out_bias.astype(jnp.float32)
    mid_normed, mid_inverse = normalize(residual)
    mid_low = (mid_normed * gain_two + shift_two).astype(jnp.bfloat16)
    mid_all = lax.all_gather(mid_low, "mp", axis=0, tiled=True)
    pre_act = jnp.dot(mid_all, full_up, preferred_element_type=jnp.float32) + up_bias.astype(
        jnp.float32
    )
    hidden = jax.nn.gelu(pre_act).astype(jnp.bfloat16)
    picked = hidden
    layer_out = (
        residual
        + lax.psum_scatter(
            jnp.dot(picked, full_down, preferred_element_type=jnp.float32).astype(jnp.bfloat16),
            "mp",
            scatter_dimension=0,
            tiled=True,
        ).astype(jnp.float32)
        + down_bias.astype(jnp.float32)
    )
    cot_all = lax.all_gather(cotangent, "mp", axis=0, tiled=True)
    hidden_grad = jnp.einsum("nd,fd->nf", cot_all, full_down, preferred_element_type=jnp.float32)
    down_grad = jnp.einsum("nf,nd->fd", hidden, cot_all, preferred_element_type=jnp.float32)
    gelu_pull = jax.vjp(jax.nn.gelu, pre_act)[1]
    pre_grad = gelu_pull(hidden_grad)[0].astype(jnp.bfloat16)
    up_grad = jnp.einsum("nd,nf->df", mid_all, pre_grad, preferred_element_type=jnp.float32)
    up_bias_part = jnp.sum(pre_grad.astype(jnp.float32), axis=0)
    picked = pre_grad
    mid_grad = lax.psum_scatter(
        jnp.einsum("nf,df->nd", picked, full_up, preferred_element_type=jnp.float32).astype(
            jnp.bfloat16
        ),
        "mp",
        scatter_dimension=0,
        tiled=True,
    ).astype(jnp.float32)
    cot_in = cotangent.astype(jnp.float32)
    resid_grad = cot_in + normalize_back(mid_normed, mid_inverse, mid_grad, gain_two)
    mlp_gain_part = jnp.sum(mid_grad * mid_normed, axis=0)
    mlp_shift_part = jnp.sum(mid_grad, axis=0)
    down_bias_part = jnp.sum(cot_in, axis=0)
    resid_low = resid_grad.astype(jnp.bfloat16)
    out_bias_part = jnp.sum(resid_low.astype(jnp.float32), axis=0)
    resid_all = lax.all_gather(resid_low, "mp", axis=0, tiled=True)
    out_grad = jnp.einsum("nf,nd->fd", context, resid_all, preferred_element_type=jnp.float32)
    context_grad = jnp.einsum(
        "nd,fd->nf", resid_all, full_out, preferred_element_type=jnp.float32
    ).astype(jnp.bfloat16)
    context_grad_blocks = context_grad.reshape(group_count, group_size, TEXT, heads_here, HEAD)

    def attend_back(bundle):
        query_blk, key_blk, value_blk, ctx_grad_blk, log_total, split_blk, length_blk, patch_blk = (
            bundle
        )
        allowed = build_mask(split_blk, length_blk, patch_blk, TEXT)
        scores = masked_scores(query_blk, key_blk, allowed, score_scale)
        weights = jnp.exp(scores - log_total)
        weights_low = weights.astype(jnp.bfloat16)
        weight_grad = jnp.einsum(
            "glhe,gshe->ghls", ctx_grad_blk, value_blk, preferred_element_type=jnp.float32
        )
        row_dot = jnp.sum(weights * weight_grad, axis=-1, keepdims=True)
        score_grad = (weights * (weight_grad - row_dot)).astype(jnp.bfloat16)
        query_grad = (
            jnp.einsum("ghls,gshe->glhe", score_grad, key_blk, preferred_element_type=jnp.float32)
            * score_scale
        ).astype(jnp.bfloat16)
        key_grad = (
            jnp.einsum("ghls,glhe->gshe", score_grad, query_blk, preferred_element_type=jnp.float32)
            * score_scale
        ).astype(jnp.bfloat16)
        value_grad = jnp.einsum(
            "ghls,glhe->gshe", weights_low, ctx_grad_blk, preferred_element_type=jnp.float32
        ).astype(jnp.bfloat16)
        return (query_grad, key_grad, value_grad)

    query_grads, key_grads, value_grads = lax.map(
        attend_back,
        (
            query_blocks,
            key_blocks,
            value_blocks,
            context_grad_blocks,
            log_totals,
            split_blocks,
            length_blocks,
            patch_blocks,
        ),
    )
    query_grads = query_grads.reshape(group_rows, local_width)
    key_grads = key_grads.reshape(examples, key_span, local_width)
    value_grads = value_grads.reshape(examples, key_span, local_width)
    query_weight_part = jnp.einsum(
        "nd,nf->df", text_all, query_grads, preferred_element_type=jnp.float32
    )
    query_bias_part = jnp.sum(query_grads.astype(jnp.float32), axis=0)
    key_weight_part = jnp.einsum(
        "gsd,gsf->df", joined, key_grads, preferred_element_type=jnp.float32
    )
    value_weight_part = jnp.einsum(
        "gsd,gsf->df", joined, value_grads, preferred_element_type=jnp.float32
    )
    value_bias_part = jnp.sum(value_grads.astype(jnp.float32), axis=(0, 1))
    text_grad = jnp.einsum("nf,df->nd", query_grads, full_query, preferred_element_type=jnp.float32)
    text_grad = text_grad + jnp.einsum(
        "gsf,df->gsd", key_grads[:, PATCHES:], full_key, preferred_element_type=jnp.float32
    ).reshape(group_rows, features)
    text_grad = text_grad + jnp.einsum(
        "gsf,df->gsd", value_grads[:, PATCHES:], full_value, preferred_element_type=jnp.float32
    ).reshape(group_rows, features)
    memory_part = jnp.einsum(
        "gsf,df->gsd", key_grads[:, :PATCHES], full_key, preferred_element_type=jnp.float32
    )
    memory_part = memory_part + jnp.einsum(
        "gsf,df->gsd", value_grads[:, :PATCHES], full_value, preferred_element_type=jnp.float32
    )
    memory_part = memory_part.reshape(examples * PATCHES, features)
    text_back, memory_back = (
        lax.psum_scatter(
            text_grad.astype(jnp.bfloat16), "mp", scatter_dimension=0, tiled=True
        ).astype(jnp.float32),
        lax.psum_scatter(
            memory_part.astype(jnp.bfloat16), "mp", scatter_dimension=0, tiled=True
        ).astype(jnp.float32),
    )
    mp_place = lax.axis_index("mp")
    query_bias_full = lax.dynamic_update_slice(
        jnp.zeros((features,), jnp.float32), query_bias_part, (mp_place * local_width,)
    )
    value_bias_full = lax.dynamic_update_slice(
        jnp.zeros((features,), jnp.float32), value_bias_part, (mp_place * local_width,)
    )
    query_sum, key_sum, value_sum, out_sum = (
        lax.psum_scatter(query_weight_part, "dp", scatter_dimension=0, tiled=True),
        lax.psum_scatter(key_weight_part, "dp", scatter_dimension=0, tiled=True),
        lax.psum_scatter(value_weight_part, "dp", scatter_dimension=0, tiled=True),
        lax.psum_scatter(out_grad, "dp", scatter_dimension=1, tiled=True),
    )
    input_grad = resid_grad + normalize_back(text_normed, text_inverse, text_back, gain_one)
    memory_grad = normalize_back(memory_normed, memory_inverse, memory_back, gain_one)
    attn_gain_part = jnp.sum(text_back * text_normed, axis=0) + jnp.sum(
        memory_back * memory_normed, axis=0
    )
    attn_shift_part = jnp.sum(text_back, axis=0) + jnp.sum(memory_back, axis=0)
    mp_index = lax.axis_index("mp")
    up_width = up_bias.shape[0]
    up_bias_full = lax.dynamic_update_slice(
        jnp.zeros((up_width * mp_count,), jnp.float32), up_bias_part, (mp_index * up_width,)
    )
    vector_stack = jnp.stack(
        [
            attn_gain_part,
            attn_shift_part,
            mlp_gain_part,
            mlp_shift_part,
            out_bias_part,
            down_bias_part,
            query_bias_full,
            value_bias_full,
        ]
    )
    vector_sums, up_bias_sum = (
        lax.psum_scatter(vector_stack, ("dp", "mp"), scatter_dimension=1, tiled=True),
        lax.psum_scatter(up_bias_full, ("dp", "mp"), scatter_dimension=0, tiled=True),
    )
    up_sum, down_sum = (
        lax.psum_scatter(up_grad, "dp", scatter_dimension=0, tiled=True),
        lax.psum_scatter(down_grad, "dp", scatter_dimension=1, tiled=True),
    )
    return (
        layer_out.astype(jnp.bfloat16),
        input_grad,
        memory_grad,
        query_sum,
        key_sum,
        value_sum,
        out_sum,
        up_sum,
        down_sum,
        vector_sums[6],
        vector_sums[7],
        up_bias_sum,
        vector_sums[4],
        vector_sums[5],
        vector_sums[0],
        vector_sums[1],
        vector_sums[2],
        vector_sums[3],
    )


def solution(mesh):
    in_specs = (
        P(("dp", "mp"), None),
        P(("dp", "mp"), None),
        P("dp"),
        P("dp"),
        P("dp", None),
        P("dp", "mp"),
        P("mp"),
        P("dp", "mp"),
        P("dp", "mp"),
        P("mp"),
        P("mp", "dp"),
        P(),
        P(),
        P(),
        P(),
        P(),
        P("dp", "mp"),
        P("mp"),
        P("mp", "dp"),
        P(),
        P(("dp", "mp"), None),
    )
    out_specs = (
        P(("dp", "mp"), None),
        P(("dp", "mp"), None),
        P(("dp", "mp"), None),
        P("dp", "mp"),
        P("dp", "mp"),
        P("dp", "mp"),
        P("mp", "dp"),
        P("dp", "mp"),
        P("mp", "dp"),
        P(("dp", "mp")),
        P(("dp", "mp")),
        P(("dp", "mp")),
        P(("dp", "mp")),
        P(("dp", "mp")),
        P(("dp", "mp")),
        P(("dp", "mp")),
        P(("dp", "mp")),
        P(("dp", "mp")),
    )
    return jax.shard_map(
        per_device, mesh=mesh, in_specs=in_specs, out_specs=out_specs, check_vma=False
    )
```

profile of v0, /device:TPU:0, one launch (start us, length us, event | category | flops | bytes accessed | tf_op | source)
XLA Modules:
  0.0 841.0 jit_solution(9052332494830410126)
XLA Ops:
  17.8 35.0 %all_gather.38 = bf16[192,768]{0,1:T(8,128)(2,1)} all-gather(bf16[192,96]{0,1:T(8,128)(2,1)S(1)} %copy.63), channel_id=1, replica_groups=mesh['dp'=8,'mp'=4] {'dp'}, dimensions={1}, use_global_device_ids=true | all-gather | bytes 331776 | tf_op jit(solution)/shard_map/all_gather | solution.py:91
  52.8 33.1 %all_gather.37 = bf16[768,192]{1,0:T(8,128)(2,1)} all-gather(bf16[96,192]{1,0:T(8,128)(2,1)S(1)} %copy-done.29), channel_id=1, replica_groups=mesh['dp'=8,'mp'=4] {'dp'}, dimensions={0}, use_global_device_ids=true | all-gather | bytes 331776 | tf_op jit(solution)/shard_map/all_gather | solution.py:89
  85.8 33.1 %all_gather.35 = bf16[768,192]{1,0:T(8,128)(2,1)} all-gather(bf16[96,192]{1,0:T(8,128)(2,1)S(1)} %copy-done.30), channel_id=1, replica_groups=mesh['dp'=8,'mp'=4] {'dp'}, dimensions={0}, use_global_device_ids=true | all-gather | bytes 331776 | tf_op jit(solution)/shard_map/all_gather | solution.py:90
  118.9 31.0 %all_gather.36 = bf16[768,192]{1,0:T(8,128)(2,1)S(1)} all-gather(bf16[96,192]{1,0:T(8,128)(2,1)S(1)} %copy-done.31), channel_id=1, replica_groups=mesh['dp'=8,'mp'=4] {'dp'}, dimensions={0}, use_global_device_ids=true | all-gather | bytes 331776 | tf_op jit(solution)/shard_map/all_gather | solution.py:88
  156.9 8.1 while.26
  168.9 29.0 %reduce-scatter.16.cloned.1.call-done = bf16[256,768]{1,0:T(8,128)(2,1)} async-done(((bf16[1024,768]{1,0:T(8,128)(2,1)}), bf16[256,768]{1,0:T(8,128)(2,1)}) %reduce-scatter.16.cloned.1.call-update) | async-done | bytes 393232 | tf_op jit(solution)/shard_map/reduce_scatter | solution.py:151
  204.0 10.0 %all-gather.13.cloned.1.call-done = bf16[768,768]{1,0:T(8,128)(2,1)} async-done(((bf16[96,768]{1,0:T(8,128)(2,1)}), bf16[768,768]{1,0:T(8,128)(2,1)}) %all-gather.13.cloned.1.call-update) | async-done | bytes 1179664 | tf_op jit(solution)/shard_map/all_gather | solution.py:92
  214.0 20.1 %all-gather.11.cloned.1.call-done = bf16[1024,768]{1,0:T(8,128)(2,1)} async-done(((bf16[256,768]{1,0:T(8,128)(2,1)}), bf16[1024,768]{1,0:T(8,128)(2,1)}) %all-gather.11.cloned.1.call-update) | async-done | bytes 1572880 | tf_op jit(solution)/shard_map/all_gather | solution.py:160
  234.1 4.8 fusion.116
  238.9 39.1 %all-gather.15.cloned.1.call-done = bf16[768,768]{0,1:T(8,128)(2,1)} async-done(((bf16[768,96]{0,1:T(8,128)(2,1)}), bf16[768,768]{0,1:T(8,128)(2,1)}) %all-gather.15.cloned.1.call-update) | async-done | bytes 1179664 | tf_op jit(solution)/shard_map/all_gather | solution.py:93
  277.9 19.7 %all-gather.17.cloned.1.call-done = bf16[1024,768]{1,0:T(8,128)(2,1)} async-done(((bf16[256,768]{1,0:T(8,128)(2,1)}), bf16[1024,768]{1,0:T(8,128)(2,1)}) %all-gather.17.cloned.1.call-update) | async-done | bytes 1572880 | tf_op jit(solution)/shard_map/all_gather | solution.py:176
  297.6 5.7 convert_reduce_fusion
  304.5 3.8 convolution_convert_fusion
  308.4 5.6 convolution_convert_fusion.1
  314.1 22.6 %reduce-scatter.20.cloned.1.call-done = bf16[256,768]{1,0:T(8,128)(2,1)} async-done(((bf16[1024,768]{1,0:T(8,128)(2,1)}), bf16[256,768]{1,0:T(8,128)(2,1)}) %reduce-scatter.20.cloned.1.call-update) | async-done | bytes 393232 | tf_op jit(solution)/shard_map/reduce_scatter | solution.py:184
  338.2 29.0 %reduce-scatter.18.cloned.1.call-done = bf16[256,768]{1,0:T(8,128)(2,1)} async-done(((bf16[1024,768]{1,0:T(8,128)(2,1)}), bf16[256,768]{1,0:T(8,128)(2,1)}) %reduce-scatter.18.cloned.1.call-update) | async-done | bytes 393232 | tf_op jit(solution)/shard_map/reduce_scatter | solution.py:168
  367.3 2.8 convert_reduce_fusion.8
  370.2 19.5 %all-gather.19.cloned.1.call-done = bf16[1024,768]{1,0:T(8,128)(2,1)} async-done(((bf16[256,768]{1,0:T(8,128)(2,1)}), bf16[1024,768]{1,0:T(8,128)(2,1)}) %all-gather.19.cloned.1.call-update) | async-done | bytes 1572880 | tf_op jit(solution)/shard_map/all_gather | solution.py:199
  389.8 3.0 convolution_convert_fusion.4
  397.8 17.2 %while.27 = (s32[]{:T(128)}, bf16[2,2,256,3,64]{2,4,3,1,0:T(8,128)(2,1)}, bf16[2,2,452,3,64]{2,4,3,1,0:T(8,128)(2,1)}, bf16[2,2,452,3,64]{2,4,3,1,0:T(8,128)(2,1...) while((s32[]{:T(128)}, ...), condition=%wide.region_17.18_spmd, body=%wide.region_15.17_spmd.sunk | while | flops 451858816 | bytes 39597732 | solution.py:232
  421.6 5.2 fusion.114
  426.8 4.9 fusion.118
  439.7 3.6 convolution_bitcast_fusion.1
  443.4 16.4 %fusion = bf16[200,768]{1,0:T(8,128)(2,1)} fusion(bf16[784,768]{1,0:T(8,128)(2,1)S(1)} %copy-done.7), kind=kCustom, calls=%all-reduce-scatter | all-reduce-scatter fusion | flops 614401 | bytes 1511936
  463.2 3.6 convolution_bitcast_fusion
  471.1 18.7 %reduce-scatter.22.cloned.1.call-done = bf16[256,768]{1,0:T(8,128)(2,1)} async-done(((bf16[1024,768]{1,0:T(8,128)(2,1)}), bf16[256,768]{1,0:T(8,128)(2,1)}) %reduce-scatter.22.cloned.1.call-update) | async-done | bytes 393232 | tf_op jit(solution)/shard_map/reduce_scatter | solution.py:274
  491.3 41.4 %all-reduce.4 = (f32[8,768]{1,0:T(8,128)S(1)}, f32[3072]{0:T(1024)S(1)}) all-reduce(f32[8,768]{1,0:T(8,128)S(1)} %stack.32, f32[3072]{0:T(1024)S(1)} %dynamic_update_slice.31), channel_id=13, replica_groups=mesh['dp'=8,'mp'=4] {'dp','mp'}, use_global_device_ids=true, to_apply=%region_40.41.clone | all-reduce | flops 9216 | bytes 73728
  536.1 27.8 %reduce-scatter.32.cloned.1.call-done = f32[768,96]{0,1:T(8,128)} async-done(((f32[768,768]{0,1:T(8,128)}), f32[768,96]{0,1:T(8,128)}) %reduce-scatter.32.cloned.1.call-update) | async-done | bytes 294928 | tf_op jit(solution)/shard_map/reduce_scatter | solution.py:323
  563.9 72.3 %reduce-scatter.30.cloned.1.call-done = f32[96,768]{1,0:T(8,128)} async-done(((f32[768,768]{1,0:T(8,128)}), f32[96,768]{1,0:T(8,128)}) %reduce-scatter.30.cloned.1.call-update) | async-done | bytes 294928 | tf_op jit(solution)/shard_map/reduce_scatter | solution.py:322
  636.2 66.0 %reduce-scatter.24.cloned.1.call-done = f32[96,192]{1,0:T(8,128)} async-done(((f32[768,192]{1,0:T(8,128)}), f32[96,192]{1,0:T(8,128)}) %reduce-scatter.24.cloned.1.call-update) | async-done | bytes 73744 | tf_op jit(solution)/shard_map/reduce_scatter | solution.py:289
  702.1 65.4 %reduce-scatter.26.cloned.1.call-done = f32[96,192]{1,0:T(8,128)} async-done(((f32[768,192]{1,0:T(8,128)}), f32[96,192]{1,0:T(8,128)}) %reduce-scatter.26.cloned.1.call-update) | async-done | bytes 73744 | tf_op jit(solution)/shard_map/reduce_scatter | solution.py:290
  767.5 65.9 %reduce-scatter.28.cloned.1.call-done = f32[96,192]{1,0:T(8,128)} async-done(((f32[768,192]{1,0:T(8,128)}), f32[96,192]{1,0:T(8,128)}) %reduce-scatter.28.cloned.1.call-update) | async-done | bytes 73744 | tf_op jit(solution)/shard_map/reduce_scatter | solution.py:291
  (296 shorter events, 85.6 us)
Async XLA Ops:
  8.1 9.6 %copy-start.44 = (bf16[192]{0:T(256)(128)(2,1)S(1)}, bf16[192]{0:T(256)(128)(2,1)}, u32[]{:S(2)}) copy-start(bf16[192]{0:T(256)(128)(2,1)} %param.31) | copy-start | bytes 1156
  8.1 9.6 %copy-start.45 = (bf16[192]{0:T(256)(128)(2,1)S(1)}, bf16[192]{0:T(256)(128)(2,1)}, u32[]{:S(2)}) copy-start(bf16[192]{0:T(256)(128)(2,1)} %param.34) | copy-start | bytes 1156
  8.1 9.6 %copy-start.33 = (s32[4,196]{1,0:T(4,128)S(1)}, s32[4,196]{1,0:T(4,128)}, u32[]{:S(2)}) copy-start(s32[4,196]{1,0:T(4,128)} %param.29) | copy-start | bytes 9412
  8.1 9.6 %copy-start.32 = (bf16[192,96]{1,0:T(8,128)(2,1)S(1)}, bf16[192,96]{1,0:T(8,128)(2,1)}, u32[]{:S(2)}) copy-start(bf16[192,96]{1,0:T(8,128)(2,1)} %param.35) | copy-start | bytes 110596
  8.1 44.7 %copy-start.29 = (bf16[96,192]{1,0:T(8,128)(2,1)S(1)}, bf16[96,192]{1,0:T(8,128)(2,1)}, u32[]{:S(2)}) copy-start(bf16[96,192]{1,0:T(8,128)(2,1)} %param.32) | copy-start | bytes 110596
  8.1 77.7 %copy-start.30 = (bf16[96,192]{1,0:T(8,128)(2,1)S(1)}, bf16[96,192]{1,0:T(8,128)(2,1)}, u32[]{:S(2)}) copy-start(bf16[96,192]{1,0:T(8,128)(2,1)} %param.33) | copy-start | bytes 110596
  8.1 110.8 %copy-start.31 = (bf16[96,192]{1,0:T(8,128)(2,1)S(1)}, bf16[96,192]{1,0:T(8,128)(2,1)}, u32[]{:S(2)}) copy-start(bf16[96,192]{1,0:T(8,128)(2,1)} %param.30) | copy-start | bytes 110596
  8.1 141.8 %all-gather.9.cloned.1.call-start = ((), (), s32[]{:S(2)}) async-start(), calls=%async_computation.10 | async-start | bytes 1966080 | tf_op jit(solution)/shard_map/all_gather | solution.py:106
  14.1 138.5 %all-gather.21.cloned.1.call-start = ((), (), s32[]{:S(2)}) async-start(), calls=%async_computation.25 | async-start | bytes 1536000 | tf_op jit(solution)/shard_map/all_gather | solution.py:107
  17.4 180.5 %reduce-scatter.16.cloned.1.call-start = ((), (), s32[]{:S(2)}) async-start(), calls=%async_computation.11 | async-start | bytes 1966080 | tf_op jit(solution)/shard_map/reduce_scatter | solution.py:151
  165.1 32.8 %copy-start = (bf16[256,768]{1,0:T(8,128)(2,1)S(1)}, bf16[256,768]{1,0:T(8,128)(2,1)}, u32[]{:S(2)}) copy-start(bf16[256,768]{1,0:T(8,128)(2,1)} %param.25) | copy-start | bytes 1179652
  166.4 34.0 %copy-start.11 = (bf16[1024,192]{0,1:T(8,128)(2,1)}, bf16[1024,192]{0,1:T(8,128)(2,1)S(1)}, u32[]{:S(2)}) copy-start(bf16[1024,192]{0,1:T(8,128)(2,1)S(1)} %reshape.371) | copy-start | bytes 1179652
  168.2 35.7 %copy-start.37 = (bf16[768]{0:T(1024)(128)(2,1)S(1)}, bf16[768]{0:T(1024)(128)(2,1)}, u32[]{:S(2)}) copy-start(bf16[768]{0:T(1024)(128)(2,1)} %param.42) | copy-start | bytes 4612
  168.2 45.8 %all-gather.13.cloned.1.call-start = ((), (), s32[]{:S(2)}) async-start(), calls=%async_computation.13 | async-start | bytes 1327104 | tf_op jit(solution)/shard_map/all_gather | solution.py:92
  168.8 65.3 %all-gather.11.cloned.1.call-start = ((), (), s32[]{:S(2)}) async-start(), calls=%async_computation.12 | async-start | bytes 1966080 | tf_op jit(solution)/shard_map/all_gather | solution.py:160
  202.4 75.5 %all-gather.15.cloned.1.call-start = ((), (), s32[]{:S(2)}) async-start(), calls=%async_computation.14 | async-start | bytes 1327104 | tf_op jit(solution)/shard_map/all_gather | solution.py:93
  203.0 94.6 %all-gather.17.cloned.1.call-start = ((), (), s32[]{:S(2)}) async-start(), calls=%async_computation.16 | async-start | bytes 1966080 | tf_op jit(solution)/shard_map/all_gather | solution.py:176
  203.7 133.0 %reduce-scatter.20.cloned.1.call-start = ((), (), s32[]{:S(2)}) async-start(), calls=%async_computation.17 | async-start | bytes 1966080 | tf_op jit(solution)/shard_map/reduce_scatter | solution.py:184
  308.4 28.3 %copy-start.1 = (bf16[256,768]{1,0:T(8,128)(2,1)S(1)}, bf16[256,768]{1,0:T(8,128)(2,1)}, u32[]{:S(2)}) copy-start(bf16[256,768]{1,0:T(8,128)(2,1)} %reduce-scatter.16.cloned.1.call-done) | copy-start | bytes 1179652
  308.4 58.9 %reduce-scatter.18.cloned.1.call-start = ((), (), s32[]{:S(2)}) async-start(), calls=%async_computation.15 | async-start | bytes 1966080 | tf_op jit(solution)/shard_map/reduce_scatter | solution.py:168
  314.0 53.2 %copy-start.19 = (bf16[256,768]{1,0:T(8,128)(2,1)S(1)}, bf16[256,768]{1,0:T(8,128)(2,1)}, u32[]{:S(2)}) copy-start(bf16[256,768]{1,0:T(8,128)(2,1)} %param.45) | copy-start | bytes 1179652
  314.1 75.7 %all-gather.19.cloned.1.call-start = ((), (), s32[]{:S(2)}) async-start(), calls=%async_computation.18 | async-start | bytes 1966080 | tf_op jit(solution)/shard_map/all_gather | solution.py:199
  370.1 99.3 %reduce-scatter.34.cloned.1.call-start = ((), (), s32[]{:S(2)}) async-start(), calls=%async_computation.26 | async-start | bytes 884736
  397.5 92.2 %reduce-scatter.22.cloned.1.call-start = ((), (), s32[]{:S(2)}) async-start(), calls=%async_computation.19 | async-start | bytes 1966080 | tf_op jit(solution)/shard_map/reduce_scatter | solution.py:274
  397.7 19.0 %copy-start.13 = (bf16[768,192]{1,0:T(8,128)(2,1)S(1)}, bf16[768,192]{1,0:T(8,128)(2,1)}, u32[]{:S(2)}) copy-start(bf16[768,192]{1,0:T(8,128)(2,1)} %all_gather.35) | copy-start | bytes 884740
  421.5 142.4 %reduce-scatter.32.cloned.1.call-start = ((), (), s32[]{:S(2)}) async-start(), calls=%async_computation.24 | async-start | bytes 2654208 | tf_op jit(solution)/shard_map/reduce_scatter | solution.py:323
  426.8 209.4 %reduce-scatter.30.cloned.1.call-start = ((), (), s32[]{:S(2)}) async-start(), calls=%async_computation.23 | async-start | bytes 2654208 | tf_op jit(solution)/shard_map/reduce_scatter | solution.py:322
  431.7 270.4 %reduce-scatter.24.cloned.1.call-start = ((), (), s32[]{:S(2)}) async-start(), calls=%async_computation.20 | async-start | bytes 884736 | tf_op jit(solution)/shard_map/reduce_scatter | solution.py:289
  433.3 334.2 %reduce-scatter.26.cloned.1.call-start = ((), (), s32[]{:S(2)}) async-start(), calls=%async_computation.21 | async-start | bytes 884736 | tf_op jit(solution)/shard_map/reduce_scatter | solution.py:290
  443.3 390.1 %reduce-scatter.28.cloned.1.call-start = ((), (), s32[]{:S(2)}) async-start(), calls=%async_computation.22 | async-start | bytes 884736 | tf_op jit(solution)/shard_map/reduce_scatter | solution.py:291
  460.5 6.8 collective-permute-start
  466.7 67.2 %copy-start.15 = (f32[256,768]{1,0:T(8,128)S(1)}, f32[256,768]{1,0:T(8,128)}, u32[]{:S(2)}) copy-start(f32[256,768]{1,0:T(8,128)} %get-tuple-element.260) | copy-start | bytes 2359300
  (42 other events, 122.0 us)
Sparse Core Ops, SparseCore 0:
  14.2 22.3 all-gather.8
  38.7 17.7 all-gather.20
  168.3 29.4 reduce-scatter.15
  308.5 28.1 reduce-scatter.19
  339.1 28.1 reduce-scatter.17
Sparse Core Ops, SparseCore 1:
  171.1 42.8 all-gather.12
  216.1 17.9 all-gather.10
  236.4 41.5 all-gather.14
  279.6 18.0 all-gather.16
  370.2 19.5 all-gather.18
  397.6 62.5 reduce-scatter.33
  462.6 27.1 reduce-scatter.21
  494.1 69.7 reduce-scatter.31
  568.2 67.9 reduce-scatter.29
  640.4 61.6 reduce-scatter.23
  705.9 61.6 reduce-scatter.25
  771.8 61.6 reduce-scatter.27
where the time goes:
time: 849 us; the launch traced here: 841 us
  waiting for transfers between devices  507 us (60%)
  blocking collectives  190 us (22%)
  matrix products  72 us (8%)
  other arithmetic  29 us (3%)
  local copies, waits for them, and re-layouts  23.1 us (3%)
  between operations  17.2 us (2%)
    reduce_scatter x1, waiting for transfers between devices, per_device(): lax.psum_scatter(up_grad, 'dp', scatter_dimension=0, tiled=True)  72.3 us
    reduce_scatter x1, waiting for transfers between devices, per_device(): lax.psum_scatter(query_weight_part, 'dp', scatter_dimension=0, tiled=True)  66 us
    reduce_scatter x1, waiting for transfers between devices, per_device(): lax.psum_scatter(value_weight_part, 'dp', scatter_dimension=0, tiled=True)  65.9 us
    reduce_scatter x1, waiting for transfers between devices, per_device(): lax.psum_scatter(key_weight_part, 'dp', scatter_dimension=0, tiled=True)  65.4 us
    unnamed x2, blocking collectives  57.8 us
    all_gather x1, waiting for transfers between devices, per_device(): lax.all_gather(down_weight, 'dp', axis=1, tiled=True)  39.1 us
    all_gather x1, blocking collectives, per_device(): lax.all_gather(out_weight, 'dp', axis=1, tiled=True)  35 us
    all_gather x1, blocking collectives, per_device(): lax.all_gather(value_weight, 'dp', axis=0, tiled=True)  33.1 us
  transfers between devices with their start and end apart: 18, of which 14 were waited for; matrix products, arithmetic and copies ran while one was open for 11% of the time, Pallas kernels for 0%

commit v1 on v0

v1 whole, which is shorter than its diff:
```python
import functools

import jax
import jax.numpy as jnp
from jax import lax
from jax.experimental import pallas as pl
from jax.experimental.pallas import tpu as pltpu
from jax.sharding import PartitionSpec as P

HEAD = 64
TEXT = 256
PATCHES = 196
SLOTS = 256
KEYS = SLOTS + TEXT
EPS = 1e-06
NEG = -1000000000.0
SCALE = HEAD ** (-0.5)
F32 = jnp.float32
BF16 = jnp.bfloat16
AXES = ("dp", "mp")

LEFT = 512
RIGHT = 256


def nn(a, b):
    return lax.dot_general(a, b, (((1,), (0,)), ((), ())), preferred_element_type=F32)


def nt(a, b):
    return lax.dot_general(a, b, (((1,), (1,)), ((), ())), preferred_element_type=F32)


def eye(n):
    rows = lax.broadcasted_iota(jnp.int32, (n, n), 0)
    cols = lax.broadcasted_iota(jnp.int32, (n, n), 1)
    return (rows == cols).astype(F32).astype(BF16)


def standard(matrix):
    average = jnp.mean(matrix, axis=-1, keepdims=True)
    centered = matrix - average
    inverse = lax.rsqrt(jnp.mean(centered * centered, axis=-1, keepdims=True) + EPS)
    return centered * inverse, inverse


def standard_back(normed, inverse, grad_out, gain):
    scaled = grad_out * gain
    return inverse * (
        scaled
        - jnp.mean(scaled, axis=-1, keepdims=True)
        - normed * jnp.mean(scaled * normed, axis=-1, keepdims=True)
    )


def call(kernel, out_shapes, *args, scratch=(), smem=0, flops=0):
    nbytes = sum(a.size * a.dtype.itemsize for a in args) + sum(
        int(functools.reduce(lambda p, q: p * q, s, 1)) * jnp.dtype(d).itemsize for s, d in out_shapes
    )
    return pl.pallas_call(
        kernel,
        out_shape=[jax.ShapeDtypeStruct(s, d) for s, d in out_shapes],
        in_specs=[pl.BlockSpec(memory_space=pltpu.SMEM)] * smem
        + [pl.BlockSpec(memory_space=pltpu.VMEM)] * (len(args) - smem),
        out_specs=[pl.BlockSpec(memory_space=pltpu.VMEM)] * len(out_shapes),
        scratch_shapes=list(scratch),
        compiler_params=pltpu.CompilerParams(vmem_limit_bytes=56 * 1024 * 1024),
        cost_estimate=pl.CostEstimate(flops=flops, bytes_accessed=nbytes, transcendentals=0),
    )(*args)


def prep_kernel(
    place, tok_o, tok_p, mem_o, mem_p, cot_o, cot_p, vec,
    x_ref, xt_ref, tok_r, cot_r, cot_t, mem_r, vec_r, hot_ref,
):
    features = tok_o.shape[1]
    lane = lax.broadcasted_iota(jnp.int32, (features, features), 1)
    hot_ref[...] = (lane == place[...]).astype(F32).astype(BF16)
    gain = vec[0:1, :].astype(F32)
    shift = vec[1:2, :].astype(F32)
    vec_r[...] = nt(vec[...], hot_ref[...])

    for at, (mem, tok) in enumerate(((mem_o, tok_o), (mem_p, tok_p))):
        for first, src in ((0, mem), (SLOTS, tok)):
            normed, _ = standard(src[...].astype(F32))
            low = (normed * gain + shift).astype(BF16)
            x_ref[at, first : first + 256, :] = nt(low, hot_ref[...]).astype(BF16)
            xt_ref[:, at * KEYS + first : at * KEYS + first + 256] = nt(hot_ref[...], low).astype(BF16)
    mem_r[...] = nt(mem_o[...], hot_ref[...]).astype(BF16)
    for at, (tok, cot) in enumerate(((tok_o, cot_o), (tok_p, cot_p))):
        rows = slice(at * TEXT, (at + 1) * TEXT)
        tok_r[rows, :] = nt(tok[...], hot_ref[...]).astype(BF16)
        cot_r[rows, :] = nt(cot[...], hot_ref[...]).astype(BF16)
        cot_t[:, rows] = nt(hot_ref[...], cot[...]).astype(BF16)


def masked(raw, cond):
    return jnp.where(cond, raw * SCALE, NEG)


def attend_kernel(
    split, length,
    own, own_y, peer, peer_d0, peer_d1, z0, z1, z2, z3, x_ref, bias, patch,
    w_ref, y_ref, p_ref, ctx_ref, out_ref,
):
    half = own.shape[0]
    block = half // 4
    w_ref[0, 0:half, 0:LEFT] = own[...]
    w_ref[0, half : 2 * half, 0:LEFT] = own_y[...]
    w_ref[1, 0:half, 0:LEFT] = peer[...]
    w_ref[1, half : half + half // 2, 0:LEFT] = peer_d0[...]
    w_ref[1, half + half // 2 : 2 * half, 0:LEFT] = peer_d1[...]
    for k, piece in enumerate((z0, z1, z2, z3)):
        for m in range(2):
            for ry in range(2):
                first = ry * half + k * block
                src = (m * 2 + ry) * block
                w_ref[m, first : first + block, LEFT : LEFT + RIGHT] = piece[src : src + block, :]

    lane = lax.broadcasted_iota(jnp.int32, (TEXT, 128), 1)
    lane_k = lax.broadcasted_iota(jnp.int32, (KEYS, 128), 1)
    zero = jnp.zeros((TEXT, 128), BF16)
    unit = eye(128)
    unit_t = eye(TEXT)
    key_place = lax.broadcasted_iota(jnp.int32, (TEXT, TEXT), 0)
    query_place = lax.broadcasted_iota(jnp.int32, (TEXT, TEXT), 1)
    out_ref[...] = jnp.zeros_like(out_ref)

    def step(at, carry):
        e, m = at // 2, at % 2
        x = x_ref[e]
        w = w_ref[m]
        b = bias[m]
        y1 = nn(x, w[:, 0:384]) + b[:, 0:384]
        y_ref[m, e, :, 0:384] = y1.astype(BF16)
        y2 = nn(x, w[:, LEFT : LEFT + RIGHT]) + b[:, 384:640]
        y_ref[m, e, :, 384:512] = y2[:, 0:128].astype(BF16)
        y_ref[m, e, :, 512:640] = jnp.where(lane_k < HEAD, y2[:, 128:256], 0.0).astype(BF16)

        patch_ok = jnp.broadcast_to(patch[e], (SLOTS, TEXT)) > 0.0
        text_ok = ((key_place < split[e]) | (key_place <= query_place)) & (key_place < length[e])

        q01 = y_ref[m, e, SLOTS:KEYS, 0:128]
        q2 = y_ref[m, e, SLOTS:KEYS, 384:512]
        v01t = nt(unit, y_ref[m, e, :, 256:384]).astype(BF16)
        v2t = nt(unit, y_ref[m, e, :, 384:512]).astype(BF16)
        ctx01 = []
        for head in range(3):
            if head == 0:
                q, first, vt = jnp.where(lane < HEAD, q01, zero), 128, v01t[0:HEAD]
            elif head == 1:
                q, first, vt = jnp.where(lane >= HEAD, q01, zero), 128, v01t[HEAD:128]
            else:
                q, first, vt = jnp.where(lane < HEAD, q2, zero), 512, v2t[HEAD:128]
            s_mem = masked(nt(y_ref[m, e, 0:SLOTS, first : first + 128], q), patch_ok)
            s_text = masked(nt(y_ref[m, e, SLOTS:KEYS, first : first + 128], q), text_ok)
            largest = jnp.maximum(
                jnp.max(s_mem, axis=0, keepdims=True), jnp.max(s_text, axis=0, keepdims=True)
            )
            e_mem = jnp.exp(s_mem - largest)
            e_text = jnp.exp(s_text - largest)
            total = jnp.sum(e_mem, axis=0, keepdims=True) + jnp.sum(e_text, axis=0, keepdims=True)
            inverse = 1.0 / total
            p_mem = (e_mem * inverse).astype(BF16)
            p_text = (e_text * inverse).astype(BF16)
            p_ref[m, e, head, 0:SLOTS, :] = p_mem
            p_ref[m, e, head, SLOTS:KEYS, :] = p_text
            ctx01.append(nn(vt[:, 0:SLOTS], p_mem) + nn(vt[:, SLOTS:KEYS], p_text))
        c01t = jnp.concatenate([ctx01[0], ctx01[1]], axis=0).astype(BF16)
        c2t = jnp.concatenate([jnp.zeros((HEAD, TEXT), F32), ctx01[2]], axis=0).astype(BF16)
        c01 = nt(unit_t, c01t).astype(BF16)
        c2 = nt(unit_t, c2t).astype(BF16)
        ctx_ref[m, e, :, 0:128] = c01
        ctx_ref[m, e, :, 128:256] = c2
        out_ref[e] += nt(c01, w[:, 384:512]) + nt(c2, w[:, 640:768])
        return carry

    lax.fori_loop(0, 4, step, 0)


def gelu_pair(v):
    c = 0.7978845608028654
    square = v * v
    t = jnp.tanh(c * v * (1.0 + 0.044715 * square))
    gelu = 0.5 * v * (1.0 + t)
    slope = 0.5 * (1.0 + t) + 0.5 * v * (1.0 - t * t) * (c * (1.0 + 3 * 0.044715 * square))
    return gelu, slope


def assemble(own, own_y, peer, peer_d0, peer_d1, w_ref):
    half = own.shape[0]
    w_ref[0, 0:half, :] = own[...]
    w_ref[0, half : 2 * half, :] = own_y[...]
    w_ref[1, 0:half, :] = peer[...]
    w_ref[1, half : half + half // 2, :] = peer_d0[...]
    w_ref[1, half + half // 2 : 2 * half, :] = peer_d1[...]


def up_kernel(
    part, part_in, tok_r, vec_r, cot_t, bias, own, own_y, peer, peer_d0, peer_d1,
    res_ref, mid_ref, mid_t, u_ref, hid_ref, slope_ref, g00, g01, g10, g11,
):
    assemble(own, own_y, peer, peer_d0, peer_d1, u_ref)
    half = own.shape[0]
    for e in range(2):
        rows = slice(e * TEXT, (e + 1) * TEXT)
        res = (
            tok_r[rows, :].astype(F32)
            + (part[e].astype(F32) + part_in[1 - e].astype(F32))
            + vec_r[4:5, :]
        )
        res_ref[rows, :] = res
        normed, _ = standard(res)
        mid_ref[rows, :] = (normed * vec_r[2:3, :] + vec_r[3:4, :]).astype(BF16)
    mid_t[...] = nt(eye(mid_ref.shape[1]), mid_ref[...]).astype(BF16)
    for m, (top, bottom) in enumerate(((g00, g01), (g10, g11))):
        for e in range(2):
            rows = slice(e * TEXT, (e + 1) * TEXT)
            pre = nn(mid_ref[rows, :], u_ref[m]) + bias[m]
            gelu, slope = gelu_pair(pre)
            hid_ref[m, rows, :] = gelu.astype(BF16)
            slope_ref[m, rows, :] = slope.astype(BF16)
        top[...] = nn(cot_t[0:half, :], hid_ref[m]).astype(BF16)
        bottom[...] = nn(cot_t[half : 2 * half, :], hid_ref[m]).astype(BF16)


def down_kernel(
    u_ref, hid_ref, slope_ref, mid_t, cot_r, own, own_y, peer, peer_d0, peer_d1,
    out_ref, grad_ref, bias_ref, g00, g01, g10, g11, d_ref, pre_ref,
):
    assemble(own, own_y, peer, peer_d0, peer_d1, d_ref)
    half = own.shape[0]
    bias_ref[...] = jnp.zeros_like(bias_ref)
    for m in range(2):
        for e in range(2):
            rows = slice(e * TEXT, (e + 1) * TEXT)
            pre = (nn(cot_r[rows, :], d_ref[m]) * slope_ref[m, rows, :].astype(F32)).astype(BF16)
            pre_ref[m, rows, :] = pre
            bias_ref[m : m + 1, :] += jnp.sum(pre.astype(F32), axis=0, keepdims=True)
    for e in range(2):
        rows = slice(e * TEXT, (e + 1) * TEXT)
        grad_ref[e] = (nt(pre_ref[0, rows, :], u_ref[0]) + nt(pre_ref[1, rows, :], u_ref[1])).astype(BF16)
    for e in range(2):
        rows = slice(e * TEXT, (e + 1) * TEXT)
        out_ref[e] = (nt(hid_ref[0, rows, :], d_ref[0]) + nt(hid_ref[1, rows, :], d_ref[1])).astype(BF16)
    for m, (top, bottom) in enumerate(((g00, g01), (g10, g11))):
        top[...] = nn(mid_t[0:half, :], pre_ref[m]).astype(BF16)
        bottom[...] = nn(mid_t[half : 2 * half, :], pre_ref[m]).astype(BF16)


def attend_back_kernel(
    grad, grad_in, res_ref, cot_r, vec_r, w_ref, y_ref, p_ref,
    rg_ref, agt_ref, dy_ref, back_o, back_p, sums, bias_ref, ag_ref, back_ref,
):
    lane = lax.broadcasted_iota(jnp.int32, (TEXT, 128), 1)
    row = lax.broadcasted_iota(jnp.int32, (128, TEXT), 0)
    zero = jnp.zeros((TEXT, 128), BF16)
    unit = eye(128)
    unit_t = eye(TEXT)
    for e in range(2):
        rows = slice(e * TEXT, (e + 1) * TEXT)
        mid_grad = grad[e].astype(F32) + grad_in[1 - e].astype(F32)
        normed, inverse = standard(res_ref[rows, :])
        cot = cot_r[rows, :].astype(F32)
        resid = cot + standard_back(normed, inverse, mid_grad, vec_r[2:3, :])
        low = resid.astype(BF16)
        ag_ref[rows, :] = low
        if e == 0:
            rg_ref[...] = resid
            sums[0:1, :] = jnp.sum(mid_grad * normed, axis=0, keepdims=True)
            sums[1:2, :] = jnp.sum(mid_grad, axis=0, keepdims=True)
            sums[2:3, :] = jnp.sum(low.astype(F32), axis=0, keepdims=True)
            sums[3:4, :] = jnp.sum(cot, axis=0, keepdims=True)
            sums[4:8, :] = jnp.zeros_like(sums[4:8, :])
    agt_ref[...] = nt(eye(ag_ref.shape[1]), ag_ref[...]).astype(BF16)
    bias_ref[...] = jnp.zeros_like(bias_ref)
    back_ref[...] = jnp.zeros_like(back_ref)

    def step(at, carry):
        e, m = at // 2, at % 2
        w = w_ref[m]
        ag = ag_ref[pl.ds(pl.multiple_of(e * TEXT, TEXT), TEXT), :]
        dc01 = nn(ag, w[:, 384:512]).astype(BF16)
        dc2 = nn(ag, w[:, 640:768]).astype(BF16)
        q01 = y_ref[m, e, SLOTS:KEYS, 0:128]
        q2 = y_ref[m, e, SLOTS:KEYS, 384:512]
        k01 = y_ref[m, e, :, 128:256]
        k2 = y_ref[m, e, :, 512:640]
        k01t = nt(unit, k01).astype(BF16)
        k2t = nt(unit, k2).astype(BF16)
        dk, dv, dqt = [], [], []
        for head in range(3):
            keep = (lane < HEAD) if head == 0 else (lane >= HEAD)
            if head < 2:
                dc = jnp.where(keep, dc01, zero)
                q = jnp.where(keep, q01, zero)
                v = y_ref[m, e, :, 256:384]
                kt = k01t[0:HEAD] if head == 0 else k01t[HEAD:128]
            else:
                dc = jnp.where(lane >= HEAD, dc2, zero)
                q = jnp.where(lane < HEAD, q2, zero)
                v = y_ref[m, e, :, 384:512]
                kt = k2t[0:HEAD]
            prob = p_ref[m, e, head]
            probs = prob.astype(F32)
            grad_p = nt(v, dc)
            dot = jnp.sum(probs * grad_p, axis=0, keepdims=True)
            score = (probs * (grad_p - dot)).astype(BF16)
            dk.append(nn(score, q))
            dv.append(nn(prob, dc))
            dqt.append(nn(kt, score))
        dk01 = ((dk[0] + dk[1]) * SCALE).astype(BF16)
        dk2 = (dk[2] * SCALE).astype(BF16)
        dv01 = (dv[0] + dv[1]).astype(BF16)
        dv2 = dv[2].astype(BF16)
        dq01 = nt(unit_t, (jnp.concatenate([dqt[0], dqt[1]], axis=0) * SCALE).astype(BF16))
        dq2 = nt(
            unit_t,
            (jnp.concatenate([dqt[2], jnp.zeros((HEAD, TEXT), F32)], axis=0) * SCALE).astype(BF16),
        )
        dy_ref[m, e, 0:SLOTS, 0:128] = zero
        dy_ref[m, e, SLOTS:KEYS, 0:128] = dq01.astype(BF16)
        dy_ref[m, e, :, 128:256] = dk01
        dy_ref[m, e, :, 256:384] = dv01
        dy_ref[m, e, 0:SLOTS, 384:512] = dv2[0:SLOTS]
        dy_ref[m, e, SLOTS:KEYS, 384:512] = (dq2 + dv2[SLOTS:KEYS].astype(F32)).astype(BF16)
        dy_ref[m, e, :, 512:640] = dk2
        dy = dy_ref[m, e]
        bias_ref[m] += jnp.sum(dy.astype(F32), axis=0, keepdims=True)
        back_ref[e] += nt(dy[:, 0:384], w[:, 0:384]) + nt(dy[:, 384:640], w[:, LEFT : LEFT + RIGHT])
        return carry

    lax.fori_loop(0, 4, step, 0)
    back_o[...] = back_ref[0]
    back_p[...] = back_ref[1].astype(BF16)


def weight_kernel(
    xt_ref, agt_ref, dy_ref, ctx_ref,
    a00, a01, a10, a11, c0, c1, c2, c3,
):
    half = a00.shape[0]
    block = half // 4
    for m, tops in enumerate(((a00, a01), (a10, a11))):
        dy = dy_ref[m].reshape(2 * KEYS, 640)
        ctx = ctx_ref[m].reshape(2 * TEXT, 256)
        for ry in range(2):
            rows = slice(ry * half, (ry + 1) * half)
            tops[ry][:, 0:384] = nn(xt_ref[rows, :], dy[:, 0:384]).astype(BF16)
            tops[ry][:, 384:512] = nn(agt_ref[rows, :], ctx[:, 0:128]).astype(BF16)
            right = nn(xt_ref[rows, :], dy[:, 384:640])
            out2 = nn(agt_ref[rows, :], ctx[:, 128:256])
            for k, piece in enumerate((c0, c1, c2, c3)):
                src = slice(k * block, (k + 1) * block)
                first = (m * 2 + ry) * block
                piece[first : first + block, 0:128] = right[src, 0:128].astype(BF16)
                piece[first : first + block, 128:256] = (right[src, 128:256] + out2[src, :]).astype(BF16)


def last_kernel(
    back_o, back_in, tok_r, mem_r, rg_ref, res_ref, out_o, out_in, vec_r, hot_ref, sums,
    layer_ref, in_ref, mem_ref, vec_out,
):
    hot = hot_ref[...]

    def restore(v):
        high = v.astype(BF16)
        low = (v - high.astype(F32)).astype(BF16)
        return nn(high, hot) + nn(low, hot)

    gain = vec_r[0:1, :]
    layer = (
        res_ref[...] + (out_o[0].astype(F32) + out_in[...].astype(F32)) + vec_r[5:6, :]
    ).astype(BF16)
    layer_ref[...] = nn(layer, hot).astype(BF16)
    mem_back = back_o[0:SLOTS, :] + back_in[0:SLOTS, :].astype(F32)
    text_back = back_o[SLOTS:KEYS, :] + back_in[SLOTS:KEYS, :].astype(F32)
    normed, inverse = standard(tok_r[...].astype(F32))
    in_ref[...] = restore(rg_ref[...] + standard_back(normed, inverse, text_back, gain))
    normed_m, inverse_m = standard(mem_r[...].astype(F32))
    grad_m = standard_back(normed_m, inverse_m, mem_back, gain)
    mem_ref[...] = restore(grad_m)[0:PATCHES, :]
    gain_sum = jnp.sum(text_back * normed, axis=0, keepdims=True) + jnp.sum(
        mem_back * normed_m, axis=0, keepdims=True
    )
    shift_sum = jnp.sum(text_back, axis=0, keepdims=True) + jnp.sum(mem_back, axis=0, keepdims=True)
    stack = jnp.concatenate([sums[0:4, :], gain_sum, shift_sum, sums[4:6, :]], axis=0)
    vec_out[...] = restore(stack)


class Links:
    def __init__(self, dp, mp):
        self.dp, self.mp, self.depth = dp, mp, dp // 2
        self.x = self.pairs(lambda d, m: (d, m ^ 2))
        self.c = self.pairs(lambda d, m: (d, m ^ 1))
        self.y = self.pairs(lambda d, m: (d ^ 1, m))

    def pairs(self, to):
        out = []
        for d in range(self.dp):
            for m in range(self.mp):
                d2, m2 = to(d, m)
                out.append((d * self.mp + m, d2 * self.mp + m2))
        return out

    def z(self, k):
        return self.pairs(lambda d, m: ((((d // 2 + k) % self.depth) * 2 + d % 2), m))

    def send(self, a, pairs):
        return lax.ppermute(a, AXES, pairs)

    def z_gather(self, shard):
        if self.depth <= 4:
            return [shard] + [self.send(shard, self.z(k)) for k in range(1, self.depth)]
        held = shard[None]
        step = 1
        while step < self.depth:
            held = jnp.concatenate([held, self.send(held, self.z(step))], axis=0)
            step *= 2
        return [held[k] for k in range(self.depth)]

    def z_scatter(self, parts):
        if self.depth <= 4:
            got = [self.send(parts[k], self.z(-k)) for k in range(1, self.depth)]
            total = parts[0].astype(F32)
            for g in got:
                total = total + g.astype(F32)
            return total
        held = jnp.stack(parts).astype(F32)
        step = self.depth // 2
        while step >= 1:
            held = held[:step] + self.send(held[step:].astype(BF16), self.z(-step)).astype(F32)
            step //= 2
        return held[0]

    def gather_rows(self, shard):
        own = jnp.concatenate(self.z_gather(shard), axis=0)
        cut = own.shape[0] // 2
        peer = self.send(own, self.x)
        own_y = self.send(own, self.y)
        d0 = self.send(own_y[:cut], self.x)
        d1 = self.send(peer[cut:], self.y)
        return own, own_y, peer, d0, d1

    def gather_quads(self, shard):
        y1 = self.send(shard, self.y)
        x1 = self.send(shard, self.x)
        d1 = self.send(y1, self.x)
        pieces = self.z_gather(jnp.concatenate([shard, y1, x1, d1], axis=0))
        if self.depth == 4:
            return pieces
        r, lanes = shard.shape
        whole = jnp.stack(pieces).reshape(self.depth, 4, r, lanes).transpose(1, 0, 2, 3)
        whole = whole.reshape(4, 4, self.depth * r // 4, lanes)
        return [whole[:, k].reshape(-1, lanes) for k in range(4)]

    def scatter_rows(self, g00, g01, g10, g11):
        cut = g00.shape[0] // 2
        rows = g00.shape[0]
        d0 = self.send(g11[:cut], self.x)
        d1 = self.send(g11[cut:], self.y)
        send_y = jnp.concatenate([(g01[:cut].astype(F32) + d0.astype(F32)).astype(BF16), g01[cut:]], axis=0)
        send_x = jnp.concatenate([g10[:cut], (g10[cut:].astype(F32) + d1.astype(F32)).astype(BF16)], axis=0)
        from_y = self.send(send_y, self.y)
        from_x = self.send(send_x, self.x)
        total = (g00.astype(F32) + from_y.astype(F32) + from_x.astype(F32)).astype(BF16)
        r = rows // self.depth
        return self.z_scatter([total[k * r : (k + 1) * r] for k in range(self.depth)])

    def scatter_quads(self, pieces):
        if self.depth != 4:
            lanes = pieces[0].shape[1]
            whole = jnp.stack([p.reshape(4, -1, lanes) for p in pieces], axis=1)
            whole = whole.reshape(4, self.depth, -1, lanes).transpose(1, 0, 2, 3)
            pieces = [whole[k].reshape(-1, lanes) for k in range(self.depth)]
        total = self.z_scatter(pieces)
        r = total.shape[0] // 4
        t00, t01, t10, t11 = (total[i * r : (i + 1) * r] for i in range(4))
        d = self.send(t11.astype(BF16), self.x)
        from_y = self.send((t01 + d.astype(F32)).astype(BF16), self.y)
        from_x = self.send(t10.astype(BF16), self.x)
        return t00 + from_y.astype(F32) + from_x.astype(F32)

    def add_all(self, a):
        a = a + self.send(a, self.c)
        a = a + self.send(a, self.x)
        a = a + self.send(a, self.y)
        if self.depth <= 4:
            got = [self.send(a, self.z(k)) for k in range(1, self.depth)]
            for g in got:
                a = a + g
            return a
        step = 1
        while step < self.depth:
            a = a + self.send(a, self.z(step))
            step *= 2
        return a


def per_device(
    tokens, memory, split_point, text_length, patch_mask,
    query_weight, query_bias, key_weight, value_weight, value_bias,
    out_weight, out_bias, attn_gain, attn_shift, mlp_gain, mlp_shift,
    up_weight, up_bias, down_weight, down_bias, cotangent,
):
    features = tokens.shape[1]
    width = query_weight.shape[1]
    hidden = up_weight.shape[1]
    dp, mp = lax.axis_size("dp"), lax.axis_size("mp")
    links = Links(dp, mp)
    dp_at, mp_at = lax.axis_index("dp"), lax.axis_index("mp")
    z_at, y_at, x_at, c_at = dp_at // 2, dp_at % 2, mp_at // 2, mp_at % 2
    depth = dp // 2
    r = features // dp
    half = features // 2

    out_t = out_weight.T
    left = jnp.concatenate(
        [query_weight[:, :128], key_weight[:, :128], value_weight[:, :128], out_t[:, :128]], axis=1
    )
    right = jnp.concatenate(
        [query_weight[:, 128:], value_weight[:, 128:], key_weight[:, 128:], out_t[:, 128:]], axis=1
    )
    down_t = down_weight.T
    biases = jnp.concatenate([query_bias, value_bias, up_bias]).astype(BF16).reshape(1, -1)
    biases_x = links.send(biases, links.x)
    tok_p = links.send(tokens, links.c)
    mem = jnp.pad(memory, ((0, SLOTS - PATCHES), (0, 0)))
    mem_p = links.send(mem, links.c)
    cot_p = links.send(cotangent, links.c)
    attn_rows = links.gather_rows(left)
    attn_quads = links.gather_quads(right)
    up_rows = links.gather_rows(up_weight)
    down_rows = links.gather_rows(down_t)

    rel = jnp.arange(features, dtype=jnp.int32)
    rest = rel % half
    place = ((z_at - rest // r) % depth) * (2 * r) + (y_at ^ (rel // half)) * r + rest % r
    place = place.astype(jnp.int32).reshape(features, 1)

    blank = jnp.zeros_like(attn_gain)
    vec = jnp.stack(
        [attn_gain, attn_shift, mlp_gain, mlp_shift, out_bias, down_bias] + [blank] * 10
    )
    x, xt, tok_r, cot_r, cot_t, mem_r, vec_r, hot = call(
        prep_kernel,
        [
            ((2, KEYS, features), BF16), ((features, 2 * KEYS), BF16),
            ((2 * TEXT, features), BF16), ((2 * TEXT, features), BF16), ((features, 2 * TEXT), BF16),
            ((SLOTS, features), BF16), ((16, features), F32), ((features, features), BF16),
        ],
        place, tokens, tok_p, mem, mem_p, cotangent, cot_p, vec,
    )

    both = jnp.stack([biases[0], biases_x[0]]).astype(F32)
    qb, vb, ub = both[:, :width], both[:, width : 2 * width], both[:, 2 * width :]
    none = jnp.zeros((2, 128), F32)
    bias = jnp.concatenate([qb[:, :128], none, vb[:, :128], qb[:, 128:], vb[:, 128:], none], axis=1)
    at_own = x_at * 2 + c_at
    at_peer = x_at * 2 + 1 - c_at
    split = jnp.stack([split_point[at_own], split_point[at_peer]])
    length = jnp.stack([text_length[at_own], text_length[at_peer]])
    patch = jnp.stack([patch_mask[at_own], patch_mask[at_peer]]).astype(F32)
    patch = jnp.pad(patch, ((0, 0), (0, SLOTS - PATCHES)))[:, :, None]

    w, y, p, ctx, part = call(
        attend_kernel,
        [
            ((2, features, features), BF16), ((2, 2, KEYS, 640), BF16), ((2, 2, 3, KEYS, TEXT), BF16),
            ((2, 2, TEXT, 256), BF16), ((2, TEXT, features), F32),
        ],
        split, length, *attn_rows, *attn_quads, x, bias.reshape(2, 1, 640), patch,
        smem=2,
    )
    part = part.astype(BF16)
    part_in = links.send(part, links.c)

    quarter = ((half, hidden), BF16)
    res, _, mid_t, u, hid, slope, d00, d01, d10, d11 = call(
        up_kernel,
        [
            ((2 * TEXT, features), F32), ((2 * TEXT, features), BF16), ((features, 2 * TEXT), BF16),
            ((2, features, hidden), BF16), ((2, 2 * TEXT, hidden), BF16), ((2, 2 * TEXT, hidden), BF16),
        ]
        + [quarter] * 4,
        part, part_in, tok_r, vec_r, cot_t, ub.reshape(2, 1, hidden), *up_rows,
    )
    down_sum = links.scatter_rows(d00, d01, d10, d11)

    layer, mid_grad, up_bias_part, u00, u01, u10, u11 = call(
        down_kernel,
        [((2, TEXT, features), BF16), ((2, TEXT, features), BF16), ((2, hidden), F32)] + [quarter] * 4,
        u, hid, slope, mid_t, cot_r, *down_rows,
        scratch=[pltpu.VMEM((2, features, hidden), BF16), pltpu.VMEM((2, 2 * TEXT, hidden), BF16)],
    )
    grad_in = links.send(mid_grad, links.c)
    layer_in = links.send(layer[1], links.c)
    up_sum = links.scatter_rows(u00, u01, u10, u11)

    rg, ag_t, dy, back_o, back_p, sums, bias_part = call(
        attend_back_kernel,
        [
            ((TEXT, features), F32), ((features, 2 * TEXT), BF16), ((2, 2, KEYS, 640), BF16),
            ((KEYS, features), F32), ((KEYS, features), BF16), ((8, features), F32), ((2, 1, 640), F32),
        ],
        mid_grad, grad_in, res, cot_r, vec_r, w, y, p,
        scratch=[pltpu.VMEM((2 * TEXT, features), BF16), pltpu.VMEM((2, KEYS, features), F32)],
    )
    back_in = links.send(back_p, links.c)
    a00, a01, a10, a11, c0, c1, c2, c3 = call(
        weight_kernel,
        [((half, LEFT), BF16)] * 4 + [((features // 2, RIGHT), BF16)] * 4,
        xt, ag_t, dy, ctx,
    )
    left_sum = links.scatter_rows(a00, a01, a10, a11)
    right_sum = links.scatter_quads([c0, c1, c2, c3])

    layer_out, input_grad, memory_grad, vec_sum = call(
        last_kernel,
        [((TEXT, features), BF16), ((TEXT, features), F32), ((PATCHES, features), F32), ((8, features), F32)],
        back_o, back_in, tok_r[:TEXT], mem_r, rg, res[:TEXT], layer, layer_in, vec_r, hot, sums,
    )

    bias_part = bias_part.reshape(2, 640)
    q_part = jnp.concatenate([bias_part[:, 0:128], bias_part[:, 384:448]], axis=1)
    v_part = jnp.concatenate([bias_part[:, 256:384], bias_part[:, 448:512]], axis=1)
    m_own, m_peer = mp_at, mp_at ^ 2
    slots = jnp.arange(mp, dtype=jnp.int32)[:, None]

    def spread(pair):
        return (
            jnp.where(slots == m_own, pair[0:1], 0.0) + jnp.where(slots == m_peer, pair[1:2], 0.0)
        ).reshape(-1, features)

    stack = jnp.concatenate([vec_sum[0:6], spread(q_part), spread(v_part), spread(up_bias_part)], axis=0)
    stack = links.add_all(stack)
    at = dp_at * mp + mp_at
    few = features // (dp * mp)
    vectors = lax.dynamic_slice(stack[:8], (0, at * few), (8, few))
    many = up_bias.shape[0] // dp
    up_bias_sum = lax.dynamic_slice(stack[8:].reshape(-1), (at * many,), (many,))

    query_sum = jnp.concatenate([left_sum[:, 0:128], right_sum[:, 0:64]], axis=1)
    key_sum = jnp.concatenate([left_sum[:, 128:256], right_sum[:, 128:192]], axis=1)
    value_sum = jnp.concatenate([left_sum[:, 256:384], right_sum[:, 64:128]], axis=1)
    out_sum = jnp.concatenate([left_sum[:, 384:512], right_sum[:, 192:256]], axis=1).T
    return (
        layer_out, input_grad, memory_grad,
        query_sum, key_sum, value_sum, out_sum, up_sum, down_sum.T,
        vectors[6], vectors[7], up_bias_sum,
        vectors[2], vectors[3], vectors[4], vectors[5], vectors[0], vectors[1],
    )


def solution(mesh):
    rows = P(AXES, None)
    flat = P(AXES)
    in_specs = (
        rows, rows, P("dp"), P("dp"), P("dp", None),
        P("dp", "mp"), P("mp"), P("dp", "mp"), P("dp", "mp"), P("mp"),
        P("mp", "dp"), P(), P(), P(), P(), P(),
        P("dp", "mp"), P("mp"), P("mp", "dp"), P(), rows,
    )
    out_specs = (
        rows, rows, rows,
        P("dp", "mp"), P("dp", "mp"), P("dp", "mp"), P("mp", "dp"), P("dp", "mp"), P("mp", "dp"),
    ) + (flat,) * 9
    return jax.shard_map(
        per_device, mesh=mesh, in_specs=in_specs, out_specs=out_specs, check_vma=False
    )
```

time: 849 us -> 301 us (0.35)
  waiting for transfers between devices: 507 us -> 74.8 us
  blocking collectives: 190 us -> 0 us
  starting transfers between devices: 2.64 us -> 83.2 us
  Pallas kernels: 0 us -> 77.8 us
  matrix products: 72 us -> 0 us
  local copies, waits for them, and re-layouts: 23.1 us -> 40.9 us
  between operations: 17.2 us -> 1.97 us
  other arithmetic: 29 us -> 17.9 us
    reduce_scatter x9 -> x0, waiting for transfers between devices: 396 us -> none  [the longest x1 72.3 us: per_device(): lax.psum_scatter(up_grad, 'dp', scatter_dimension=0, tiled=True)]
    all_gather x4 -> x0, blocking collectives: 132 us -> none  [the longest x1 35 us: per_device(): lax.all_gather(out_weight, 'dp', axis=1, tiled=True)]
    all_gather x7 -> x0, waiting for transfers between devices: 108 us -> none  [the longest x1 39.1 us: per_device(): lax.all_gather(down_weight, 'dp', axis=1, tiled=True)]
    ppermute x0 -> x68, starting transfers between devices: none -> 83.2 us  [send(): return lax.ppermute(a, AXES, pairs)]
    pallas_call x0 -> x7, Pallas kernels: none -> 77.8 us  [call(): pl.pallas_call(kernel, out_shape=[jax.ShapeDtypeStruct(s, d) for s, d in...]
    ppermute x0 -> x68, waiting for transfers between devices: none -> 74.8 us  [send(): return lax.ppermute(a, AXES, pairs)]
    dot_general x33 -> x0, matrix products: 69.3 us -> none  [the longest x1 5.72 us: per_device(): jnp.einsum('nd,fd->nf', cot_all, full_down, preferred_element_type=jnp.fl...]
    unnamed x2 -> x0, blocking collectives: 57.8 us -> none
  transfers between devices with their start and end apart: 18 -> 68, of which waited for: 14 -> 20; matrix products, arithmetic and copies ran while one was open for 11% -> 17% of each run, Pallas kernels for 0% -> 21%
where the time goes in v1:
time: 301 us; the launch traced here: 297 us
  starting transfers between devices  83.2 us (28%)
  Pallas kernels  77.8 us (26%)
  waiting for transfers between devices  74.8 us (25%)
  local copies, waits for them, and re-layouts  40.9 us (14%)
  other arithmetic  17.9 us (6%)
    ppermute x68, starting transfers between devices, send(): return lax.ppermute(a, AXES, pairs)  83.2 us
    pallas_call x7, Pallas kernels, call(): pl.pallas_call(kernel, out_shape=[jax.ShapeDtypeStruct(s, d) for s, d in...  77.8 us
    ppermute x68, waiting for transfers between devices, send(): return lax.ppermute(a, AXES, pairs)  74.8 us
    unnamed x118, local copies, waits for them, and re-layouts  9.67 us
  transfers between devices with their start and end apart: 68, of which 20 were waited for; matrix products, arithmetic and copies ran while one was open for 17% of the time, Pallas kernels for 21%

profile of v1, /device:TPU:0, one launch (start us, length us, event | category | flops | bytes accessed | tf_op | source)
XLA Modules:
  0.0 296.5 jit_solution(685198014947456791)
XLA Ops:
  4.0 3.1 %collective-permute-start = (bf16[96,512]{1,0:T(8,128)(2,1)S(1)}, bf16[96,512]{1,0:T(8,128)(2,1)S(1)}, u32[]{:S(2)}, u32[]{:S(2)}) collective-permute-start(bf16[96,512]{1,0:T(8,128)(2,1)S(1)} %pad_maximum_fusion.9), channel_id=1, source_target_pairs={{0,8},{1,9},{2,10},{3,11},{4,12},{5,13},{6,14},{7,15},{8,16},{9,17... | collective-permute-start | bytes 294920 | tf_op jit(solution)/shard_map/ppermute | solution.py:410
  7.0 2.6 collective-permute-start.1
  26.0 2.9 collective-permute-start.20
  31.7 8.9 %collective-permute-done.19 = bf16[96,768]{1,0:T(8,128)(2,1)S(1)} collective-permute-done((bf16[96,768]{1,0:T(8,128)(2,1)S(1)}, bf16[96,768]{1,0:T(8,128)(2,1)S(1)}, u32[]{:S(2)}, u32[]{:S(2)}) %collective-permute-start.19) | collective-permute-done | bytes 147488 | tf_op jit(solution)/shard_map/ppermute | solution.py:410
  43.0 3.9 %collective-permute-start.10 = (bf16[384,256]{1,0:T(8,128)(2,1)S(1)}, bf16[384,256]{1,0:T(8,128)(2,1)S(1)}, u32[]{:S(2)}, u32[]{:S(2)}) collective-permute-start(bf16[384,256]{1,0:T(8,128)(2,1)S(1)} %pad_maximum_fusion.8.z0), channel_id=1, source_target_pairs={{0,8},{1,9},{2,10},{3,11},{4,12},{5,13},{6,14},{7,15},{8,16},{9,17... | collective-permute-start | bytes 589832 | tf_op jit(solution)/shard_map/ppermute | solution.py:410
  46.9 5.3 %collective-permute-done.26 = bf16[96,768]{1,0:T(8,128)(2,1)} collective-permute-done((bf16[96,768]{1,0:T(8,128)(2,1)S(1)}, bf16[96,768]{1,0:T(8,128)(2,1)}, u32[]{:S(2)}, u32[]{:S(2)}) %collective-permute-start.26) | collective-permute-done | bytes 147488 | tf_op jit(solution)/shard_map/ppermute | solution.py:410
  52.2 3.2 %pad_add_fusion = (s32[2]{0:T(128)}, s32[2]{0:T(128)}) fusion(s32[1]{0:T(128)} %get-tuple-element.224, s32[1]{0:T(128)} %get-tuple-element.223, s32[1]{0:T(128)} %get-tuple-element.222, s32[1]{0:T(128)} %get-tuple-element.221), kind=kLoop, calls=%fused_computation.92 | loop fusion | flops 4 | bytes 32 | tf_op jit(solution)/shard_map/stack | solution.py:561
  60.3 3.0 %collective-permute-done.11.z2 = bf16[384,256]{1,0:T(8,128)(2,1)S(1)} collective-permute-done((bf16[384,256]{1,0:T(8,128)(2,1)S(1)}, bf16[384,256]{1,0:T(8,128)(2,1)S(1)}, u32[]{:S(2)}, u32[]{:S(2)}) %collective-permute-start.11) | collective-permute-done | bytes 196640 | tf_op jit(solution)/shard_map/ppermute | solution.py:410
  80.8 8.3 %shard_map.340 = (bf16[2,512,768]{2,1,0:T(8,128)(2,1)}, bf16[768,1024]{1,0:T(8,128)(2,1)}, bf16[512,768]{1,0:T(8,128)(2,1)}, bf16[512,768]{1,0:T(8,128)(2,1)}, b...) custom-call(s32[768,1]{1,0:T(8,128)} %fusion.3.place, ...), custom_call_target="tpu_custom_call" | custom-call | bytes 9513984 | tf_op jit(solution)/shard_map/pallas_call | solution.py:60
  89.8 17.7 %shard_map.341 = (bf16[2,768,768]{2,1,0:T(8,128)(2,1)}, bf16[2,2,512,640]{3,2,1,0:T(8,128)(2,1)}, bf16[2,2,3,512,256]{4,3,2,1,0:T(8,128)(2,1)}, bf16[2,2,256,256]{3,2,1,0:T(8,128)(2,1)}, f32[2,256,768]{2,1,0:T(8,128)}) custom-call(s32[2]{0:T(128)} %get-tuple-element.225.split, s32[2]{0:T(128)} %get-tuple-element.226.length, bf16[384,512]{1,0:T(8,128)(2,1)} %copy-done.4, ...), custom_call_target="tpu_custom_call" | custom-call | bytes 14162960 | tf_op jit(solution)/shard_map/pallas_call | solution.py:60
  121.4 3.2 %collective-permute-done.24.peer_d1 = bf16[192,768]{1,0:T(8,128)(2,1)} collective-permute-done((bf16[192,768]{1,0:T(8,128)(2,1)}, bf16[192,768]{1,0:T(8,128)(2,1)}, u32[]{:S(2)}, u32[]{:S(2)}) %collective-permute-start.24) | collective-permute-done | bytes 294944 | tf_op jit(solution)/shard_map/ppermute | solution.py:410
  124.6 9.1 %shard_map.342 = (f32[512,768]{1,0:T(8,128)}, bf16[512,768]{1,0:T(8,128)(2,1)}, bf16[768,512]{1,0:T(8,128)(2,1)}, bf16[2,768,768]{2,1,0:T(8,128)(2,1)}, bf16[2,5...) custom-call(bf16[2,256,768]{2,1,0:T(8,128)(2,1)} %copy-done.1, ...), custom_call_target="tpu_custom_call" | custom-call | bytes 16570368 | tf_op jit(solution)/shard_map/pallas_call | solution.py:60
  134.4 9.6 %shard_map.343 = (bf16[2,256,768]{2,1,0:T(8,128)(2,1)}, bf16[2,256,768]{2,1,0:T(8,128)(2,1)}, f32[2,768]{1,0:T(2,128)}, bf16[384,768]{1,0:T(8,128)(2,1)}, bf16[3...) custom-call(bf16[2,768,768]{2,1,0:T(8,128)(2,1)} %get-tuple-element.71.u_ref, ...), custom_call_target="tpu_custom_call" | custom-call | bytes 13375488 | tf_op jit(solution)/shard_map/pallas_call | solution.py:60
  151.5 5.9 %collective-permute-done.55 = bf16[192,768]{1,0:T(8,128)(2,1)S(1)} collective-permute-done((bf16[192,768]{1,0:T(8,128)(2,1)S(1)}, bf16[192,768]{1,0:T(8,128)(2,1)S(1)}, u32[]{:S(2)}, u32[]{:S(2)}) %collective-permute-start.55) | collective-permute-done | bytes 294944 | tf_op jit(solution)/shard_map/ppermute | solution.py:410
  159.7 3.0 %collective-permute-done.48 = bf16[192,768]{1,0:T(8,128)(2,1)S(1)} collective-permute-done((bf16[192,768]{1,0:T(8,128)(2,1)S(1)}, bf16[192,768]{1,0:T(8,128)(2,1)S(1)}, u32[]{:S(2)}, u32[]{:S(2)}) %collective-permute-start.48) | collective-permute-done | bytes 294944 | tf_op jit(solution)/shard_map/ppermute | solution.py:410
  163.4 3.9 %collective-permute-done.50 = bf16[192,768]{1,0:T(8,128)(2,1)S(1)} collective-permute-done((bf16[192,768]{1,0:T(8,128)(2,1)S(1)}, bf16[192,768]{1,0:T(8,128)(2,1)S(1)}, u32[]{:S(2)}, u32[]{:S(2)}) %collective-permute-start.50) | collective-permute-done | bytes 294944 | tf_op jit(solution)/shard_map/ppermute | solution.py:410
  169.8 19.7 %shard_map.344 = (f32[256,768]{1,0:T(8,128)}, bf16[768,512]{1,0:T(8,128)(2,1)}, bf16[2,2,512,640]{3,2,1,0:T(8,128)(2,1)}, f32[512,768]{1,0:T(8,128)}, bf16[512,7...) custom-call(bf16[2,256,768]{2,1,0:T(8,128)(2,1)} %get-tuple-element.76.grad, ...), custom_call_target="tpu_custom_call" | custom-call | bytes 18691072 | tf_op jit(solution)/shard_map/pallas_call | solution.py:60
  190.3 6.9 %shard_map.346 = (bf16[384,512]{1,0:T(8,128)(2,1)}, bf16[384,512]{1,0:T(8,128)(2,1)}, bf16[384,512]{1,0:T(8,128)(2,1)}, bf16[384,512]{1,0:T(8,128)(2,1)}, bf16[3...) custom-call(bf16[768,1024]{1,0:T(8,128)(2,1)} %get-tuple-element.91.xt_ref, ...), custom_call_target="tpu_custom_call" | custom-call | bytes 7864320 | tf_op jit(solution)/shard_map/pallas_call | solution.py:60
  207.0 3.1 %collective-permute-start.42 = (bf16[384,256]{1,0:T(8,128)(2,1)S(1)}, bf16[384,256]{1,0:T(8,128)(2,1)S(1)}, u32[]{:S(2)}, u32[]{:S(2)}) collective-permute-start(bf16[384,256]{1,0:T(8,128)(2,1)S(1)} %copy-done.55), channel_id=1, source_target_pairs={{0,24},{1,25},{2,26},{3,27},{4,28},{5,29},{6,30},{7,31},{8,0},{9,1... | collective-permute-start | bytes 589832 | tf_op jit(solution)/shard_map/ppermute | solution.py:410
  212.5 5.0 %collective-permute-done.42 = bf16[384,256]{1,0:T(8,128)(2,1)S(1)} collective-permute-done((bf16[384,256]{1,0:T(8,128)(2,1)S(1)}, bf16[384,256]{1,0:T(8,128)(2,1)S(1)}, u32[]{:S(2)}, u32[]{:S(2)}) %collective-permute-start.42) | collective-permute-done | bytes 196640 | tf_op jit(solution)/shard_map/ppermute | solution.py:410
  219.3 9.1 %collective-permute-done.43 = bf16[384,256]{1,0:T(8,128)(2,1)S(1)} collective-permute-done((bf16[384,256]{1,0:T(8,128)(2,1)S(1)}, bf16[384,256]{1,0:T(8,128)(2,1)S(1)}, u32[]{:S(2)}, u32[]{:S(2)}) %collective-permute-start.43) | collective-permute-done | bytes 196640 | tf_op jit(solution)/shard_map/ppermute | solution.py:410
  228.3 5.1 %collective-permute-start.61 = (bf16[96,768]{1,0:T(8,128)(2,1)S(1)}, bf16[96,768]{1,0:T(8,128)(2,1)S(1)}, u32[]{:S(2)}, u32[]{:S(2)}) collective-permute-start(bf16[96,768]{1,0:T(8,128)(2,1)S(1)} %get-tuple-element.173), channel_id=1, source_target_pairs={{0,8},{1,9},{2,10},{3,11},{4,12},{5,13},{6,14},{7,15},{8,16},{9,17... | collective-permute-start | bytes 442376 | tf_op jit(solution)/shard_map/ppermute | solution.py:410
  233.8 4.5 %collective-permute-start.53 = (bf16[96,768]{1,0:T(8,128)(2,1)S(1)}, bf16[96,768]{1,0:T(8,128)(2,1)S(1)}, u32[]{:S(2)}, u32[]{:S(2)}) collective-permute-start(bf16[96,768]{1,0:T(8,128)(2,1)S(1)} %get-tuple-element.179), channel_id=1, source_target_pairs={{0,16},{1,17},{2,18},{3,19},{4,20},{5,21},{6,22},{7,23},{8,24},{9,... | collective-permute-start | bytes 442376 | tf_op jit(solution)/shard_map/ppermute | solution.py:410
  238.3 2.7 collective-permute-done.60
  250.9 3.5 %collective-permute-done.47 = bf16[96,256]{1,0:T(8,128)(2,1)S(1)} collective-permute-done((bf16[96,256]{1,0:T(8,128)(2,1)S(1)}, bf16[96,256]{1,0:T(8,128)(2,1)S(1)}, u32[]{:S(2)}, u32[]{:S(2)}) %collective-permute-start.47) | collective-permute-done | bytes 49184 | tf_op jit(solution)/shard_map/ppermute | solution.py:410
  254.6 3.9 %collective-permute-start.39 = (bf16[96,512]{1,0:T(8,128)(2,1)S(1)}, bf16[96,512]{1,0:T(8,128)(2,1)S(1)}, u32[]{:S(2)}, u32[]{:S(2)}) collective-permute-start(bf16[96,512]{1,0:T(8,128)(2,1)S(1)} %get-tuple-element.182), channel_id=1, source_target_pairs={{0,24},{1,25},{2,26},{3,27},{4,28},{5,29},{6,30},{7,31},{8,0},{9,1... | collective-permute-start | bytes 294920 | tf_op jit(solution)/shard_map/ppermute | solution.py:410
  260.3 2.2 collective-permute-start.41
  262.6 7.4 %collective-permute-done.40 = bf16[96,512]{1,0:T(8,128)(2,1)S(1)} collective-permute-done((bf16[96,512]{1,0:T(8,128)(2,1)S(1)}, bf16[96,512]{1,0:T(8,128)(2,1)S(1)}, u32[]{:S(2)}, u32[]{:S(2)}) %collective-permute-start.40) | collective-permute-done | bytes 98336 | tf_op jit(solution)/shard_map/ppermute | solution.py:410
  271.0 6.4 %shard_map.345 = (bf16[256,768]{1,0:T(8,128)(2,1)}, f32[256,768]{1,0:T(8,128)}, f32[196,768]{1,0:T(8,128)}, f32[8,768]{1,0:T(8,128)}) custom-call(f32[512,768]{1,0:T(8,128)} %get-tuple-element.81.back_o, bf16[512,768]{1,0:T(8,128)(2,1)} %copy-done.12, bf16[256,768]{1,0:T(8,128)(2,1)} %slice.282.tok_r, bf16[256,768]{1,0:T(8,128)(2,1)} %get-tuple-element.83.mem_r, ...), custom_call_target="tpu_custom_call" | custom-call | bytes 8957952 | tf_op jit(solution)/shard_map/pallas_call | solution.py:60
  281.7 2.6 collective-permute-done.63
  285.5 3.0 %collective-permute-done.64 = f32[12,768]{1,0:T(8,128)S(1)} collective-permute-done((f32[12,768]{1,0:T(8,128)S(1)}, f32[12,768]{1,0:T(8,128)S(1)}, u32[]{:S(2)}, u32[]{:S(2)}) %collective-permute-start.64) | collective-permute-done | bytes 36896 | tf_op jit(solution)/shard_map/ppermute | solution.py:410
  289.6 2.8 collective-permute-start.67
  (341 shorter events, 113.1 us)
Async XLA Ops:
  4.0 21.7 %collective-permute-start = (bf16[96,512]{1,0:T(8,128)(2,1)S(1)}, bf16[96,512]{1,0:T(8,128)(2,1)S(1)}, u32[]{:S(2)}, u32[]{:S(2)}) collective-permute-start(bf16[96,512]{1,0:T(8,128)(2,1)S(1)} %pad_maximum_fusion.9), channel_id=1, source_target_pairs={{0,8},{1,9},{2,10},{3,11},{4,12},{5,13},{6,14},{7,15},{8,16},{9,17... | collective-permute-start | bytes 294920 | tf_op jit(solution)/shard_map/ppermute | solution.py:410
  7.0 18.9 %collective-permute-start.1 = (bf16[96,512]{1,0:T(8,128)(2,1)S(1)}, bf16[96,512]{1,0:T(8,128)(2,1)S(1)}, u32[]{:S(2)}, u32[]{:S(2)}) collective-permute-start(bf16[96,512]{1,0:T(8,128)(2,1)S(1)} %pad_maximum_fusion.9), channel_id=1, source_target_pairs={{0,16},{1,17},{2,18},{3,19},{4,20},{5,21},{6,22},{7,23},{8,24},{9,... | collective-permute-start | bytes 294920 | tf_op jit(solution)/shard_map/ppermute | solution.py:410
  25.6 14.9 %collective-permute-start.19 = (bf16[96,768]{1,0:T(8,128)(2,1)S(1)}, bf16[96,768]{1,0:T(8,128)(2,1)S(1)}, u32[]{:S(2)}, u32[]{:S(2)}) collective-permute-start(bf16[96,768]{1,0:T(8,128)(2,1)S(1)} %copy-done.39), channel_id=1, source_target_pairs={{0,16},{1,17},{2,18},{3,19},{4,20},{5,21},{6,22},{7,23},{8,24},{9,... | collective-permute-start | bytes 442376 | tf_op jit(solution)/shard_map/ppermute | solution.py:410
  26.0 15.6 %collective-permute-start.20 = (bf16[96,768]{1,0:T(8,128)(2,1)S(1)}, bf16[96,768]{1,0:T(8,128)(2,1)}, u32[]{:S(2)}, u32[]{:S(2)}) collective-permute-start(bf16[96,768]{1,0:T(8,128)(2,1)S(1)} %copy-done.39), channel_id=1, source_target_pairs={{0,24},{1,25},{2,26},{3,27},{4,28},{5,29},{6,30},{7,31},{8,0},{9,1... | collective-permute-start | bytes 442376 | tf_op jit(solution)/shard_map/ppermute | solution.py:410
  28.9 14.1 %collective-permute-start.25 = (bf16[96,768]{1,0:T(8,128)(2,1)S(1)}, bf16[96,768]{1,0:T(8,128)(2,1)S(1)}, u32[]{:S(2)}, u32[]{:S(2)}) collective-permute-start(bf16[96,768]{1,0:T(8,128)(2,1)S(1)} %bitcast.38), channel_id=1, source_target_pairs={{0,8},{1,9},{2,10},{3,11},{4,12},{5,13},{6,14},{7,15},{8,16},{9,17... | collective-permute-start | bytes 442376 | tf_op jit(solution)/shard_map/ppermute | solution.py:410
  29.4 22.8 %collective-permute-start.26 = (bf16[96,768]{1,0:T(8,128)(2,1)S(1)}, bf16[96,768]{1,0:T(8,128)(2,1)}, u32[]{:S(2)}, u32[]{:S(2)}) collective-permute-start(bf16[96,768]{1,0:T(8,128)(2,1)S(1)} %bitcast.39), channel_id=1, source_target_pairs={{0,16},{1,17},{2,18},{3,19},{4,20},{5,21},{6,22},{7,23},{8,24},{9,... | collective-permute-start | bytes 442376 | tf_op jit(solution)/shard_map/ppermute | solution.py:410
  31.0 34.2 %collective-permute-start.3 = (bf16[384,512]{1,0:T(8,128)(2,1)S(1)}, bf16[384,512]{1,0:T(8,128)(2,1)S(1)}, u32[]{:S(2)}, u32[]{:S(2)}) collective-permute-start(bf16[384,512]{1,0:T(8,128)(2,1)S(1)} %pad_maximum_fusion.5.own), channel_id=1, source_target_pairs={{0,4},{1,5},{2,6},{3,7},{4,0},{5,1},{6,2},{7,3},{8,12},{9,13},{10,... | collective-permute-start | bytes 1179656 | tf_op jit(solution)/shard_map/ppermute | solution.py:410
  40.5 19.2 %collective-permute-start.27 = (bf16[96,768]{1,0:T(8,128)(2,1)S(1)}, bf16[96,768]{1,0:T(8,128)(2,1)}, u32[]{:S(2)}, u32[]{:S(2)}) collective-permute-start(bf16[96,768]{1,0:T(8,128)(2,1)S(1)} %bitcast.40), channel_id=1, source_target_pairs={{0,24},{1,25},{2,26},{3,27},{4,28},{5,29},{6,30},{7,31},{8,0},{9,1... | collective-permute-start | bytes 442376 | tf_op jit(solution)/shard_map/ppermute | solution.py:410
  41.6 26.1 %collective-permute-start.4 = (bf16[384,512]{1,0:T(8,128)(2,1)S(1)}, bf16[384,512]{1,0:T(8,128)(2,1)S(1)}, u32[]{:S(2)}, u32[]{:S(2)}) collective-permute-start(bf16[384,512]{1,0:T(8,128)(2,1)S(1)} %pad_maximum_fusion.5.own), channel_id=1, source_target_pairs={{0,2},{1,3},{2,0},{3,1},{4,6},{5,7},{6,4},{7,5},{8,10},{9,11},{10,... | collective-permute-start | bytes 1179656 | tf_op jit(solution)/shard_map/ppermute | solution.py:410
  43.0 16.7 %collective-permute-start.10 = (bf16[384,256]{1,0:T(8,128)(2,1)S(1)}, bf16[384,256]{1,0:T(8,128)(2,1)S(1)}, u32[]{:S(2)}, u32[]{:S(2)}) collective-permute-start(bf16[384,256]{1,0:T(8,128)(2,1)S(1)} %pad_maximum_fusion.8.z0), channel_id=1, source_target_pairs={{0,8},{1,9},{2,10},{3,11},{4,12},{5,13},{6,14},{7,15},{8,16},{9,17... | collective-permute-start | bytes 589832 | tf_op jit(solution)/shard_map/ppermute | solution.py:410
  59.7 15.4 %collective-permute-start.14 = (bf16[256,768]{1,0:T(8,128)(2,1)S(1)}, bf16[256,768]{1,0:T(8,128)(2,1)S(1)}, u32[]{:S(2)}, u32[]{:S(2)}) collective-permute-start(bf16[256,768]{1,0:T(8,128)(2,1)S(1)} %pad.8.mem_o), channel_id=1, source_target_pairs={{0,1},{1,0},{2,3},{3,2},{4,5},{5,4},{6,7},{7,6},{8,9},{9,8},{10,11... | collective-permute-start | bytes 1179656 | tf_op jit(solution)/shard_map/ppermute | solution.py:410
  59.8 16.9 %collective-permute-start.13 = (bf16[256,768]{1,0:T(8,128)(2,1)S(1)}, bf16[256,768]{1,0:T(8,128)(2,1)S(1)}, u32[]{:S(2)}, u32[]{:S(2)}) collective-permute-start(bf16[256,768]{1,0:T(8,128)(2,1)S(1)} %copy-done.24), channel_id=1, source_target_pairs={{0,1},{1,0},{2,3},{3,2},{4,5},{5,4},{6,7},{7,6},{8,9},{9,8},{10,11... | collective-permute-start | bytes 1179656 | tf_op jit(solution)/shard_map/ppermute | solution.py:410
  64.0 14.2 %collective-permute-start.15 = (bf16[256,768]{1,0:T(8,128)(2,1)S(1)}, bf16[256,768]{1,0:T(8,128)(2,1)S(1)}, u32[]{:S(2)}, u32[]{:S(2)}) collective-permute-start(bf16[256,768]{1,0:T(8,128)(2,1)S(1)} %copy-done.25), channel_id=1, source_target_pairs={{0,1},{1,0},{2,3},{3,2},{4,5},{5,4},{6,7},{7,6},{8,9},{9,8},{10,11... | collective-permute-start | bytes 1179656 | tf_op jit(solution)/shard_map/ppermute | solution.py:410
  73.1 16.1 %collective-permute-start.6 = (bf16[192,512]{1,0:T(8,128)(2,1)}, bf16[192,512]{1,0:T(8,128)(2,1)S(1)}, u32[]{:S(2)}, u32[]{:S(2)}) collective-permute-start(bf16[192,512]{1,0:T(8,128)(2,1)} %slice.350), channel_id=1, source_target_pairs={{0,4},{1,5},{2,6},{3,7},{4,0},{5,1},{6,2},{7,3},{8,12},{9,13},{10,... | collective-permute-start | bytes 589832 | tf_op jit(solution)/shard_map/ppermute | solution.py:410
  75.2 34.0 %collective-permute-start.21 = (bf16[384,768]{1,0:T(8,128)(2,1)}, bf16[384,768]{1,0:T(8,128)(2,1)}, u32[]{:S(2)}, u32[]{:S(2)}) collective-permute-start(bf16[384,768]{1,0:T(8,128)(2,1)} %constant_dynamic-update-slice_fusion.own), channel_id=1, source_target_pairs={{0,4},{1,5},{2,6},{3,7},{4,0},{5,1},{6,2},{7,3},{8,12},{9,13},{10,... | collective-permute-start | bytes 1769480 | tf_op jit(solution)/shard_map/ppermute | solution.py:410
  76.7 36.0 %collective-permute-start.22 = (bf16[384,768]{1,0:T(8,128)(2,1)}, bf16[384,768]{1,0:T(8,128)(2,1)}, u32[]{:S(2)}, u32[]{:S(2)}) collective-permute-start(bf16[384,768]{1,0:T(8,128)(2,1)} %constant_dynamic-update-slice_fusion.own), channel_id=1, source_target_pairs={{0,2},{1,3},{2,0},{3,1},{4,6},{5,7},{6,4},{7,5},{8,10},{9,11},{10,... | collective-permute-start | bytes 1769480 | tf_op jit(solution)/shard_map/ppermute | solution.py:410
  78.2 37.7 %collective-permute-start.28 = (bf16[384,768]{1,0:T(8,128)(2,1)S(1)}, bf16[384,768]{1,0:T(8,128)(2,1)S(1)}, u32[]{:S(2)}, u32[]{:S(2)}) collective-permute-start(bf16[384,768]{1,0:T(8,128)(2,1)S(1)} %pad_maximum_fusion.own), channel_id=1, source_target_pairs={{0,4},{1,5},{2,6},{3,7},{4,0},{5,1},{6,2},{7,3},{8,12},{9,13},{10,... | collective-permute-start | bytes 1769480 | tf_op jit(solution)/shard_map/ppermute | solution.py:410
  78.7 38.5 %collective-permute-start.29 = (bf16[384,768]{1,0:T(8,128)(2,1)S(1)}, bf16[384,768]{1,0:T(8,128)(2,1)S(1)}, u32[]{:S(2)}, u32[]{:S(2)}) collective-permute-start(bf16[384,768]{1,0:T(8,128)(2,1)S(1)} %pad_maximum_fusion.own), channel_id=1, source_target_pairs={{0,2},{1,3},{2,0},{3,1},{4,6},{5,7},{6,4},{7,5},{8,10},{9,11},{10,... | collective-permute-start | bytes 1769480 | tf_op jit(solution)/shard_map/ppermute | solution.py:410
  109.1 15.5 %collective-permute-start.17 = (bf16[2,256,768]{2,1,0:T(8,128)(2,1)S(1)}, bf16[2,256,768]{2,1,0:T(8,128)(2,1)}, u32[]{:S(2)}, u32[]{:S(2)}) collective-permute-start(bf16[2,256,768]{2,1,0:T(8,128)(2,1)S(1)} %convert_element_type.167.part), channel_id=1, source_target_pairs={{0,1},{1,0},{2,3},{3,2},{4,5},{5,4},{6,7},{7,6},{8,9},{9,8},{10,11... | collective-permute-start | bytes 2359304 | tf_op jit(solution)/shard_map/ppermute | solution.py:410
  116.7 17.0 %collective-permute-start.30 = (bf16[192,768]{1,0:T(8,128)(2,1)}, bf16[192,768]{1,0:T(8,128)(2,1)}, u32[]{:S(2)}, u32[]{:S(2)}) collective-permute-start(bf16[192,768]{1,0:T(8,128)(2,1)} %slice.354), channel_id=1, source_target_pairs={{0,2},{1,3},{2,0},{3,1},{4,6},{5,7},{6,4},{7,5},{8,10},{9,11},{10,... | collective-permute-start | bytes 884744 | tf_op jit(solution)/shard_map/ppermute | solution.py:410
  117.3 16.4 %collective-permute-start.31 = (bf16[192,768]{1,0:T(8,128)(2,1)S(1)}, bf16[192,768]{1,0:T(8,128)(2,1)S(1)}, u32[]{:S(2)}, u32[]{:S(2)}) collective-permute-start(bf16[192,768]{1,0:T(8,128)(2,1)S(1)} %slice.355), channel_id=1, source_target_pairs={{0,4},{1,5},{2,6},{3,7},{4,0},{5,1},{6,2},{7,3},{8,12},{9,13},{10,... | collective-permute-start | bytes 884744 | tf_op jit(solution)/shard_map/ppermute | solution.py:410
  144.1 24.9 %collective-permute-start.32 = (bf16[2,256,768]{2,1,0:T(8,128)(2,1)}, bf16[2,256,768]{2,1,0:T(8,128)(2,1)S(1)}, u32[]{:S(2)}, u32[]{:S(2)}) collective-permute-start(bf16[2,256,768]{2,1,0:T(8,128)(2,1)} %get-tuple-element.76.grad), channel_id=1, source_target_pairs={{0,1},{1,0},{2,3},{3,2},{4,5},{5,4},{6,7},{7,6},{8,9},{9,8},{10,11... | collective-permute-start | bytes 2359304 | tf_op jit(solution)/shard_map/ppermute | solution.py:410
  145.9 124.1 %collective-permute-start.34 = (bf16[256,768]{1,0:T(8,128)(2,1)}, bf16[256,768]{1,0:T(8,128)(2,1)}, u32[]{:S(2)}, u32[]{:S(2)}) collective-permute-start(bf16[256,768]{1,0:T(8,128)(2,1)} %slice_bitcast_fusion), channel_id=1, source_target_pairs={{0,1},{1,0},{2,3},{3,2},{4,5},{5,4},{6,7},{7,6},{8,9},{9,8},{10,11... | collective-permute-start | bytes 1179656 | tf_op jit(solution)/shard_map/ppermute | solution.py:410
  159.0 44.7 %collective-permute-start.56 = (bf16[384,768]{1,0:T(8,128)(2,1)S(1)}, bf16[384,768]{1,0:T(8,128)(2,1)S(1)}, u32[]{:S(2)}, u32[]{:S(2)}) collective-permute-start(bf16[384,768]{1,0:T(8,128)(2,1)S(1)} %pad_maximum_fusion.3), channel_id=1, source_target_pairs={{0,4},{1,5},{2,6},{3,7},{4,0},{5,1},{6,2},{7,3},{8,12},{9,13},{10,... | collective-permute-start | bytes 1769480 | tf_op jit(solution)/shard_map/ppermute | solution.py:410
  162.7 42.3 %collective-permute-start.58 = (bf16[384,768]{1,0:T(8,128)(2,1)S(1)}, bf16[384,768]{1,0:T(8,128)(2,1)}, u32[]{:S(2)}, u32[]{:S(2)}) collective-permute-start(bf16[384,768]{1,0:T(8,128)(2,1)S(1)} %pad_maximum_fusion.4), channel_id=1, source_target_pairs={{0,2},{1,3},{2,0},{3,1},{4,6},{5,7},{6,4},{7,5},{8,10},{9,11},{10,... | collective-permute-start | bytes 1769480 | tf_op jit(solution)/shard_map/ppermute | solution.py:410
  167.3 39.7 %collective-permute-start.49 = (bf16[384,768]{1,0:T(8,128)(2,1)S(1)}, bf16[384,768]{1,0:T(8,128)(2,1)}, u32[]{:S(2)}, u32[]{:S(2)}) collective-permute-start(bf16[384,768]{1,0:T(8,128)(2,1)S(1)} %pad_maximum_fusion.1), channel_id=1, source_target_pairs={{0,4},{1,5},{2,6},{3,7},{4,0},{5,1},{6,2},{7,3},{8,12},{9,13},{10,... | collective-permute-start | bytes 1769480 | tf_op jit(solution)/shard_map/ppermute | solution.py:410
  169.0 41.1 %collective-permute-start.51 = (bf16[384,768]{1,0:T(8,128)(2,1)S(1)}, bf16[384,768]{1,0:T(8,128)(2,1)}, u32[]{:S(2)}, u32[]{:S(2)}) collective-permute-start(bf16[384,768]{1,0:T(8,128)(2,1)S(1)} %pad_maximum_fusion.2), channel_id=1, source_target_pairs={{0,2},{1,3},{2,0},{3,1},{4,6},{5,7},{6,4},{7,5},{8,10},{9,11},{10,... | collective-permute-start | bytes 1769480 | tf_op jit(solution)/shard_map/ppermute | solution.py:410
  205.1 28.5 %collective-permute-start.37 = (bf16[192,512]{1,0:T(8,128)(2,1)}, bf16[192,512]{1,0:T(8,128)(2,1)S(1)}, u32[]{:S(2)}, u32[]{:S(2)}) collective-permute-start(bf16[192,512]{1,0:T(8,128)(2,1)} %get-tuple-element.186), channel_id=1, source_target_pairs={{0,4},{1,5},{2,6},{3,7},{4,0},{5,1},{6,2},{7,3},{8,12},{9,13},{10,... | collective-permute-start | bytes 589832 | tf_op jit(solution)/shard_map/ppermute | solution.py:410
  210.1 18.2 %collective-permute-start.43 = (bf16[384,256]{1,0:T(8,128)(2,1)S(1)}, bf16[384,256]{1,0:T(8,128)(2,1)S(1)}, u32[]{:S(2)}, u32[]{:S(2)}) collective-permute-start(bf16[384,256]{1,0:T(8,128)(2,1)S(1)} %copy-done.54), channel_id=1, source_target_pairs={{0,16},{1,17},{2,18},{3,19},{4,20},{5,21},{6,22},{7,23},{8,24},{9,... | collective-permute-start | bytes 589832 | tf_op jit(solution)/shard_map/ppermute | solution.py:410
  211.7 16.6 %collective-permute-start.44 = (bf16[384,256]{1,0:T(8,128)(2,1)S(1)}, bf16[384,256]{1,0:T(8,128)(2,1)S(1)}, u32[]{:S(2)}, u32[]{:S(2)}) collective-permute-start(bf16[384,256]{1,0:T(8,128)(2,1)S(1)} %copy-done.53), channel_id=1, source_target_pairs={{0,8},{1,9},{2,10},{3,11},{4,12},{5,13},{6,14},{7,15},{8,16},{9,17... | collective-permute-start | bytes 589832 | tf_op jit(solution)/shard_map/ppermute | solution.py:410
  217.5 16.3 %collective-permute-start.59 = (bf16[96,768]{1,0:T(8,128)(2,1)S(1)}, bf16[96,768]{1,0:T(8,128)(2,1)S(1)}, u32[]{:S(2)}, u32[]{:S(2)}) collective-permute-start(bf16[96,768]{1,0:T(8,128)(2,1)S(1)} %get-tuple-element.172), channel_id=1, source_target_pairs={{0,24},{1,25},{2,26},{3,27},{4,28},{5,29},{6,30},{7,31},{8,0},{9,1... | collective-permute-start | bytes 442376 | tf_op jit(solution)/shard_map/ppermute | solution.py:410
  254.4 15.7 %collective-permute-start.33 = (bf16[512,768]{1,0:T(8,128)(2,1)S(1)}, bf16[512,768]{1,0:T(8,128)(2,1)S(1)}, u32[]{:S(2)}, u32[]{:S(2)}) collective-permute-start(bf16[512,768]{1,0:T(8,128)(2,1)S(1)} %copy-done.52), channel_id=1, source_target_pairs={{0,1},{1,0},{2,3},{3,2},{4,5},{5,4},{6,7},{7,6},{8,9},{9,8},{10,11... | collective-permute-start | bytes 2359304 | tf_op jit(solution)/shard_map/ppermute | solution.py:410
  (92 other events, 1146.7 us)

commit v2 on v1

v2 whole, which is shorter than its diff:
```python
import functools

import jax
import jax.numpy as jnp
from jax import lax
from jax.experimental import pallas as pl
from jax.experimental.pallas import tpu as pltpu
from jax.sharding import PartitionSpec as P

HEAD = 64
TEXT = 256
PATCHES = 196
SLOTS = 256
KEYS = SLOTS + TEXT
EPS = 1e-06
NEG = -1000000000.0
SCALE = HEAD ** (-0.5)
F32 = jnp.float32
BF16 = jnp.bfloat16
AXES = ("dp", "mp")

CUT = 384


def nn(a, b):
    return lax.dot_general(a, b, (((1,), (0,)), ((), ())), preferred_element_type=F32)


def nt(a, b):
    return lax.dot_general(a, b, (((1,), (1,)), ((), ())), preferred_element_type=F32)


def eye(n):
    rows = lax.broadcasted_iota(jnp.int32, (n, n), 0)
    cols = lax.broadcasted_iota(jnp.int32, (n, n), 1)
    return (rows == cols).astype(F32).astype(BF16)


def standard(matrix):
    average = jnp.mean(matrix, axis=-1, keepdims=True)
    centered = matrix - average
    inverse = lax.rsqrt(jnp.mean(centered * centered, axis=-1, keepdims=True) + EPS)
    return centered * inverse, inverse


def standard_back(normed, inverse, grad_out, gain):
    scaled = grad_out * gain
    return inverse * (
        scaled
        - jnp.mean(scaled, axis=-1, keepdims=True)
        - normed * jnp.mean(scaled * normed, axis=-1, keepdims=True)
    )


UNIT = 1e9
COST = {
    "prep_kernel": 8.0, "attend_kernel": 17.0, "up_kernel": 9.0, "down_kernel": 9.0,
    "gate_kernel": 12.0, "add_kernel": 30.0, "attend_back_kernel": 19.0, "weight_kernel": 6.0, "last_kernel": 6.0,
}


def call(kernel, out_shapes, *args, scratch=(), smem=0, after=(), anywhere=False):
    name = getattr(kernel, "func", kernel).__name__
    waits = len(after)

    def body(*refs):
        return kernel(*refs[waits:])

    place = pl.BlockSpec(memory_space=pl.ANY if anywhere else pltpu.VMEM)
    return pl.pallas_call(
        body,
        out_shape=[jax.ShapeDtypeStruct(s, d) for s, d in out_shapes],
        in_specs=[pl.BlockSpec(memory_space=pl.ANY)] * waits
        + [pl.BlockSpec(memory_space=pltpu.SMEM)] * smem
        + [place] * (len(args) - smem),
        out_specs=[place] * len(out_shapes),
        scratch_shapes=list(scratch),
        compiler_params=pltpu.CompilerParams(vmem_limit_bytes=56 * 1024 * 1024),
        cost_estimate=pl.CostEstimate(
            flops=int(COST.get(name, 2.0) * UNIT), bytes_accessed=0, transcendentals=0
        ),
        name=name,
    )(*after, *args)


def pack_kernel(q, k, v, o, a_ref):
    ot = nt(eye(q.shape[0]), o[...]).astype(BF16)
    a_ref[:, 0:128] = q[:, 0:128]
    a_ref[:, 128:256] = k[:, 0:128]
    a_ref[:, 256:384] = v[:, 0:128]
    a_ref[:, 384:512] = jnp.concatenate([q[:, 128:192], v[:, 128:192]], axis=1)
    a_ref[:, 512:640] = jnp.concatenate([k[:, 128:192], ot[:, 128:192]], axis=1)
    a_ref[:, 640:768] = ot[:, 0:128]


def stack_kernel(count, *refs):
    extra = (len(refs) - count - 1) // 2
    pieces, others, out, copies = refs[:count], refs[count : count + extra], refs[count + extra], refs[count + extra + 1 :]
    rows = pieces[0].shape[0]
    for k, piece in enumerate(pieces):
        out[k * rows : (k + 1) * rows, :] = piece[...]
    for src, dst in zip(others, copies):
        dst[...] = src[...]


def cut_kernel(a, b, out_a, out_b):
    cut = out_a.shape[0]
    out_a[...] = a[0:cut, :]
    out_b[...] = b[cut : 2 * cut, :]


def gate_kernel(token):
    token[...] = jnp.zeros_like(token)


def add_kernel(top, far_top, bottom, far_bottom, out_top, out_bottom):
    cut = far_top.shape[0]
    out_top[0:cut, :] = (top[0:cut, :].astype(F32) + far_top[...].astype(F32)).astype(BF16)
    out_top[cut:, :] = top[cut:, :]
    out_bottom[0:cut, :] = bottom[0:cut, :]
    out_bottom[cut:, :] = (bottom[cut:, :].astype(F32) + far_bottom[...].astype(F32)).astype(BF16)


def total_kernel(count, *refs):
    rows = refs[count].shape[0]
    for k, dst in enumerate(refs[count:]):
        at = slice(k * rows, (k + 1) * rows)
        value = refs[0][at, :].astype(F32)
        for other in refs[1:count]:
            value += other[at, :].astype(F32)
        dst[...] = value.astype(dst.dtype)


def total_vec_kernel(count, vec, *refs):
    vec_out, dsts = refs[count], refs[count + 1 :]
    rows, more = dsts[0].shape[0], vec.shape[0]
    total_kernel(count, *refs[:count], *(d.at[0:rows, :] for d in dsts))
    first = 4 * rows
    sums = vec[...]
    for other in refs[1:count]:
        sums += other[first : first + more, :].astype(F32) + other[first + more : first + 2 * more, :].astype(F32)
    vec_out[...] = sums
    high = sums.astype(BF16)
    low = (sums - high.astype(F32)).astype(BF16)
    for dst in dsts[1:]:
        dst[rows : rows + more, :] = high
        dst[rows + more : rows + 2 * more, :] = low


def finish_kernel(*refs):
    vec, (parts, (q, k, v, o, vec_out)) = refs[0], (refs[1:-5], refs[-5:])
    rows, more = parts[0].shape[0], vec.shape[0]
    total = parts[0][...]
    sums = vec[...]
    for part in parts[1:]:
        total += part[0:rows, :].astype(F32)
        sums += part[rows : rows + more, :].astype(F32) + part[rows + more : rows + 2 * more, :].astype(F32)
    vec_out[...] = sums
    q[...] = jnp.concatenate([total[:, 0:128], total[:, 384:448]], axis=1)
    k[...] = jnp.concatenate([total[:, 128:256], total[:, 512:576]], axis=1)
    v[...] = jnp.concatenate([total[:, 256:384], total[:, 448:512]], axis=1)
    out = jnp.concatenate([total[:, 640:768], total[:, 576:640]], axis=1)
    high = out.astype(BF16)
    low = (out - high.astype(F32)).astype(BF16)
    unit = eye(out.shape[1])
    o[...] = nt(unit, high) + nt(unit, low)


def place_of(depth, r, z, y, count):
    rel = lax.broadcasted_iota(jnp.int32, (count, 1), 0)
    half = count // 2
    ry = (rel >= half).astype(jnp.int32)
    rest = rel - ry * half
    rz = jnp.zeros_like(rel)
    for k in range(1, depth):
        rz += (rest >= k * r).astype(jnp.int32)
    az = z - rz
    az += depth * (az < 0).astype(jnp.int32)
    ay = y + ry - 2 * y * ry
    return az * (2 * r) + ay * r + rest - rz * r


def prep_kernel(
    depth, where, tok_o, tok_p, mem_o, mem_p, cot_o, cot_p, vec, patch, bias_o, bias_p,
    x_ref, xt_ref, tok_r, cot_r, cot_t, mem_r, vec_r, hot_ref, ok_ref, bias_ref, up_ref, unscaled,
):
    features = tok_o.shape[1]
    lane = lax.broadcasted_iota(jnp.int32, (features, features), 1)
    place = place_of(depth, features // (2 * depth), where[0], where[1], features)
    hot_ref[...] = (lane == place).astype(F32).astype(BF16)
    gain = vec[0:1, :].astype(F32)
    shift = vec[1:2, :].astype(F32)
    vec_r[...] = nt(vec[...], hot_ref[...])
    for m, bias in enumerate((bias_o, bias_p)):
        row = bias[...].astype(F32)
        bias_ref[m] = jnp.zeros_like(bias_ref[m])
        bias_ref[m, :, 0:128] = row[:, 0:128]
        bias_ref[m, :, 256:512] = row[:, 128:384]
        up_ref[m] = row[:, 384:]

    rows = lax.broadcasted_iota(jnp.int32, (SLOTS, PATCHES), 0)
    cols = lax.broadcasted_iota(jnp.int32, (SLOTS, PATCHES), 1)
    columns = nt((rows == cols).astype(F32), (patch[...] > 0).astype(F32))
    which = lax.broadcasted_iota(jnp.int32, columns.shape, 1)
    for at in range(2):
        one = jnp.sum(jnp.where(which == where[2 + at], columns, 0.0), axis=1, keepdims=True)
        ok_ref[at] = jnp.broadcast_to(one, (SLOTS, 128))

    for at, (mem, tok) in enumerate(((mem_o, tok_o), (mem_p, tok_p))):
        normed, _ = standard(tok[...].astype(F32))
        low = (normed * gain + shift).astype(BF16)
        x_ref[at, SLOTS:KEYS, :] = nt(low, hot_ref[...]).astype(BF16)
        unscaled[at, SLOTS:KEYS, :] = nt(normed.astype(BF16), hot_ref[...]).astype(BF16)
        xt_ref[:, at * KEYS + SLOTS : (at + 1) * KEYS] = nt(hot_ref[...], low).astype(BF16)
        normed, _ = standard(mem[...].astype(F32))
        normed = jnp.concatenate([normed, jnp.zeros((SLOTS - PATCHES, features), F32)], axis=0)
        unscaled[at, 0:SLOTS, :] = nt(normed.astype(BF16), hot_ref[...]).astype(BF16)
        low = (normed * gain + shift).astype(BF16)
        x_ref[at, 0:SLOTS, :] = nt(low, hot_ref[...]).astype(BF16)
        xt_ref[:, at * KEYS : at * KEYS + SLOTS] = nt(hot_ref[...], low).astype(BF16)
    raw = jnp.concatenate([mem_o[...].astype(F32), jnp.zeros((SLOTS - PATCHES, features), F32)], axis=0)
    mem_r[...] = nt(raw.astype(BF16), hot_ref[...]).astype(BF16)
    for at, (tok, cot) in enumerate(((tok_o, cot_o), (tok_p, cot_p))):
        rows = slice(at * TEXT, (at + 1) * TEXT)
        tok_r[rows, :] = nt(tok[...], hot_ref[...]).astype(BF16)
        cot_r[rows, :] = nt(cot[...], hot_ref[...]).astype(BF16)
        cot_t[:, rows] = nt(hot_ref[...], cot[...]).astype(BF16)


def masked(raw, cond):
    return jnp.where(cond, raw * SCALE, NEG)


def assemble(quads, w_ref):
    half = quads[0].shape[0]
    for k, quad in enumerate(quads):
        w_ref[k // 2, (k % 2) * half : (k % 2 + 1) * half, :] = quad[...]


def arrange(depth, where, whole, w_ref):
    rows = whole.shape[1]
    half = depth * rows
    x = where[4] // 2
    for m in range(2):
        for ry in range(2):
            for rz in range(depth):
                az = lax.rem(where[0] - rz + depth, depth)
                ay = where[1] if ry == 0 else 1 - where[1]
                ax = x if m == 0 else 1 - x
                first = ry * half + rz * rows
                w_ref[m, first : first + rows, :] = whole[(az * 2 + ay) * 2 + ax]


def attend_kernel(
    where, split, length,
    own, own_y, peer, far_top, far_bottom, x_ref, bias, ok_ref,
    w_ref, y_ref, p_ref, ctx_ref, part_ref, out_ref,
):
    assemble((own, own_y, peer), w_ref)
    half, cut = own.shape[0], far_top.shape[0]
    w_ref[1, half : half + cut, :] = far_top[...]
    w_ref[1, half + cut : 2 * half, :] = far_bottom[...]
    lane = lax.broadcasted_iota(jnp.int32, (TEXT, 128), 1)
    lane_k = lax.broadcasted_iota(jnp.int32, (KEYS, 128), 1)
    zero = jnp.zeros((TEXT, 128), BF16)
    unit = eye(128)
    unit_t = eye(TEXT)
    key_place = lax.broadcasted_iota(jnp.int32, (TEXT, TEXT), 0)
    query_place = lax.broadcasted_iota(jnp.int32, (TEXT, TEXT), 1)
    out_ref[...] = jnp.zeros_like(out_ref)

    def step(at, carry):
        e, m = at // 2, at % 2
        x = x_ref[e]
        w = w_ref[m]
        b = bias[m]
        y1 = nn(x, w[:, 0:384]) + b[:, 0:384]
        y_ref[m, e, :, 0:384] = y1.astype(BF16)
        y2 = nn(x, w[:, 384:640]) + b[:, 384:640]
        y_ref[m, e, :, 384:512] = y2[:, 0:128].astype(BF16)
        y_ref[m, e, :, 512:640] = jnp.where(lane_k < HEAD, y2[:, 128:256], 0.0).astype(BF16)

        patch_ok = jnp.concatenate([ok_ref[e], ok_ref[e]], axis=1) > 0.0
        prefix, valid = split[where[2 + e]], length[where[2 + e]]
        text_ok = ((key_place < prefix) | (key_place <= query_place)) & (key_place < valid)

        q01 = y_ref[m, e, SLOTS:KEYS, 0:128]
        q2 = y_ref[m, e, SLOTS:KEYS, 384:512]
        v01t = nt(unit, y_ref[m, e, :, 256:384]).astype(BF16)
        v2t = nt(unit, y_ref[m, e, :, 384:512]).astype(BF16)
        ctx01 = []
        for head in range(3):
            if head == 0:
                q, first, vt = jnp.where(lane < HEAD, q01, zero), 128, v01t[0:HEAD]
            elif head == 1:
                q, first, vt = jnp.where(lane >= HEAD, q01, zero), 128, v01t[HEAD:128]
            else:
                q, first, vt = jnp.where(lane < HEAD, q2, zero), 512, v2t[HEAD:128]
            s_mem = masked(nt(y_ref[m, e, 0:SLOTS, first : first + 128], q), patch_ok)
            s_text = masked(nt(y_ref[m, e, SLOTS:KEYS, first : first + 128], q), text_ok)
            largest = jnp.maximum(
                jnp.max(s_mem, axis=0, keepdims=True), jnp.max(s_text, axis=0, keepdims=True)
            )
            e_mem = jnp.exp(s_mem - largest)
            e_text = jnp.exp(s_text - largest)
            total = jnp.sum(e_mem, axis=0, keepdims=True) + jnp.sum(e_text, axis=0, keepdims=True)
            inverse = 1.0 / total
            p_mem = (e_mem * inverse).astype(BF16)
            p_text = (e_text * inverse).astype(BF16)
            p_ref[m, e, head, 0:SLOTS, :] = p_mem
            p_ref[m, e, head, SLOTS:KEYS, :] = p_text
            ctx01.append(nn(vt[:, 0:SLOTS], p_mem) + nn(vt[:, SLOTS:KEYS], p_text))
        c01t = jnp.concatenate([ctx01[0], ctx01[1]], axis=0).astype(BF16)
        c2t = jnp.concatenate([jnp.zeros((HEAD, TEXT), F32), ctx01[2]], axis=0).astype(BF16)
        c01 = nt(unit_t, c01t).astype(BF16)
        c2 = nt(unit_t, c2t).astype(BF16)
        ctx_ref[m, e, :, 0:128] = c01
        ctx_ref[m, e, :, 128:256] = c2
        out_ref[e] += nt(c01, w[:, 640:768]) + nt(c2, w[:, 512:640])
        return carry

    lax.fori_loop(0, 4, step, 0)
    part_ref[...] = out_ref[...].astype(BF16)


def gelu_pair(v):
    c = 0.7978845608028654
    square = v * v
    t = jnp.tanh(c * v * (1.0 + 0.044715 * square))
    gelu = 0.5 * v * (1.0 + t)
    slope = 0.5 * (1.0 + t) + 0.5 * v * (1.0 - t * t) * (c * (1.0 + 3 * 0.044715 * square))
    return gelu, slope


def up_kernel(
    depth, where, part, part_in, tok_r, vec_r, cot_t, bias, whole,
    res_ref, mid_t, hid_ref, slope_ref, g00, g01, g10, g11_top, g11_bottom, mid_ref, u_ref,
):
    half = g00.shape[0]
    arrange(depth, where, whole, u_ref)
    for e in range(2):
        rows = slice(e * TEXT, (e + 1) * TEXT)
        res = (
            tok_r[rows, :].astype(F32)
            + (part[e].astype(F32) + part_in[1 - e].astype(F32))
            + vec_r[4:5, :]
        )
        res_ref[rows, :] = res
        normed, _ = standard(res)
        mid_ref[rows, :] = (normed * vec_r[2:3, :] + vec_r[3:4, :]).astype(BF16)
    mid_t[...] = nt(eye(mid_ref.shape[1]), mid_ref[...]).astype(BF16)
    for m in range(2):
        for e in range(2):
            rows = slice(e * TEXT, (e + 1) * TEXT)
            pre = nn(mid_ref[rows, :], u_ref[m]) + bias[m]
            gelu, slope = gelu_pair(pre)
            hid_ref[m, rows, :] = gelu.astype(BF16)
            slope_ref[m, rows, :] = slope.astype(BF16)
    for dst, m, first in (
        (g11_top, 1, half), (g11_bottom, 1, half + half // 2), (g01, 0, half), (g10, 1, 0), (g00, 0, 0)
    ):
        dst[...] = nn(cot_t[first : first + dst.shape[0], :], hid_ref[m]).astype(BF16)


def down_kernel(
    depth, where, whole, hid_ref, slope_ref, mid_t, cot_r, w0, w1, w2, w3,
    out_o, grad_ref, bias_ref, g00, g01, g10, g11_top, g11_bottom, d_ref, pre_ref, u_ref,
):
    half = g00.shape[0]
    arrange(depth, where, whole, u_ref)
    assemble((w0, w1, w2, w3), d_ref)
    bias_ref[...] = jnp.zeros_like(bias_ref)
    for m in range(2):
        for e in range(2):
            rows = slice(e * TEXT, (e + 1) * TEXT)
            pre = (nn(cot_r[rows, :], d_ref[m]) * slope_ref[m, rows, :].astype(F32)).astype(BF16)
            pre_ref[m, rows, :] = pre
            bias_ref[m : m + 1, :] += jnp.sum(pre.astype(F32), axis=0, keepdims=True)
    for e in range(2):
        rows = slice(e * TEXT, (e + 1) * TEXT)
        grad_ref[e] = (nt(pre_ref[0, rows, :], u_ref[0]) + nt(pre_ref[1, rows, :], u_ref[1])).astype(BF16)
    for e, out in enumerate((out_o, grad_ref.at[2])):
        rows = slice(e * TEXT, (e + 1) * TEXT)
        out[...] = (nt(hid_ref[0, rows, :], d_ref[0]) + nt(hid_ref[1, rows, :], d_ref[1])).astype(BF16)
    for dst, m, first in (
        (g11_top, 1, half), (g11_bottom, 1, half + half // 2), (g01, 0, half), (g10, 1, 0), (g00, 0, 0)
    ):
        dst[...] = nn(mid_t[first : first + dst.shape[0], :], pre_ref[m]).astype(BF16)


def attend_back_kernel(
    where, grad, grad_in, res_ref, cot_r, vec_r, w_ref, y_ref, p_ref, unscaled, up_bias,
    rg_ref, agt_ref, dy_ref, back_o, back_p, sums, bias_ref, ag_ref, back_ref,
):
    lane = lax.broadcasted_iota(jnp.int32, (TEXT, 128), 1)
    row = lax.broadcasted_iota(jnp.int32, (128, TEXT), 0)
    zero = jnp.zeros((TEXT, 128), BF16)
    unit = eye(128)
    unit_t = eye(TEXT)
    for e in range(2):
        rows = slice(e * TEXT, (e + 1) * TEXT)
        mid_grad = grad[e].astype(F32) + grad_in[1 - e].astype(F32)
        normed, inverse = standard(res_ref[rows, :])
        cot = cot_r[rows, :].astype(F32)
        resid = cot + standard_back(normed, inverse, mid_grad, vec_r[2:3, :])
        low = resid.astype(BF16)
        ag_ref[rows, :] = low
        if e == 0:
            rg_ref[...] = resid
            sums[0:1, :] = jnp.sum(mid_grad * normed, axis=0, keepdims=True)
            sums[1:2, :] = jnp.sum(mid_grad, axis=0, keepdims=True)
            sums[2:3, :] = jnp.sum(low.astype(F32), axis=0, keepdims=True)
            sums[3:4, :] = jnp.sum(cot, axis=0, keepdims=True)
            sums[4:8, :] = jnp.zeros_like(sums[4:8, :])
    agt_ref[...] = nt(eye(ag_ref.shape[1]), ag_ref[...]).astype(BF16)
    bias_ref[...] = jnp.zeros_like(bias_ref)
    back_ref[...] = jnp.zeros_like(back_ref)

    def step(at, carry):
        e, m = at // 2, at % 2
        w = w_ref[m]
        ag = ag_ref[pl.ds(pl.multiple_of(e * TEXT, TEXT), TEXT), :]
        dc01 = nn(ag, w[:, 640:768]).astype(BF16)
        dc2 = nn(ag, w[:, 512:640]).astype(BF16)
        q01 = y_ref[m, e, SLOTS:KEYS, 0:128]
        q2 = y_ref[m, e, SLOTS:KEYS, 384:512]
        k01 = y_ref[m, e, :, 128:256]
        k2 = y_ref[m, e, :, 512:640]
        k01t = nt(unit, k01).astype(BF16)
        k2t = nt(unit, k2).astype(BF16)
        dk, dv, dqt = [], [], []
        for head in range(3):
            keep = (lane < HEAD) if head == 0 else (lane >= HEAD)
            if head < 2:
                dc = jnp.where(keep, dc01, zero)
                q = jnp.where(keep, q01, zero)
                v = y_ref[m, e, :, 256:384]
                kt = k01t[0:HEAD] if head == 0 else k01t[HEAD:128]
            else:
                dc = jnp.where(lane >= HEAD, dc2, zero)
                q = jnp.where(lane < HEAD, q2, zero)
                v = y_ref[m, e, :, 384:512]
                kt = k2t[0:HEAD]
            prob = p_ref[m, e, head]
            probs = prob.astype(F32)
            grad_p = nt(v, dc)
            dot = jnp.sum(probs * grad_p, axis=0, keepdims=True)
            score = (probs * (grad_p - dot)).astype(BF16)
            dk.append(nn(score, q))
            dv.append(nn(prob, dc))
            dqt.append(nn(kt, score))
        dk01 = ((dk[0] + dk[1]) * SCALE).astype(BF16)
        dk2 = (dk[2] * SCALE).astype(BF16)
        dv01 = (dv[0] + dv[1]).astype(BF16)
        dv2 = dv[2].astype(BF16)
        dq01 = nt(unit_t, (jnp.concatenate([dqt[0], dqt[1]], axis=0) * SCALE).astype(BF16))
        dq2 = nt(
            unit_t,
            (jnp.concatenate([dqt[2], jnp.zeros((HEAD, TEXT), F32)], axis=0) * SCALE).astype(BF16),
        )
        dy_ref[m, e, 0:SLOTS, 0:128] = zero
        dy_ref[m, e, SLOTS:KEYS, 0:128] = dq01.astype(BF16)
        dy_ref[m, e, :, 128:256] = dk01
        dy_ref[m, e, :, 256:384] = dv01
        dy_ref[m, e, 0:SLOTS, 384:512] = dv2[0:SLOTS]
        dy_ref[m, e, SLOTS:KEYS, 384:512] = (dq2 + dv2[SLOTS:KEYS].astype(F32)).astype(BF16)
        dy_ref[m, e, :, 512:640] = dk2
        dy = dy_ref[m, e]
        bias_ref[m] += jnp.sum(dy.astype(F32), axis=0, keepdims=True)
        back_ref[e] += nt(dy, w[:, 0:640])
        return carry

    lax.fori_loop(0, 4, step, 0)
    back_o[...] = back_ref[0]
    back_p[0:KEYS, :] = back_ref[1].astype(BF16)
    for e in range(2):
        sums[4:5, :] += jnp.sum(back_ref[e] * unscaled[e].astype(F32), axis=0, keepdims=True)
        sums[5:6, :] += jnp.sum(back_ref[e], axis=0, keepdims=True)
    index = lax.broadcasted_iota(jnp.int32, (4, 1), 0)
    own, peer = index == where[4], index == where[5]
    sums[8:12, 0:640] = jnp.where(own, bias_ref[0], 0.0) + jnp.where(peer, bias_ref[1], 0.0)
    sums[8:12, 640:768] = jnp.zeros((4, 128), F32)
    sums[12:16, :] = jnp.where(own, up_bias[0:1, :], 0.0) + jnp.where(peer, up_bias[1:2, :], 0.0)
    high = sums[...].astype(BF16)
    back_p[KEYS : KEYS + 16, :] = high
    back_p[KEYS + 16 : KEYS + 32, :] = (sums[...] - high.astype(F32)).astype(BF16)


def weight_kernel(
    xt_ref, agt_ref, dy_ref, ctx_ref, sums, back_in, hot_ref, g00, g01, g10, g11, vec_ref,
):
    half = g00.shape[0]
    more = vec_ref.shape[0]
    vec = sums[...] + back_in[KEYS : KEYS + more, :].astype(F32) + back_in[KEYS + more :, :].astype(F32)
    vec_ref[...] = vec
    vec_ref[0:8, :] = restore(vec[0:8, :], hot_ref[...])
    high = vec_ref[...].astype(BF16)
    low = (vec_ref[...] - high.astype(F32)).astype(BF16)
    for dst in (g01, g10, g11):
        dst[half : half + more, :] = high
        dst[half + more : half + 2 * more, :] = low
    for dst, m, first in ((g11, 1, half), (g01, 0, half), (g10, 1, 0), (g00, 0, 0)):
        rows = slice(first, first + half)
        dy = dy_ref[m].reshape(2 * KEYS, 640)
        ctx = ctx_ref[m].reshape(2 * TEXT, 256)
        grad = nn(xt_ref[rows, :], dy)
        out = nn(agt_ref[rows, :], ctx)
        dst[0:half, 0:512] = grad[:, 0:512].astype(BF16)
        dst[0:half, 512:640] = (grad[:, 512:640] + out[:, 128:256]).astype(BF16)
        dst[0:half, 640:768] = out[:, 0:128].astype(BF16)


def restore(v, hot):
    high = v.astype(BF16)
    low = (v - high.astype(F32)).astype(BF16)
    return nn(high, hot) + nn(low, hot)


def last_kernel(
    back_o, back_in, tok_r, mem_r, rg_ref, res_ref, out_o, out_in, vec_r, hot_ref,
    layer_ref, in_ref, mem_ref,
):
    hot = hot_ref[...]
    gain = vec_r[0:1, :]
    layer = (
        res_ref[0:TEXT, :] + (out_o[...].astype(F32) + out_in[2].astype(F32)) + vec_r[5:6, :]
    ).astype(BF16)
    layer_ref[...] = nn(layer, hot).astype(BF16)
    mem_back = back_o[0:SLOTS, :] + back_in[0:SLOTS, :].astype(F32)
    text_back = back_o[SLOTS:KEYS, :] + back_in[SLOTS:KEYS, :].astype(F32)
    normed, inverse = standard(tok_r[0:TEXT, :].astype(F32))
    in_ref[...] = restore(rg_ref[...] + standard_back(normed, inverse, text_back, gain), hot)
    normed, inverse = standard(mem_r[...].astype(F32))
    mem_ref[...] = restore(standard_back(normed, inverse, mem_back, gain), hot)[0:PATCHES, :]


class Links:
    def __init__(self, dp, mp):
        self.dp, self.mp, self.depth = dp, mp, dp // 2
        self.x = self.pairs(lambda d, m: (d, m ^ 2))
        self.c = self.pairs(lambda d, m: (d, m ^ 1))
        self.y = self.pairs(lambda d, m: (d ^ 1, m))
        self.xy = self.pairs(lambda d, m: (d ^ 1, m ^ 2))

    def pairs(self, to):
        out = []
        for d in range(self.dp):
            for m in range(self.mp):
                d2, m2 = to(d, m)
                out.append((d * self.mp + m, d2 * self.mp + m2))
        return out

    def z(self, k):
        return self.pairs(lambda d, m: ((((d // 2 + k) % self.depth) * 2 + d % 2), m))

    def send(self, a, pairs):
        return lax.ppermute(a, AXES, pairs)

    def line(self, shard, *others, after=()):
        if self.depth == 4:
            pieces = [shard] + [self.send(shard, self.z(k)) for k in range(1, 4)]
            rows, lanes = shard.shape
            return call(
                functools.partial(stack_kernel, 4),
                [((4 * rows, lanes), BF16)] + [(o.shape, BF16) for o in others],
                *pieces, *others, after=after,
            )
        held = shard[None]
        step = 1
        while step < self.depth:
            held = jnp.concatenate([held, self.send(held, self.z(step))], axis=0)
            step *= 2
        return (held.reshape(-1, shard.shape[1]),) + others

    def home(self, after, *parts):
        rows, lanes = parts[0].shape
        if self.depth == 4:
            r = rows // 4
            own, *rest = call(
                functools.partial(total_kernel, len(parts)),
                [((r, lanes), F32)] + [((r, lanes), BF16)] * 3, *parts, after=after,
            )
            return [own] + [self.send(rest[k], self.z(-k - 1)) for k in range(3)]
        held = sum(p.astype(F32) for p in parts).reshape(self.depth, -1, lanes)
        step = self.depth // 2
        while step >= 1:
            held = held[:step] + self.send(held[step:].astype(BF16), self.z(-step)).astype(F32)
            step //= 2
        return [held[0]]

    def meet(self, after, g01, g10, far_top, far_bottom):
        to_y, to_x = call(
            add_kernel, [(g01.shape, BF16), (g10.shape, BF16)], g01, far_top, g10, far_bottom, after=after
        )
        return self.send(to_y, self.y), self.send(to_x, self.x), to_x

    def direct(self, g01, g10, g11):
        return self.send(g11, self.xy), self.send(g01, self.y), self.send(g10, self.x)

    def fold(self, after, *parts):
        if self.depth != 4:
            return self.home(after, *parts)[0], None
        rows, lanes = parts[0].shape
        near, far = call(
            functools.partial(total_kernel, len(parts)),
            [((rows // 2, lanes), F32), ((rows // 2, lanes), BF16)], *parts, after=after,
        )
        return near, self.send(far, self.z(-2))

    def fold_more(self, after, near, far):
        if self.depth != 4:
            return [near]
        rows, lanes = near.shape
        own, other = call(
            functools.partial(total_kernel, 2),
            [((rows // 2, lanes), F32), ((rows // 2, lanes), BF16)], near, far, after=after,
        )
        return [own, self.send(other, self.z(-1))]

    def home_with(self, after, vec, own, *got):
        rows, lanes = own.shape
        more = vec.shape[0]
        if self.depth == 4:
            r = rows // 4
            vec, own, *rest = call(
                functools.partial(total_vec_kernel, 1 + len(got)),
                [(vec.shape, F32), ((r, lanes), F32)] + [((r + 2 * more, lanes), BF16)] * 3,
                vec, own, *got, after=after,
            )
            return [vec, own] + [self.send(rest[k], self.z(-k - 1)) for k in range(3)]
        for g in got:
            vec = vec + g[rows : rows + more].astype(F32) + g[rows + more :].astype(F32)
        step = 1
        while step < self.depth:
            vec = vec + self.send(vec, self.z(step))
            step *= 2
        return [vec] + self.home((), own, *(g[:rows] for g in got))


def add_up(parts):
    total = parts[0]
    for part in parts[1:]:
        total = total + part.astype(F32)
    return total


def per_device(
    tokens, memory, split_point, text_length, patch_mask,
    query_weight, query_bias, key_weight, value_weight, value_bias,
    out_weight, out_bias, attn_gain, attn_shift, mlp_gain, mlp_shift,
    up_weight, up_bias, down_weight, down_bias, cotangent,
):
    features = tokens.shape[1]
    width = query_weight.shape[1]
    hidden = up_weight.shape[1]
    dp, mp = lax.axis_size("dp"), lax.axis_size("mp")
    links = Links(dp, mp)
    dp_at, mp_at = lax.axis_index("dp"), lax.axis_index("mp")
    r = features // dp
    half = features // 2

    sides = [[d * mp + 2 * i + c for d in range(dp) for i in range(mp // 2)] for c in range(2)]
    up_all = lax.all_gather(up_weight, AXES, axis=0, axis_index_groups=sides)

    biases = jnp.concatenate(
        [query_bias[:128], value_bias[:128], query_bias[128:], value_bias[128:], up_bias]
    ).reshape(1, -1)
    biases_x = links.send(biases, links.x)
    tok_p = links.send(tokens, links.c)
    mem_p = links.send(memory, links.c)
    cot_p = links.send(cotangent, links.c)
    (attn_own,) = call(
        pack_kernel, [((r, features), BF16)], query_weight, key_weight, value_weight, out_weight
    )

    where = jnp.stack([dp_at // 2, dp_at % 2, mp_at, mp_at ^ 1, mp_at, mp_at ^ 2]).astype(jnp.int32)
    blank = jnp.zeros_like(attn_gain)
    vec = jnp.stack(
        [attn_gain, attn_shift, mlp_gain, mlp_shift, out_bias, down_bias] + [blank] * 10
    )
    x, xt, tok_r, cot_r, cot_t, mem_r, vec_r, hot, ok, bias, ub, unscaled = call(
        functools.partial(prep_kernel, dp // 2),
        [
            ((2, KEYS, features), BF16), ((features, 2 * KEYS), BF16),
            ((2 * TEXT, features), BF16), ((2 * TEXT, features), BF16), ((features, 2 * TEXT), BF16),
            ((SLOTS, features), BF16), ((16, features), F32), ((features, features), BF16),
            ((2, SLOTS, 128), F32), ((2, 1, 640), F32), ((2, 1, hidden), F32),
            ((2, KEYS, features), BF16),
        ],
        where, tokens, tok_p, memory, mem_p, cotangent, cot_p, vec, patch_mask, biases, biases_x,
        smem=1, after=(attn_own,),
    )
    own, down_own = links.line(attn_own, down_weight.T, after=(ok,))
    own_y, peer = links.send(own, links.y), links.send(own, links.x)
    cut_y, cut_x = call(cut_kernel, [((half // 2, features), BF16)] * 2, own_y, peer)
    far_top, far_bottom = links.send(cut_y, links.x), links.send(cut_x, links.y)
    (down_rows,) = links.line(down_own, after=(cut_x,))
    quads_d = [
        down_rows, links.send(down_rows, links.y), links.send(down_rows, links.x), links.send(down_rows, links.xy)
    ]

    w, y, p, ctx, part = call(
        attend_kernel,
        [
            ((2, features, features), BF16), ((2, 2, KEYS, 640), BF16), ((2, 2, 3, KEYS, TEXT), BF16),
            ((2, 2, TEXT, 256), BF16), ((2, TEXT, features), BF16),
        ],
        where, split_point, text_length, own, own_y, peer, far_top, far_bottom,
        x, bias, ok,
        smem=3, scratch=[pltpu.VMEM((2, TEXT, features), F32)], after=(down_rows,),
    )
    part_in = links.send(part, links.c)
    (token,) = call(gate_kernel, [((8, 128), F32)], after=(part, *quads_d[1:]))

    quarter = ((half, hidden), BF16)
    eighth = ((half // 2, hidden), BF16)
    res, mid_t, hid, slope, d00, d01, d10, d11t, d11b = call(
        functools.partial(up_kernel, dp // 2),
        [
            ((2 * TEXT, features), F32), ((features, 2 * TEXT), BF16),
            ((2, 2 * TEXT, hidden), BF16), ((2, 2 * TEXT, hidden), BF16),
        ]
        + [quarter] * 3 + [eighth] * 2,
        where, part, part_in, tok_r, vec_r, cot_t, ub, up_all, smem=1, after=(token,),
        scratch=[pltpu.VMEM((2 * TEXT, features), BF16), pltpu.VMEM((2, features, hidden), BF16)],
    )
    d_far = links.send(d11t, links.x), links.send(d11b, links.y)

    layer_o, mid_grad, up_bias_part, u00, u01, u10, u11t, u11b = call(
        functools.partial(down_kernel, dp // 2),
        [((TEXT, features), BF16), ((3, TEXT, features), BF16), ((2, hidden), F32)]
        + [quarter] * 3 + [eighth] * 2,
        where, up_all, hid, slope, mid_t, cot_r, *quads_d, smem=1,
        scratch=[
            pltpu.VMEM((2, features, hidden), BF16), pltpu.VMEM((2, 2 * TEXT, hidden), BF16),
            pltpu.VMEM((2, features, hidden), BF16),
        ],
    )
    grad_in = links.send(mid_grad, links.c)
    d_y, d_x, token = links.meet((mid_grad,), d01, d10, *d_far)
    u_far = links.send(u11t, links.x), links.send(u11b, links.y)

    rg, ag_t, dy, back_o, back_p, sums = call(
        attend_back_kernel,
        [
            ((TEXT, features), F32), ((features, 2 * TEXT), BF16), ((2, 2, KEYS, 640), BF16),
            ((KEYS, features), F32), ((KEYS + 32, features), BF16), ((16, features), F32),
        ],
        where, mid_grad, grad_in, res, cot_r, vec_r, w, y, p, unscaled, up_bias_part, smem=1, after=(token,),
        scratch=[
            pltpu.VMEM((2, 1, 640), F32), pltpu.VMEM((2 * TEXT, features), BF16), pltpu.VMEM((2, KEYS, features), F32)
        ],
    )
    back_in = links.send(back_p, links.c)
    u_y, u_x, token = links.meet((dy, d_y, d_x), u01, u10, *u_far)
    a00, a01, a10, a11, stack = call(
        weight_kernel,
        [((half, features), BF16)] + [((half + 32, features), BF16)] * 3 + [((16, features), F32)],
        xt, ag_t, dy, ctx, sums, back_in, hot, after=(token,),
    )
    a_got = links.direct(a01, a10, a11)
    down_total, down_more = links.fold((a00,), d00, d_y, d_x)
    layer_out, input_grad, memory_grad = call(
        last_kernel,
        [((TEXT, features), BF16), ((TEXT, features), F32), ((PATCHES, features), F32)],
        back_o, back_in, tok_r, mem_r, rg, res, layer_o, grad_in, vec_r, hot, after=(down_total,),
    )
    down_parts = links.fold_more((input_grad,), down_total, down_more)
    up_total, up_more = links.fold((down_parts[0],), u00, u_y, u_x)
    up_parts = links.fold_more((), up_total, up_more)
    attn_parts = links.home_with((up_parts[0],), stack, a00, *a_got)
    query_sum, key_sum, value_sum, out_sum, stack = call(
        finish_kernel,
        [((r, width), F32)] * 3 + [((width, r), F32), (stack.shape, F32)], *attn_parts,
    )

    at = dp_at * mp + mp_at
    few = features // (dp * mp)
    q_bias = jnp.concatenate([stack[8:12, 0:128], stack[8:12, 384:448]], axis=1).reshape(1, features)
    v_bias = jnp.concatenate([stack[8:12, 256:384], stack[8:12, 448:512]], axis=1).reshape(1, features)
    vectors = lax.dynamic_slice(jnp.concatenate([stack[0:6], q_bias, v_bias]), (0, at * few), (8, few))
    many = up_bias.shape[0] // dp
    up_bias_sum = lax.dynamic_slice(stack[12:16].reshape(-1), (at * many,), (many,))

    return (
        layer_out, input_grad, memory_grad,
        query_sum, key_sum, value_sum, out_sum, add_up(up_parts), add_up(down_parts).T,
        vectors[6], vectors[7], up_bias_sum,
        vectors[2], vectors[3], vectors[4], vectors[5], vectors[0], vectors[1],
    )


def solution(mesh):
    rows = P(AXES, None)
    flat = P(AXES)
    in_specs = (
        rows, rows, P("dp"), P("dp"), P("dp", None),
        P("dp", "mp"), P("mp"), P("dp", "mp"), P("dp", "mp"), P("mp"),
        P("mp", "dp"), P(), P(), P(), P(), P(),
        P("dp", "mp"), P("mp"), P("mp", "dp"), P(), rows,
    )
    out_specs = (
        rows, rows, rows,
        P("dp", "mp"), P("dp", "mp"), P("dp", "mp"), P("mp", "dp"), P("dp", "mp"), P("mp", "dp"),
    ) + (flat,) * 9
    return jax.shard_map(
        per_device, mesh=mesh, in_specs=in_specs, out_specs=out_specs, check_vma=False
    )
```

time: 301 us -> 255 us (0.85); the launches traced: 297 us -> 254 us
  starting transfers between devices: 83.2 us -> 39.3 us
  Pallas kernels: 77.8 us -> 108 us
  other arithmetic: 17.9 us -> 1.57 us
  local copies, waits for them, and re-layouts: 40.9 us -> 25.1 us
  between operations: 1.97 us -> 14.5 us
  waiting for transfers between devices: 74.8 us -> 65.4 us
    ppermute x68 -> x38, starting transfers between devices: 83.2 us -> 39.3 us  [send(): return lax.ppermute(a, AXES, pairs)]
    pallas_call x7 -> x20, Pallas kernels: 77.8 us -> 108 us  [call(): pl.pallas_call(body, out_shape=[jax.ShapeDtypeStruct(s, d) for s, d in ou...]
    slice x36 -> x6, local copies, waits for them, and re-layouts: 15.6 us -> 4.32 us  [the longest x1 0.83 us: per_device(): stack[8:12, 448:512]]
    ppermute x68 -> x38, waiting for transfers between devices: 74.8 us -> 65.4 us  [send(): return lax.ppermute(a, AXES, pairs)]
    unnamed x118 -> x92, local copies, waits for them, and re-layouts: 9.67 us -> 15.5 us
    convert_element_type x13 -> x0, other arithmetic: 4.93 us -> none  [the longest x3 3.03 us: scatter_rows(): (g00.astype(F32) + from_y.astype(F32) + from_x.astype(F32)).astype(BF16)]
    concatenate x17 -> x2, other arithmetic: 4.33 us -> 0.09 us  [the longest x1 0.08 us: per_device(): jnp.concatenate([stack[0:6], q_bias, v_bias])]
    another operation x2 -> x0, other arithmetic: 3.29 us -> none  [the longest x1 3.18 us: per_device(): split = jnp.stack([split_point[at_own], split_point[at_peer]])]
  transfers between devices with their start and end apart: 68 -> 39, of which waited for: 20 -> 10; matrix products, arithmetic and copies ran while one was open for 17% -> 3% of each run, Pallas kernels for 21% -> 38%
where the time goes in v2:
time: 255 us; the launch traced here: 254 us
  Pallas kernels  108 us (42%)
  waiting for transfers between devices  65.4 us (26%)
  starting transfers between devices  39.3 us (15%)
  local copies, waits for them, and re-layouts  25.1 us (10%)
  between operations  14.5 us (6%)
    pallas_call x20, Pallas kernels, call(): pl.pallas_call(body, out_shape=[jax.ShapeDtypeStruct(s, d) for s, d in ou...  108 us
    ppermute x38, waiting for transfers between devices, send(): return lax.ppermute(a, AXES, pairs)  65.4 us
    ppermute x38, starting transfers between devices, send(): return lax.ppermute(a, AXES, pairs)  39.3 us
    unnamed x92, local copies, waits for them, and re-layouts  15.5 us
  transfers between devices with their start and end apart: 39, of which 10 were waited for; matrix products, arithmetic and copies ran while one was open for 3% of the time, Pallas kernels for 38%

profile of v2, /device:TPU:0, one launch (start us, length us, event | category | flops | bytes accessed | tf_op | source)
XLA Modules:
  0.0 254.0 jit_solution(13622865539308650001)
XLA Ops:
  9.6 2.1 concatenate.12
  11.8 2.6 %collective-permute-start.3 = (bf16[1,1152]{1,0:T(2,128)(2,1)S(1)}, bf16[1,1152]{1,0:T(2,128)(2,1)S(1)}, u32[]{:S(2)}, u32[]{:S(2)}) collective-permute-start(bf16[1,1152]{1,0:T(2,128)(2,1)S(1)} %reshape.48.refs_10_), channel_id=1, source_target_pairs={{0,2},{1,3},{2,0},{3,1},{4,6},{5,7},{6,4},{7,5},{8,10},{9,11},{10,... | collective-permute-start | bytes 6920 | tf_op jit(solution)/shard_map/ppermute | solution.py:557
  16.2 3.6 %collective-permute-start.6 = (bf16[96,768]{1,0:T(8,128)(2,1)}, bf16[96,768]{1,0:T(8,128)(2,1)S(1)}, u32[]{:S(2)}, u32[]{:S(2)}) collective-permute-start(bf16[96,768]{1,0:T(8,128)(2,1)} %pack_kernel.1.refs_0_.refs_1_), channel_id=1, source_target_pairs={{0,24},{1,25},{2,26},{3,27},{4,28},{5,29},{6,30},{7,31},{8,0},{9,1... | collective-permute-start | bytes 442376 | tf_op jit(solution)/shard_map/ppermute | solution.py:557
  24.3 9.5 %prep_kernel.1 = (bf16[2,512,768]{2,1,0:T(8,128)(2,1)}, bf16[768,1024]{1,0:T(8,128)(2,1)}, bf16[512,768]{1,0:T(8,128)(2,1)}, bf16[512,768]{1,0:T(8,128)(2,1)}, b...) custom-call(bf16[96,768]{1,0:T(8,128)(2,1)} %pack_kernel.1.refs_0_.r, ...), custom_call_target="tpu_custom_call" | custom-call | flops 8000000000 | tf_op jit(solution)/shard_map/prep_kernel/pallas_call | solution.py:70
  33.8 2.9 %collective-permute-done.5.refs_3_ = bf16[96,768]{1,0:T(8,128)(2,1)S(1)} collective-permute-done((bf16[96,768]{1,0:T(8,128)(2,1)}, bf16[96,768]{1,0:T(8,128)(2,1)S(1)}, u32[]{:S(2)}, u32[]{:S(2)}) %collective-permute-start.5) | collective-permute-done | bytes 147488 | tf_op jit(solution)/shard_map/ppermute | solution.py:557
  37.5 2.1 stack_kernel.2
  41.6 2.6 %collective-permute-start.10 = (bf16[96,768]{1,0:T(8,128)(2,1)}, bf16[96,768]{1,0:T(8,128)(2,1)S(1)}, u32[]{:S(2)}, u32[]{:S(2)}) collective-permute-start(bf16[96,768]{1,0:T(8,128)(2,1)} %get-tuple-element.95.refs_1_), channel_id=1, source_target_pairs={{0,16},{1,17},{2,18},{3,19},{4,20},{5,21},{6,22},{7,23},{8,24},{9,... | collective-permute-start | bytes 442376 | tf_op jit(solution)/shard_map/ppermute | solution.py:557
  44.2 2.0 collective-permute-start.9
  46.2 13.1 %collective-permute-done.8.refs_1_.refs_6_ = bf16[384,768]{1,0:T(8,128)(2,1)S(1)} collective-permute-done((bf16[384,768]{1,0:T(8,128)(2,1)}, bf16[384,768]{1,0:T(8,128)(2,1)S(1)}, u32[]{:S(2)}, u32[]{:S(2)}) %collective-permute-start.8) | collective-permute-done | bytes 589856 | tf_op jit(solution)/shard_map/ppermute | solution.py:557
  61.0 2.1 cut_kernel.1
  66.3 2.0 stack_kernel.3.refs_0_.refs_6_
  71.8 4.9 %collective-permute-done.12.refs_7_ = bf16[192,768]{1,0:T(8,128)(2,1)S(1)} collective-permute-done((bf16[192,768]{1,0:T(8,128)(2,1)}, bf16[192,768]{1,0:T(8,128)(2,1)S(1)}, u32[]{:S(2)}, u32[]{:S(2)}) %collective-permute-start.12) | collective-permute-done | bytes 294944 | tf_op jit(solution)/shard_map/ppermute | solution.py:557
  76.7 5.0 %collective-permute-done.13.refs_8_ = bf16[192,768]{1,0:T(8,128)(2,1)S(1)} collective-permute-done((bf16[192,768]{1,0:T(8,128)(2,1)}, bf16[192,768]{1,0:T(8,128)(2,1)S(1)}, u32[]{:S(2)}, u32[]{:S(2)}) %collective-permute-start.13) | collective-permute-done | bytes 294944 | tf_op jit(solution)/shard_map/ppermute | solution.py:557
  82.4 17.4 %attend_kernel.1 = (bf16[2,768,768]{2,1,0:T(8,128)(2,1)}, bf16[2,2,512,640]{3,2,1,0:T(8,128)(2,1)}, bf16[2,2,3,512,256]{4,3,2,1,0:T(8,128)(2,1)}, bf16[2,2,256,256]{3,2,1,0:T(8,128)(2,1)}, bf16[2,256,768]{2,1,0:T(8,128)(2,1)}) custom-call(bf16[384,768]{1,0:T(8,128)(2,1)} %stack_kernel.3.refs_0_.refs_6_, s32[6]{0:T(128)} %stack.51.refs_1_.refs_0_, s32[4]{0:T(128)} %refs_2_.5, ...), custom_call_target="tpu_custom_call" | custom-call | flops 16999999488 | tf_op jit(solution)/shard_map/attend_kernel/pallas_call | solution.py:70
  99.9 5.3 %collective-permute-done.15.refs_2_.refs_8_ = bf16[384,768]{1,0:T(8,128)(2,1)S(1)} collective-permute-done((bf16[384,768]{1,0:T(8,128)(2,1)}, bf16[384,768]{1,0:T(8,128)(2,1)S(1)}, u32[]{:S(2)}, u32[]{:S(2)}) %collective-permute-start.15) | collective-permute-done | bytes 589856 | tf_op jit(solution)/shard_map/ppermute | solution.py:557
  108.4 8.8 %up_kernel.1 = (f32[512,768]{1,0:T(8,128)}, bf16[768,512]{1,0:T(8,128)(2,1)}, bf16[2,512,768]{2,1,0:T(8,128)(2,1)}, bf16[2,512,768]{2,1,0:T(8,128)(2,1)}, bf16[3...) custom-call(f32[8,128]{1,0:T(8,128)} %gate_kernel.1.refs_0_, ...), custom_call_target="tpu_custom_call" | custom-call | flops 8999999488 | tf_op jit(solution)/shard_map/up_kernel/pallas_call | solution.py:70
  119.6 9.9 %down_kernel.1 = (bf16[256,768]{1,0:T(8,128)(2,1)}, bf16[3,256,768]{2,1,0:T(8,128)(2,1)}, f32[2,768]{1,0:T(2,128)}, bf16[384,768]{1,0:T(8,128)(2,1)}, bf16[384,7...) custom-call(s32[6]{0:T(128)} %stack.51.refs_1_.refs_0_, ...), custom_call_target="tpu_custom_call" | custom-call | flops 8999999488 | tf_op jit(solution)/shard_map/down_kernel/pallas_call | solution.py:70
  131.9 2.5 add_kernel.2
  137.9 21.1 %attend_back_kernel.1 = (f32[256,768]{1,0:T(8,128)}, bf16[768,512]{1,0:T(8,128)(2,1)}, bf16[2,2,512,640]{3,2,1,0:T(8,128)(2,1)}, f32[512,768]{1,0:T(8,128)}, bf1...) custom-call(bf16[384,768]{1,0:T(8,128)(2,1)} %get-tuple-element.113.refs_0_, s32[6]{0:T(128)} %stack.51.refs_1_.refs_0_, ...), custom_call_target="tpu_custom_call" | custom-call | flops 19000000512 | tf_op jit(solution)/shard_map/attend_back_kernel/pallas_call | solution.py:70
  160.2 2.5 add_kernel.3
  165.3 7.3 %weight_kernel.1 = (bf16[384,768]{1,0:T(8,128)(2,1)}, bf16[416,768]{1,0:T(8,128)(2,1)}, bf16[416,768]{1,0:T(8,128)(2,1)}, bf16[416,768]{1,0:T(8,128)(2,1)}, f32[16,768]{1,0:T(8,128)}) custom-call(bf16[384,768]{1,0:T(8,128)(2,1)} %get-tuple-element.126.refs_0_, bf16[768,1024]{1,0:T(8,128)(2,1)} %get-tuple-element.127.refs_1_, ...), custom_call_target="tpu_custom_call" | custom-call | flops 6000000000 | tf_op jit(solution)/shard_map/weight_kernel/pallas_call | solution.py:70
  172.6 2.5 total_kernel.4
  175.2 2.3 collective-permute-start.26
  179.8 6.7 %last_kernel.1 = (bf16[256,768]{1,0:T(8,128)(2,1)}, f32[256,768]{1,0:T(8,128)}, f32[196,768]{1,0:T(8,128)}) custom-call(f32[192,768]{1,0:T(8,128)} %get-tuple-element.135.refs_0_.refs_1_, f32[512,768]{1,0:T(8,128)} %get-tuple-element.136.refs_1_, bf16[544,768]{1,0:T(8,128)(2,1)} %copy-done.10, bf16[512,768]{1,0:T(8,128)(2,1)} %get-tuple-element.100.refs_4_.refs_3_, ...), custom_call_target="tpu_custom_call" | custom-call | flops 6000000000 | tf_op jit(solution)/shard_map/last_kernel/pallas_call | solution.py:70
  186.5 4.3 %collective-permute-done.26.refs_2_ = bf16[192,768]{1,0:T(8,128)(2,1)S(1)} collective-permute-done((bf16[192,768]{1,0:T(8,128)(2,1)}, bf16[192,768]{1,0:T(8,128)(2,1)S(1)}, u32[]{:S(2)}, u32[]{:S(2)}) %collective-permute-start.26) | collective-permute-done | bytes 294944 | tf_op jit(solution)/shard_map/ppermute | solution.py:557
  196.2 2.5 total_kernel.6
  200.2 13.4 %collective-permute-done.29.refs_1_ = bf16[192,768]{1,0:T(8,128)(2,1)S(1)} collective-permute-done((bf16[192,768]{1,0:T(8,128)(2,1)}, bf16[192,768]{1,0:T(8,128)(2,1)S(1)}, u32[]{:S(2)}, u32[]{:S(2)}) %collective-permute-start.29) | collective-permute-done | bytes 294944 | tf_op jit(solution)/shard_map/ppermute | solution.py:557
  214.3 1.9 total_kernel.7
  218.7 2.7 %total_vec_kernel.1 = (f32[16,768]{1,0:T(8,128)}, f32[96,768]{1,0:T(8,128)}, bf16[128,768]{1,0:T(8,128)(2,1)}, bf16[128,768]{1,0:T(8,128)(2,1)}, bf16[128,768]{1,0:T(8,128)(2,1)}) custom-call(f32[96,768]{1,0:T(8,128)} %get-tuple-element.149.refs_0_, f32[16,768]{1,0:T(8,128)} %get-tuple-element.150.refs_1_, ...), custom_call_target="tpu_custom_call" | custom-call | flops 2000000000 | tf_op jit(solution)/shard_map/total_vec_kernel/pallas_call | solution.py:70
  224.2 4.8 %collective-permute-done.33.refs_2_ = bf16[128,768]{1,0:T(8,128)(2,1)S(1)} collective-permute-done((bf16[128,768]{1,0:T(8,128)(2,1)}, bf16[128,768]{1,0:T(8,128)(2,1)S(1)}, u32[]{:S(2)}, u32[]{:S(2)}) %collective-permute-start.33) | collective-permute-done | bytes 196640 | tf_op jit(solution)/shard_map/ppermute | solution.py:557
  229.1 10.8 %collective-permute-done.34.refs_3_ = bf16[128,768]{1,0:T(8,128)(2,1)S(1)} collective-permute-done((bf16[128,768]{1,0:T(8,128)(2,1)}, bf16[128,768]{1,0:T(8,128)(2,1)S(1)}, u32[]{:S(2)}, u32[]{:S(2)}) %collective-permute-start.34) | collective-permute-done | bytes 196640 | tf_op jit(solution)/shard_map/ppermute | solution.py:557
  240.6 2.1 finish_kernel.1
  (186 shorter events, 55.9 us)
Async XLA Ops:
  7.2 100.3 %all-gather.3.cloned.1.call-start = ((), (), s32[]{:S(2)}) async-start(), calls=%async_computation | async-start | bytes 2506752 | tf_op jit(solution)/shard_map/all_gather | solution.py:663
  7.2 15.6 %collective-permute-start = (bf16[256,768]{1,0:T(8,128)(2,1)}, bf16[256,768]{1,0:T(8,128)(2,1)S(1)}, u32[]{:S(2)}, u32[]{:S(2)}) collective-permute-start(bf16[256,768]{1,0:T(8,128)(2,1)} %refs_2_.4), channel_id=1, source_target_pairs={{0,1},{1,0},{2,3},{3,2},{4,5},{5,4},{6,7},{7,6},{8,9},{9,8},{10,11... | collective-permute-start | bytes 1179656 | tf_op jit(solution)/shard_map/ppermute | solution.py:557
  7.8 15.1 %collective-permute-start.2 = (bf16[256,768]{1,0:T(8,128)(2,1)}, bf16[256,768]{1,0:T(8,128)(2,1)S(1)}, u32[]{:S(2)}, u32[]{:S(2)}) collective-permute-start(bf16[256,768]{1,0:T(8,128)(2,1)} %refs_6_.1), channel_id=1, source_target_pairs={{0,1},{1,0},{2,3},{3,2},{4,5},{5,4},{6,7},{7,6},{8,9},{9,8},{10,11... | collective-permute-start | bytes 1179656 | tf_op jit(solution)/shard_map/ppermute | solution.py:557
  7.8 14.0 %collective-permute-start.1 = (bf16[196,768]{1,0:T(8,128)(2,1)}, bf16[196,768]{1,0:T(8,128)(2,1)S(1)}, u32[]{:S(2)}, u32[]{:S(2)}) collective-permute-start(bf16[196,768]{1,0:T(8,128)(2,1)} %refs_4_.1), channel_id=1, source_target_pairs={{0,1},{1,0},{2,3},{3,2},{4,5},{5,4},{6,7},{7,6},{8,9},{9,8},{10,11... | collective-permute-start | bytes 903176 | tf_op jit(solution)/shard_map/ppermute | solution.py:557
  16.2 17.6 %collective-permute-start.6 = (bf16[96,768]{1,0:T(8,128)(2,1)}, bf16[96,768]{1,0:T(8,128)(2,1)S(1)}, u32[]{:S(2)}, u32[]{:S(2)}) collective-permute-start(bf16[96,768]{1,0:T(8,128)(2,1)} %pack_kernel.1.refs_0_.refs_1_), channel_id=1, source_target_pairs={{0,24},{1,25},{2,26},{3,27},{4,28},{5,29},{6,30},{7,31},{8,0},{9,1... | collective-permute-start | bytes 442376 | tf_op jit(solution)/shard_map/ppermute | solution.py:557
  21.8 15.0 %collective-permute-start.5 = (bf16[96,768]{1,0:T(8,128)(2,1)}, bf16[96,768]{1,0:T(8,128)(2,1)S(1)}, u32[]{:S(2)}, u32[]{:S(2)}) collective-permute-start(bf16[96,768]{1,0:T(8,128)(2,1)} %pack_kernel.1.refs_0_.refs_1_), channel_id=1, source_target_pairs={{0,16},{1,17},{2,18},{3,19},{4,20},{5,21},{6,22},{7,23},{8,24},{9,... | collective-permute-start | bytes 442376 | tf_op jit(solution)/shard_map/ppermute | solution.py:557
  21.8 15.0 %collective-permute-start.4 = (bf16[96,768]{1,0:T(8,128)(2,1)}, bf16[96,768]{1,0:T(8,128)(2,1)S(1)}, u32[]{:S(2)}, u32[]{:S(2)}) collective-permute-start(bf16[96,768]{1,0:T(8,128)(2,1)} %pack_kernel.1.refs_0_.refs_1_), channel_id=1, source_target_pairs={{0,8},{1,9},{2,10},{3,11},{4,12},{5,13},{6,14},{7,15},{8,16},{9,17... | collective-permute-start | bytes 442376 | tf_op jit(solution)/shard_map/ppermute | solution.py:557
  39.6 19.7 %collective-permute-start.8 = (bf16[384,768]{1,0:T(8,128)(2,1)}, bf16[384,768]{1,0:T(8,128)(2,1)S(1)}, u32[]{:S(2)}, u32[]{:S(2)}) collective-permute-start(bf16[384,768]{1,0:T(8,128)(2,1)} %get-tuple-element.93.refs_4_), channel_id=1, source_target_pairs={{0,2},{1,3},{2,0},{3,1},{4,6},{5,7},{6,4},{7,5},{8,10},{9,11},{10,... | collective-permute-start | bytes 1769480 | tf_op jit(solution)/shard_map/ppermute | solution.py:557
  39.9 19.4 %collective-permute-start.7 = (bf16[384,768]{1,0:T(8,128)(2,1)}, bf16[384,768]{1,0:T(8,128)(2,1)S(1)}, u32[]{:S(2)}, u32[]{:S(2)}) collective-permute-start(bf16[384,768]{1,0:T(8,128)(2,1)} %get-tuple-element.93.refs_4_), channel_id=1, source_target_pairs={{0,4},{1,5},{2,6},{3,7},{4,0},{5,1},{6,2},{7,3},{8,12},{9,13},{10,... | collective-permute-start | bytes 1769480 | tf_op jit(solution)/shard_map/ppermute | solution.py:557
  41.4 23.5 %collective-permute-start.11 = (bf16[96,768]{1,0:T(8,128)(2,1)}, bf16[96,768]{1,0:T(8,128)(2,1)S(1)}, u32[]{:S(2)}, u32[]{:S(2)}) collective-permute-start(bf16[96,768]{1,0:T(8,128)(2,1)} %get-tuple-element.95.refs_1_), channel_id=1, source_target_pairs={{0,24},{1,25},{2,26},{3,27},{4,28},{5,29},{6,30},{7,31},{8,0},{9,1... | collective-permute-start | bytes 442376 | tf_op jit(solution)/shard_map/ppermute | solution.py:557
  41.6 23.3 %collective-permute-start.10 = (bf16[96,768]{1,0:T(8,128)(2,1)}, bf16[96,768]{1,0:T(8,128)(2,1)S(1)}, u32[]{:S(2)}, u32[]{:S(2)}) collective-permute-start(bf16[96,768]{1,0:T(8,128)(2,1)} %get-tuple-element.95.refs_1_), channel_id=1, source_target_pairs={{0,16},{1,17},{2,18},{3,19},{4,20},{5,21},{6,22},{7,23},{8,24},{9,... | collective-permute-start | bytes 442376 | tf_op jit(solution)/shard_map/ppermute | solution.py:557
  44.2 20.7 %collective-permute-start.9 = (bf16[96,768]{1,0:T(8,128)(2,1)}, bf16[96,768]{1,0:T(8,128)(2,1)S(1)}, u32[]{:S(2)}, u32[]{:S(2)}) collective-permute-start(bf16[96,768]{1,0:T(8,128)(2,1)} %get-tuple-element.95.refs_1_), channel_id=1, source_target_pairs={{0,8},{1,9},{2,10},{3,11},{4,12},{5,13},{6,14},{7,15},{8,16},{9,17... | collective-permute-start | bytes 442376 | tf_op jit(solution)/shard_map/ppermute | solution.py:557
  63.0 13.6 %collective-permute-start.12 = (bf16[192,768]{1,0:T(8,128)(2,1)}, bf16[192,768]{1,0:T(8,128)(2,1)S(1)}, u32[]{:S(2)}, u32[]{:S(2)}) collective-permute-start(bf16[192,768]{1,0:T(8,128)(2,1)} %get-tuple-element.96), channel_id=1, source_target_pairs={{0,2},{1,3},{2,0},{3,1},{4,6},{5,7},{6,4},{7,5},{8,10},{9,11},{10,... | collective-permute-start | bytes 884744 | tf_op jit(solution)/shard_map/ppermute | solution.py:557
  63.4 18.4 %collective-permute-start.13 = (bf16[192,768]{1,0:T(8,128)(2,1)}, bf16[192,768]{1,0:T(8,128)(2,1)S(1)}, u32[]{:S(2)}, u32[]{:S(2)}) collective-permute-start(bf16[192,768]{1,0:T(8,128)(2,1)} %get-tuple-element.94.refs_0_), channel_id=1, source_target_pairs={{0,4},{1,5},{2,6},{3,7},{4,0},{5,1},{6,2},{7,3},{8,12},{9,13},{10,... | collective-permute-start | bytes 884744 | tf_op jit(solution)/shard_map/ppermute | solution.py:557
  68.3 31.6 %collective-permute-start.16 = (bf16[384,768]{1,0:T(8,128)(2,1)}, bf16[384,768]{1,0:T(8,128)(2,1)S(1)}, u32[]{:S(2)}, u32[]{:S(2)}) collective-permute-start(bf16[384,768]{1,0:T(8,128)(2,1)} %stack_kernel.3.refs_0_.refs_6_), channel_id=1, source_target_pairs={{0,6},{1,7},{2,4},{3,5},{4,2},{5,3},{6,0},{7,1},{8,14},{9,15},{10,... | collective-permute-start | bytes 1769480 | tf_op jit(solution)/shard_map/ppermute | solution.py:557
  69.9 35.3 %collective-permute-start.15 = (bf16[384,768]{1,0:T(8,128)(2,1)}, bf16[384,768]{1,0:T(8,128)(2,1)S(1)}, u32[]{:S(2)}, u32[]{:S(2)}) collective-permute-start(bf16[384,768]{1,0:T(8,128)(2,1)} %stack_kernel.3.refs_0_.refs_6_), channel_id=1, source_target_pairs={{0,2},{1,3},{2,0},{3,1},{4,6},{5,7},{6,4},{7,5},{8,10},{9,11},{10,... | collective-permute-start | bytes 1769480 | tf_op jit(solution)/shard_map/ppermute | solution.py:557
  70.2 35.0 %collective-permute-start.14 = (bf16[384,768]{1,0:T(8,128)(2,1)}, bf16[384,768]{1,0:T(8,128)(2,1)S(1)}, u32[]{:S(2)}, u32[]{:S(2)}) collective-permute-start(bf16[384,768]{1,0:T(8,128)(2,1)} %stack_kernel.3.refs_0_.refs_6_), channel_id=1, source_target_pairs={{0,4},{1,5},{2,6},{3,7},{4,0},{5,1},{6,2},{7,3},{8,12},{9,13},{10,... | collective-permute-start | bytes 1769480 | tf_op jit(solution)/shard_map/ppermute | solution.py:557
  117.2 13.9 %collective-permute-start.18 = (bf16[192,768]{1,0:T(8,128)(2,1)}, bf16[192,768]{1,0:T(8,128)(2,1)S(1)}, u32[]{:S(2)}, u32[]{:S(2)}) collective-permute-start(bf16[192,768]{1,0:T(8,128)(2,1)} %get-tuple-element.110), channel_id=1, source_target_pairs={{0,2},{1,3},{2,0},{3,1},{4,6},{5,7},{6,4},{7,5},{8,10},{9,11},{10,... | collective-permute-start | bytes 884744 | tf_op jit(solution)/shard_map/ppermute | solution.py:557
  118.0 13.1 %collective-permute-start.19 = (bf16[192,768]{1,0:T(8,128)(2,1)}, bf16[192,768]{1,0:T(8,128)(2,1)S(1)}, u32[]{:S(2)}, u32[]{:S(2)}) collective-permute-start(bf16[192,768]{1,0:T(8,128)(2,1)} %get-tuple-element.112), channel_id=1, source_target_pairs={{0,4},{1,5},{2,6},{3,7},{4,0},{5,1},{6,2},{7,3},{8,12},{9,13},{10,... | collective-permute-start | bytes 884744 | tf_op jit(solution)/shard_map/ppermute | solution.py:557
  129.5 29.5 %collective-permute-start.23 = (bf16[192,768]{1,0:T(8,128)(2,1)}, bf16[192,768]{1,0:T(8,128)(2,1)S(1)}, u32[]{:S(2)}, u32[]{:S(2)}) collective-permute-start(bf16[192,768]{1,0:T(8,128)(2,1)} %get-tuple-element.123), channel_id=1, source_target_pairs={{0,2},{1,3},{2,0},{3,1},{4,6},{5,7},{6,4},{7,5},{8,10},{9,11},{10,... | collective-permute-start | bytes 884744 | tf_op jit(solution)/shard_map/ppermute | solution.py:557
  130.6 28.4 %collective-permute-start.24 = (bf16[192,768]{1,0:T(8,128)(2,1)}, bf16[192,768]{1,0:T(8,128)(2,1)S(1)}, u32[]{:S(2)}, u32[]{:S(2)}) collective-permute-start(bf16[192,768]{1,0:T(8,128)(2,1)} %get-tuple-element.125), channel_id=1, source_target_pairs={{0,4},{1,5},{2,6},{3,7},{4,0},{5,1},{6,2},{7,3},{8,12},{9,13},{10,... | collective-permute-start | bytes 884744 | tf_op jit(solution)/shard_map/ppermute | solution.py:557
  134.5 24.6 %collective-permute-start.21 = (bf16[384,768]{1,0:T(8,128)(2,1)}, bf16[384,768]{1,0:T(8,128)(2,1)S(1)}, u32[]{:S(2)}, u32[]{:S(2)}) collective-permute-start(bf16[384,768]{1,0:T(8,128)(2,1)} %get-tuple-element.121), channel_id=1, source_target_pairs={{0,4},{1,5},{2,6},{3,7},{4,0},{5,1},{6,2},{7,3},{8,12},{9,13},{10,... | collective-permute-start | bytes 1769480 | tf_op jit(solution)/shard_map/ppermute | solution.py:557
  136.0 23.1 %collective-permute-start.22 = (bf16[384,768]{1,0:T(8,128)(2,1)}, bf16[384,768]{1,0:T(8,128)(2,1)S(1)}, u32[]{:S(2)}, u32[]{:S(2)}) collective-permute-start(bf16[384,768]{1,0:T(8,128)(2,1)} %get-tuple-element.113.refs_0_), channel_id=1, source_target_pairs={{0,2},{1,3},{2,0},{3,1},{4,6},{5,7},{6,4},{7,5},{8,10},{9,11},{10,... | collective-permute-start | bytes 1769480 | tf_op jit(solution)/shard_map/ppermute | solution.py:557
  162.7 30.9 %collective-permute-start.27 = (bf16[384,768]{1,0:T(8,128)(2,1)}, bf16[384,768]{1,0:T(8,128)(2,1)S(1)}, u32[]{:S(2)}, u32[]{:S(2)}) collective-permute-start(bf16[384,768]{1,0:T(8,128)(2,1)} %get-tuple-element.146), channel_id=1, source_target_pairs={{0,4},{1,5},{2,6},{3,7},{4,0},{5,1},{6,2},{7,3},{8,12},{9,13},{10,... | collective-permute-start | bytes 1769480 | tf_op jit(solution)/shard_map/ppermute | solution.py:557
  163.2 32.2 %collective-permute-start.28 = (bf16[384,768]{1,0:T(8,128)(2,1)}, bf16[384,768]{1,0:T(8,128)(2,1)S(1)}, u32[]{:S(2)}, u32[]{:S(2)}) collective-permute-start(bf16[384,768]{1,0:T(8,128)(2,1)} %get-tuple-element.126.refs_0_), channel_id=1, source_target_pairs={{0,2},{1,3},{2,0},{3,1},{4,6},{5,7},{6,4},{7,5},{8,10},{9,11},{10,... | collective-permute-start | bytes 1769480 | tf_op jit(solution)/shard_map/ppermute | solution.py:557
  175.2 15.7 %collective-permute-start.26 = (bf16[192,768]{1,0:T(8,128)(2,1)}, bf16[192,768]{1,0:T(8,128)(2,1)S(1)}, u32[]{:S(2)}, u32[]{:S(2)}) collective-permute-start(bf16[192,768]{1,0:T(8,128)(2,1)} %get-tuple-element.143), channel_id=1, source_target_pairs={{0,16},{1,17},{2,18},{3,19},{4,20},{5,21},{6,22},{7,23},{8,24},{9,... | collective-permute-start | bytes 884744 | tf_op jit(solution)/shard_map/ppermute | solution.py:557
  177.4 40.4 %collective-permute-start.30 = (bf16[416,768]{1,0:T(8,128)(2,1)S(1)}, bf16[416,768]{1,0:T(8,128)(2,1)S(1)}, u32[]{:S(2)}, u32[]{:S(2)}) collective-permute-start(bf16[416,768]{1,0:T(8,128)(2,1)S(1)} %copy-done.14), channel_id=1, source_target_pairs={{0,6},{1,7},{2,4},{3,5},{4,2},{5,3},{6,0},{7,1},{8,14},{9,15},{10,... | collective-permute-start | bytes 1916936 | tf_op jit(solution)/shard_map/ppermute | solution.py:557
  179.4 38.5 %collective-permute-start.31 = (bf16[416,768]{1,0:T(8,128)(2,1)S(1)}, bf16[416,768]{1,0:T(8,128)(2,1)}, u32[]{:S(2)}, u32[]{:S(2)}) collective-permute-start(bf16[416,768]{1,0:T(8,128)(2,1)S(1)} %copy-done.13), channel_id=1, source_target_pairs={{0,4},{1,5},{2,6},{3,7},{4,0},{5,1},{6,2},{7,3},{8,12},{9,13},{10,... | collective-permute-start | bytes 1916936 | tf_op jit(solution)/shard_map/ppermute | solution.py:557
  190.8 27.1 %collective-permute-start.32 = (bf16[416,768]{1,0:T(8,128)(2,1)S(1)}, bf16[416,768]{1,0:T(8,128)(2,1)}, u32[]{:S(2)}, u32[]{:S(2)}) collective-permute-start(bf16[416,768]{1,0:T(8,128)(2,1)S(1)} %copy-done.12), channel_id=1, source_target_pairs={{0,2},{1,3},{2,0},{3,1},{4,6},{5,7},{6,4},{7,5},{8,10},{9,11},{10,... | collective-permute-start | bytes 1916936 | tf_op jit(solution)/shard_map/ppermute | solution.py:557
  198.7 14.8 %collective-permute-start.29 = (bf16[192,768]{1,0:T(8,128)(2,1)}, bf16[192,768]{1,0:T(8,128)(2,1)S(1)}, u32[]{:S(2)}, u32[]{:S(2)}) collective-permute-start(bf16[192,768]{1,0:T(8,128)(2,1)} %get-tuple-element.148), channel_id=1, source_target_pairs={{0,16},{1,17},{2,18},{3,19},{4,20},{5,21},{6,22},{7,23},{8,24},{9,... | collective-permute-start | bytes 884744 | tf_op jit(solution)/shard_map/ppermute | solution.py:557
  221.4 18.4 %collective-permute-start.34 = (bf16[128,768]{1,0:T(8,128)(2,1)}, bf16[128,768]{1,0:T(8,128)(2,1)S(1)}, u32[]{:S(2)}, u32[]{:S(2)}) collective-permute-start(bf16[128,768]{1,0:T(8,128)(2,1)} %get-tuple-element.157), channel_id=1, source_target_pairs={{0,16},{1,17},{2,18},{3,19},{4,20},{5,21},{6,22},{7,23},{8,24},{9,... | collective-permute-start | bytes 589832 | tf_op jit(solution)/shard_map/ppermute | solution.py:557
  223.3 16.6 %collective-permute-start.35 = (bf16[128,768]{1,0:T(8,128)(2,1)}, bf16[128,768]{1,0:T(8,128)(2,1)S(1)}, u32[]{:S(2)}, u32[]{:S(2)}) collective-permute-start(bf16[128,768]{1,0:T(8,128)(2,1)} %get-tuple-element.158), channel_id=1, source_target_pairs={{0,8},{1,9},{2,10},{3,11},{4,12},{5,13},{6,14},{7,15},{8,16},{9,17... | collective-permute-start | bytes 589832 | tf_op jit(solution)/shard_map/ppermute | solution.py:557
  (53 other events, 182.9 us)
Sparse Core Ops, SparseCore 0:
  10.8 96.4 all-gather.2

commit v3 on v2

--- a/solution.py
+++ b/solution.py
@@ -55,7 +55,13 @@
 UNIT = 1e9
 COST = {
     "prep_kernel": 8.0, "attend_kernel": 17.0, "up_kernel": 9.0, "down_kernel": 9.0,
-    "gate_kernel": 12.0, "add_kernel": 30.0, "attend_back_kernel": 19.0, "weight_kernel": 6.0, "last_kernel": 6.0,
+    "gate_kernel": 12.0, "add_kernel": 30.0, "turn_kernel": 30.0, "attend_back_kernel": 19.0, "weight_kernel": 6.0, "last_kernel": 6.0,
+}
+
+
+ROOM = {
+    "prep_kernel": 24, "attend_kernel": 26, "up_kernel": 26, "down_kernel": 26,
+    "attend_back_kernel": 26, "weight_kernel": 20, "last_kernel": 16,
 }
 
 
@@ -75,7 +81,7 @@
         + [place] * (len(args) - smem),
         out_specs=[place] * len(out_shapes),
         scratch_shapes=list(scratch),
-        compiler_params=pltpu.CompilerParams(vmem_limit_bytes=56 * 1024 * 1024),
+        compiler_params=pltpu.CompilerParams(vmem_limit_bytes=ROOM.get(name, 8) * 1024 * 1024),
         cost_estimate=pl.CostEstimate(
             flops=int(COST.get(name, 2.0) * UNIT), bytes_accessed=0, transcendentals=0
         ),
@@ -93,20 +99,23 @@
     a_ref[:, 640:768] = ot[:, 0:128]
 
 
+def bias_kernel(qb, vb, ub, bias_ref):
+    blank = jnp.zeros((1, 128), F32)
+    qf, vf = qb[...].astype(F32), vb[...].astype(F32)
+    row = jnp.concatenate(
+        [qf[:, 0:128], blank, vf[:, 0:128], qf[:, 128:192], vf[:, 128:192], blank, blank], axis=1
+    )
+    rest = jnp.zeros((14, row.shape[1]), F32)
+    bias_ref[...] = jnp.concatenate([row, ub[...].astype(F32), rest], axis=0).astype(BF16)
+
+
 def stack_kernel(count, *refs):
-    extra = (len(refs) - count - 1) // 2
-    pieces, others, out, copies = refs[:count], refs[count : count + extra], refs[count + extra], refs[count + extra + 1 :]
-    rows = pieces[0].shape[0]
-    for k, piece in enumerate(pieces):
-        out[k * rows : (k + 1) * rows, :] = piece[...]
-    for src, dst in zip(others, copies):
-        dst[...] = src[...]
-
-
-def cut_kernel(a, b, out_a, out_b):
-    cut = out_a.shape[0]
-    out_a[...] = a[0:cut, :]
-    out_b[...] = b[cut : 2 * cut, :]
+    pieces, other, out, copy = refs[:count], refs[count], refs[count + 1], refs[count + 2]
+    first = 0
+    for piece in pieces:
+        out[first : first + piece.shape[0], :] = piece[...]
+        first += piece.shape[0]
+    copy[...] = other[...]
 
 
 def gate_kernel(token):
@@ -119,6 +128,11 @@
     out_top[cut:, :] = top[cut:, :]
     out_bottom[0:cut, :] = bottom[0:cut, :]
     out_bottom[cut:, :] = (bottom[cut:, :].astype(F32) + far_bottom[...].astype(F32)).astype(BF16)
+
+
+def turn_kernel(top, far_top, bottom, far_bottom, a, b, c, out_top, out_bottom, near, far):
+    add_kernel(top, far_top, bottom, far_bottom, out_top, out_bottom)
+    total_kernel(3, a, b, c, near, far)
 
 
 def total_kernel(count, *refs):
@@ -181,8 +195,8 @@
 
 
 def prep_kernel(
-    depth, where, tok_o, tok_p, mem_o, mem_p, cot_o, cot_p, vec, patch, bias_o, bias_p,
-    x_ref, xt_ref, tok_r, cot_r, cot_t, mem_r, vec_r, hot_ref, ok_ref, bias_ref, up_ref, unscaled,
+    depth, where, tok_o, tok_p, mem_o, mem_p, cot_o, cot_p, vec, patch,
+    x_ref, xt_ref, tok_r, cot_r, cot_t, mem_r, vec_r, hot_ref, ok_ref, unscaled,
 ):
     features = tok_o.shape[1]
     lane = lax.broadcasted_iota(jnp.int32, (features, features), 1)
@@ -191,13 +205,6 @@
     gain = vec[0:1, :].astype(F32)
     shift = vec[1:2, :].astype(F32)
     vec_r[...] = nt(vec[...], hot_ref[...])
-    for m, bias in enumerate((bias_o, bias_p)):
-        row = bias[...].astype(F32)
-        bias_ref[m] = jnp.zeros_like(bias_ref[m])
-        bias_ref[m, :, 0:128] = row[:, 0:128]
-        bias_ref[m, :, 256:512] = row[:, 128:384]
-        up_ref[m] = row[:, 384:]
-
     rows = lax.broadcasted_iota(jnp.int32, (SLOTS, PATCHES), 0)
     cols = lax.broadcasted_iota(jnp.int32, (SLOTS, PATCHES), 1)
     columns = nt((rows == cols).astype(F32), (patch[...] > 0).astype(F32))
@@ -232,34 +239,22 @@
 
 
 def assemble(quads, w_ref):
-    half = quads[0].shape[0]
+    half = w_ref.shape[1] // 2
     for k, quad in enumerate(quads):
-        w_ref[k // 2, (k % 2) * half : (k % 2 + 1) * half, :] = quad[...]
-
-
-def arrange(depth, where, whole, w_ref):
-    rows = whole.shape[1]
-    half = depth * rows
-    x = where[4] // 2
-    for m in range(2):
-        for ry in range(2):
-            for rz in range(depth):
-                az = lax.rem(where[0] - rz + depth, depth)
-                ay = where[1] if ry == 0 else 1 - where[1]
-                ax = x if m == 0 else 1 - x
-                first = ry * half + rz * rows
-                w_ref[m, first : first + rows, :] = whole[(az * 2 + ay) * 2 + ax]
+        w_ref[k // 2, (k % 2) * half : (k % 2 + 1) * half, :] = quad[0:half, :]
 
 
 def attend_kernel(
     where, split, length,
-    own, own_y, peer, far_top, far_bottom, x_ref, bias, ok_ref,
-    w_ref, y_ref, p_ref, ctx_ref, part_ref, out_ref,
+    own, own_y, peer, far, x_ref, ok_ref,
+    w_ref, y_ref, p_ref, ctx_ref, part_ref, up_ref, out_ref, bias,
 ):
-    assemble((own, own_y, peer), w_ref)
-    half, cut = own.shape[0], far_top.shape[0]
-    w_ref[1, half : half + cut, :] = far_top[...]
-    w_ref[1, half + cut : 2 * half, :] = far_bottom[...]
+    assemble((own, own_y, peer, far), w_ref)
+    half = w_ref.shape[1] // 2
+    for m, src in enumerate((own, peer)):
+        tail = src[half : half + 16, :].astype(F32)
+        bias[m] = tail[0:1, 0:640]
+        up_ref[m] = tail[1:2, :]
     lane = lax.broadcasted_iota(jnp.int32, (TEXT, 128), 1)
     lane_k = lax.broadcasted_iota(jnp.int32, (KEYS, 128), 1)
     zero = jnp.zeros((TEXT, 128), BF16)
@@ -333,11 +328,11 @@
 
 
 def up_kernel(
-    depth, where, part, part_in, tok_r, vec_r, cot_t, bias, whole,
+    part, part_in, tok_r, vec_r, cot_t, bias, w0, w1, w2, w3,
     res_ref, mid_t, hid_ref, slope_ref, g00, g01, g10, g11_top, g11_bottom, mid_ref, u_ref,
 ):
     half = g00.shape[0]
-    arrange(depth, where, whole, u_ref)
+    assemble((w0, w1, w2, w3), u_ref)
     for e in range(2):
         rows = slice(e * TEXT, (e + 1) * TEXT)
         res = (
@@ -363,11 +358,11 @@
 
 
 def down_kernel(
-    depth, where, whole, hid_ref, slope_ref, mid_t, cot_r, w0, w1, w2, w3,
+    v0, v1, v2, v3, hid_ref, slope_ref, mid_t, cot_r, w0, w1, w2, w3,
     out_o, grad_ref, bias_ref, g00, g01, g10, g11_top, g11_bottom, d_ref, pre_ref, u_ref,
 ):
     half = g00.shape[0]
-    arrange(depth, where, whole, u_ref)
+    assemble((v0, v1, v2, v3), u_ref)
     assemble((w0, w1, w2, w3), d_ref)
     bias_ref[...] = jnp.zeros_like(bias_ref)
     for m in range(2):
@@ -556,21 +551,35 @@
     def send(self, a, pairs):
         return lax.ppermute(a, AXES, pairs)
 
-    def line(self, shard, *others, after=()):
+    def line(self, shard, other, tail=None, after=()):
+        more = [] if tail is None else [tail]
         if self.depth == 4:
-            pieces = [shard] + [self.send(shard, self.z(k)) for k in range(1, 4)]
-            rows, lanes = shard.shape
+            pieces = [shard] + [self.send(shard, self.z(k)) for k in range(1, 4)] + more
             return call(
-                functools.partial(stack_kernel, 4),
-                [((4 * rows, lanes), BF16)] + [(o.shape, BF16) for o in others],
-                *pieces, *others, after=after,
+                functools.partial(stack_kernel, len(pieces)),
+                [((sum(p.shape[0] for p in pieces), shard.shape[1]), BF16), (other.shape, other.dtype)],
+                *pieces, other, after=after,
             )
         held = shard[None]
         step = 1
         while step < self.depth:
             held = jnp.concatenate([held, self.send(held, self.z(step))], axis=0)
             step *= 2
-        return (held.reshape(-1, shard.shape[1]),) + others
+        return jnp.concatenate([held.reshape(-1, shard.shape[1])] + more, axis=0), other
+
+    def plane(self, rows):
+        return [rows, self.send(rows, self.y), self.send(rows, self.x), self.send(rows, self.xy)]
+
+    def turn(self, after, g01, g10, far_top, far_bottom, *parts):
+        if self.depth != 4:
+            return self.meet(after, g01, g10, far_top, far_bottom) + self.fold((), *parts)
+        rows, lanes = parts[0].shape
+        to_y, to_x, near, far = call(
+            turn_kernel,
+            [(g01.shape, BF16), (g10.shape, BF16), ((rows // 2, lanes), F32), ((rows // 2, lanes), BF16)],
+            g01, far_top, g10, far_bottom, *parts, after=after,
+        )
+        return self.send(to_y, self.y), self.send(to_x, self.x), to_x, near, self.send(far, self.z(-2))
 
     def home(self, after, *parts):
         rows, lanes = parts[0].shape
@@ -659,78 +668,72 @@
     r = features // dp
     half = features // 2
 
-    sides = [[d * mp + 2 * i + c for d in range(dp) for i in range(mp // 2)] for c in range(2)]
-    up_all = lax.all_gather(up_weight, AXES, axis=0, axis_index_groups=sides)
-
-    biases = jnp.concatenate(
-        [query_bias[:128], value_bias[:128], query_bias[128:], value_bias[128:], up_bias]
-    ).reshape(1, -1)
-    biases_x = links.send(biases, links.x)
     tok_p = links.send(tokens, links.c)
     mem_p = links.send(memory, links.c)
     cot_p = links.send(cotangent, links.c)
     (attn_own,) = call(
         pack_kernel, [((r, features), BF16)], query_weight, key_weight, value_weight, out_weight
     )
+    (biases,) = call(
+        bias_kernel, [((16, features), BF16)],
+        query_bias.reshape(1, -1), value_bias.reshape(1, -1), up_bias.reshape(1, -1),
+        after=(attn_own, tok_p, mem_p, cot_p),
+    )
 
     where = jnp.stack([dp_at // 2, dp_at % 2, mp_at, mp_at ^ 1, mp_at, mp_at ^ 2]).astype(jnp.int32)
     blank = jnp.zeros_like(attn_gain)
     vec = jnp.stack(
         [attn_gain, attn_shift, mlp_gain, mlp_shift, out_bias, down_bias] + [blank] * 10
     )
-    x, xt, tok_r, cot_r, cot_t, mem_r, vec_r, hot, ok, bias, ub, unscaled = call(
+    x, xt, tok_r, cot_r, cot_t, mem_r, vec_r, hot, ok, unscaled = call(
         functools.partial(prep_kernel, dp // 2),
         [
             ((2, KEYS, features), BF16), ((features, 2 * KEYS), BF16),
             ((2 * TEXT, features), BF16), ((2 * TEXT, features), BF16), ((features, 2 * TEXT), BF16),
             ((SLOTS, features), BF16), ((16, features), F32), ((features, features), BF16),
-            ((2, SLOTS, 128), F32), ((2, 1, 640), F32), ((2, 1, hidden), F32),
-            ((2, KEYS, features), BF16),
+            ((2, SLOTS, 128), F32), ((2, KEYS, features), BF16),
         ],
-        where, tokens, tok_p, memory, mem_p, cotangent, cot_p, vec, patch_mask, biases, biases_x,
-        smem=1, after=(attn_own,),
-    )
-    own, down_own = links.line(attn_own, down_weight.T, after=(ok,))
-    own_y, peer = links.send(own, links.y), links.send(own, links.x)
-    cut_y, cut_x = call(cut_kernel, [((half // 2, features), BF16)] * 2, own_y, peer)
-    far_top, far_bottom = links.send(cut_y, links.x), links.send(cut_x, links.y)
-    (down_rows,) = links.line(down_own, after=(cut_x,))
-    quads_d = [
-        down_rows, links.send(down_rows, links.y), links.send(down_rows, links.x), links.send(down_rows, links.xy)
-    ]
-
-    w, y, p, ctx, part = call(
+        where, tokens, tok_p, memory, mem_p, cotangent, cot_p, vec, patch_mask,
+        smem=1, after=(biases,),
+    )
+    rows_a, up_own = links.line(attn_own, up_weight, biases, after=(ok,))
+    quads_a = links.plane(rows_a)
+    rows_u, down_own = links.line(up_own, down_weight.T, after=(rows_a,))
+    quads_u = links.plane(rows_u)
+
+    w, y, p, ctx, part, ub = call(
         attend_kernel,
         [
             ((2, features, features), BF16), ((2, 2, KEYS, 640), BF16), ((2, 2, 3, KEYS, TEXT), BF16),
-            ((2, 2, TEXT, 256), BF16), ((2, TEXT, features), BF16),
+            ((2, 2, TEXT, 256), BF16), ((2, TEXT, features), BF16), ((2, 1, hidden), F32),
         ],
-        where, split_point, text_length, own, own_y, peer, far_top, far_bottom,
-        x, bias, ok,
-        smem=3, scratch=[pltpu.VMEM((2, TEXT, features), F32)], after=(down_rows,),
+        where, split_point, text_length, *quads_a, x, ok,
+        smem=3, scratch=[pltpu.VMEM((2, TEXT, features), F32), pltpu.VMEM((2, 1, 640), F32)], after=(rows_u,),
     )
     part_in = links.send(part, links.c)
-    (token,) = call(gate_kernel, [((8, 128), F32)], after=(part, *quads_d[1:]))
+    (token,) = call(gate_kernel, [((8, 128), F32)], after=(part, *quads_u[1:]))
+    rows_d, _ = links.line(down_own, where, after=(part,))
+    quads_d = links.plane(rows_d)
 
     quarter = ((half, hidden), BF16)
     eighth = ((half // 2, hidden), BF16)
     res, mid_t, hid, slope, d00, d01, d10, d11t, d11b = call(
-        functools.partial(up_kernel, dp // 2),
+        up_kernel,
         [
             ((2 * TEXT, features), F32), ((features, 2 * TEXT), BF16),
             ((2, 2 * TEXT, hidden), BF16), ((2, 2 * TEXT, hidden), BF16),
         ]
         + [quarter] * 3 + [eighth] * 2,
-        where, part, part_in, tok_r, vec_r, cot_t, ub, up_all, smem=1, after=(token,),
+        part, part_in, tok_r, vec_r, cot_t, ub, *quads_u, after=(token, rows_d),
         scratch=[pltpu.VMEM((2 * TEXT, features), BF16), pltpu.VMEM((2, features, hidden), BF16)],
     )
     d_far = links.send(d11t, links.x), links.send(d11b, links.y)
 
     layer_o, mid_grad, up_bias_part, u00, u01, u10, u11t, u11b = call(
-        functools.partial(down_kernel, dp // 2),
+        down_kernel,
         [((TEXT, features), BF16), ((3, TEXT, features), BF16), ((2, hidden), F32)]
         + [quarter] * 3 + [eighth] * 2,
-        where, up_all, hid, slope, mid_t, cot_r, *quads_d, smem=1,
+        *quads_u, hid, slope, mid_t, cot_r, *quads_d,
         scratch=[
             pltpu.VMEM((2, features, hidden), BF16), pltpu.VMEM((2, 2 * TEXT, hidden), BF16),
             pltpu.VMEM((2, features, hidden), BF16),
@@ -752,18 +755,17 @@
         ],
     )
     back_in = links.send(back_p, links.c)
-    u_y, u_x, token = links.meet((dy, d_y, d_x), u01, u10, *u_far)
+    u_y, u_x, token, down_total, down_more = links.turn((dy,), u01, u10, *u_far, d00, d_y, d_x)
     a00, a01, a10, a11, stack = call(
         weight_kernel,
         [((half, features), BF16)] + [((half + 32, features), BF16)] * 3 + [((16, features), F32)],
         xt, ag_t, dy, ctx, sums, back_in, hot, after=(token,),
     )
     a_got = links.direct(a01, a10, a11)
-    down_total, down_more = links.fold((a00,), d00, d_y, d_x)
     layer_out, input_grad, memory_grad = call(
         last_kernel,
         [((TEXT, features), BF16), ((TEXT, features), F32), ((PATCHES, features), F32)],
-        back_o, back_in, tok_r, mem_r, rg, res, layer_o, grad_in, vec_r, hot, after=(down_total,),
+        back_o, back_in, tok_r, mem_r, rg, res, layer_o, grad_in, vec_r, hot, after=(a00,),
     )
     down_parts = links.fold_more((input_grad,), down_total, down_more)
     up_total, up_more = links.fold((down_parts[0],), u00, u_y, u_x)

time: 255 us -> 207 us (0.81)
  Pallas kernels: 108 us -> 59.5 us
  waiting for transfers between devices: 65.4 us -> 84.8 us
  local copies, waits for them, and re-layouts: 25.1 us -> 7.89 us
  between operations: 14.5 us -> 1.09 us
  starting transfers between devices: 39.3 us -> 50.3 us
    pallas_call x20, Pallas kernels: 108 us -> 59.5 us  [call(): pl.pallas_call(body, out_shape=[jax.ShapeDtypeStruct(s, d) for s, d in ou...]
    ppermute x38 -> x42, waiting for transfers between devices: 65.4 us -> 84.8 us  [send(): return lax.ppermute(a, AXES, pairs)]
    ppermute x38 -> x42, starting transfers between devices: 39.3 us -> 50.3 us  [send(): return lax.ppermute(a, AXES, pairs)]
    unnamed x92 -> x52, local copies, waits for them, and re-layouts: 15.5 us -> 6.31 us
  transfers between devices with their start and end apart: 39 -> 42, of which waited for: 10 -> 16; matrix products, arithmetic and copies ran while one was open for 3% -> 1% of each run, Pallas kernels for 38% -> 28%
where the time goes in v3:
time: 207 us; the launch traced here: 206 us
  waiting for transfers between devices  84.8 us (41%)
  Pallas kernels  59.5 us (29%)
  starting transfers between devices  50.3 us (24%)
  local copies, waits for them, and re-layouts  7.89 us (4%)
  other arithmetic  2.47 us (1%)
    ppermute x42, waiting for transfers between devices, send(): return lax.ppermute(a, AXES, pairs)  84.8 us
    pallas_call x20, Pallas kernels, call(): pl.pallas_call(body, out_shape=[jax.ShapeDtypeStruct(s, d) for s, d in ou...  59.5 us
    ppermute x42, starting transfers between devices, send(): return lax.ppermute(a, AXES, pairs)  50.3 us
    unnamed x52, local copies, waits for them, and re-layouts  6.31 us
  transfers between devices with their start and end apart: 42, of which 16 were waited for; matrix products, arithmetic and copies ran while one was open for 1% of the time, Pallas kernels for 28%

profile of v3, /device:TPU:0, one launch (start us, length us, event | category | flops | bytes accessed | tf_op | source)
XLA Modules:
  0.0 206.1 jit_solution(11260682375853138364)
XLA Ops:
  5.2 4.7 %collective-permute-start.5 = (bf16[96,768]{1,0:T(8,128)(2,1)S(1)}, bf16[96,768]{1,0:T(8,128)(2,1)S(1)}, u32[]{:S(2)}, u32[]{:S(2)}) collective-permute-start(bf16[96,768]{1,0:T(8,128)(2,1)S(1)} %pack_kernel.1.refs_0_.refs_1_), channel_id=1, source_target_pairs={{0,24},{1,25},{2,26},{3,27},{4,28},{5,29},{6,30},{7,31},{8,0},{9,1... | collective-permute-start | bytes 442376 | tf_op jit(solution)/shard_map/ppermute | solution.py:552
  11.5 7.4 %prep_kernel.1 = (bf16[2,512,768]{2,1,0:T(8,128)(2,1)S(1)}, bf16[768,1024]{1,0:T(8,128)(2,1)S(1)}, bf16[512,768]{1,0:T(8,128)(2,1)S(1)}, bf16[512,768]{1,0:T(8,1...) custom-call(bf16[16,768]{1,0:T(8,128)(2,1)S(1)} %bias_kernel.1.refs_, ...), custom_call_target="tpu_custom_call" | custom-call | flops 8000000000 | tf_op jit(solution)/shard_map/prep_kernel/pallas_call | solution.py:76
  18.9 4.1 %collective-permute-done.4.refs_3_ = bf16[96,768]{1,0:T(8,128)(2,1)S(1)} collective-permute-done((bf16[96,768]{1,0:T(8,128)(2,1)S(1)}, bf16[96,768]{1,0:T(8,128)(2,1)S(1)}, u32[]{:S(2)}, u32[]{:S(2)}) %collective-permute-start.4) | collective-permute-done | bytes 147488 | tf_op jit(solution)/shard_map/ppermute | solution.py:552
  24.4 2.4 %collective-permute-start.14 = (bf16[400,768]{1,0:T(8,128)(2,1)S(1)}, bf16[400,768]{1,0:T(8,128)(2,1)S(1)}, u32[]{:S(2)}, u32[]{:S(2)}) collective-permute-start(bf16[400,768]{1,0:T(8,128)(2,1)S(1)} %get-tuple-element.93.refs_0_.refs_4_), channel_id=1, source_target_pairs={{0,6},{1,7},{2,4},{3,5},{4,2},{5,3},{6,0},{7,1},{8,14},{9,15},{10,... | collective-permute-start | bytes 1843208 | tf_op jit(solution)/shard_map/ppermute | solution.py:552
  27.9 1.6 collective-permute-start.7
  29.5 1.9 collective-permute-start.6
  31.4 7.3 %collective-permute-done.7.refs_3_ = bf16[96,768]{1,0:T(8,128)(2,1)S(1)} collective-permute-done((bf16[96,768]{1,0:T(8,128)(2,1)S(1)}, bf16[96,768]{1,0:T(8,128)(2,1)S(1)}, u32[]{:S(2)}, u32[]{:S(2)}) %collective-permute-start.7) | collective-permute-done | bytes 147488 | tf_op jit(solution)/shard_map/ppermute | solution.py:552
  41.1 3.7 %collective-permute-done.17.refs_4_ = bf16[96,768]{1,0:T(8,128)(2,1)S(1)} collective-permute-done((bf16[96,768]{1,0:T(8,128)(2,1)S(1)}, bf16[96,768]{1,0:T(8,128)(2,1)S(1)}, u32[]{:S(2)}, u32[]{:S(2)}) %collective-permute-start.17) | collective-permute-done | bytes 147488 | tf_op jit(solution)/shard_map/ppermute | solution.py:552
  44.9 6.3 %collective-permute-start.15 = (bf16[96,768]{1,0:T(8,128)(2,1)S(1)}, bf16[96,768]{1,0:T(8,128)(2,1)S(1)}, u32[]{:S(2)}, u32[]{:S(2)}) collective-permute-start(bf16[96,768]{1,0:T(8,128)(2,1)S(1)} %get-tuple-element.98.refs_1_), channel_id=1, source_target_pairs={{0,8},{1,9},{2,10},{3,11},{4,12},{5,13},{6,14},{7,15},{8,16},{9,17... | collective-permute-start | bytes 442376 | tf_op jit(solution)/shard_map/ppermute | solution.py:552
  51.1 2.4 %collective-permute-start.11 = (bf16[384,768]{1,0:T(8,128)(2,1)S(1)}, bf16[384,768]{1,0:T(8,128)(2,1)S(1)}, u32[]{:S(2)}, u32[]{:S(2)}) collective-permute-start(bf16[384,768]{1,0:T(8,128)(2,1)S(1)} %get-tuple-element.95.refs_0_.refs_8_), channel_id=1, source_target_pairs={{0,6},{1,7},{2,4},{3,5},{4,2},{5,3},{6,0},{7,1},{8,14},{9,15},{10,... | collective-permute-start | bytes 1769480 | tf_op jit(solution)/shard_map/ppermute | solution.py:552
  53.6 1.7 collective-permute-done.13.refs_6_
  57.4 13.5 %attend_kernel.1 = (bf16[2,768,768]{2,1,0:T(8,128)(2,1)S(1)}, bf16[2,2,512,640]{3,2,1,0:T(8,128)(2,1)S(1)}, bf16[2,2,3,512,256]{4,3,2,1,0:T(8,128)(2,1)S(1)}, bf...) custom-call(bf16[384,768]{1,0:T(8,128)(2,1)S(1)} %get-tuple-element.95.refs_0_.refs_8_, ...), custom_call_target="tpu_custom_call" | custom-call | flops 16999999488 | tf_op jit(solution)/shard_map/attend_kernel/pallas_call | solution.py:76
  74.9 6.1 %collective-permute-done.10.refs_2_.refs_10_ = bf16[384,768]{1,0:T(8,128)(2,1)S(1)} collective-permute-done((bf16[384,768]{1,0:T(8,128)(2,1)S(1)}, bf16[384,768]{1,0:T(8,128)(2,1)S(1)}, u32[]{:S(2)}, u32[]{:S(2)}) %collective-permute-start.10) | collective-permute-done | bytes 589856 | tf_op jit(solution)/shard_map/ppermute | solution.py:552
  81.1 2.3 %collective-permute-done.18.refs_3_ = bf16[2,256,768]{2,1,0:T(8,128)(2,1)S(1)} collective-permute-done((bf16[2,256,768]{2,1,0:T(8,128)(2,1)S(1)}, bf16[2,256,768]{2,1,0:T(8,128)(2,1)S(1)}, u32[]{:S(2)}, u32[]{:S(2)}) %collective-permute-start.18) | collective-permute-done | bytes 786464 | tf_op jit(solution)/shard_map/ppermute | solution.py:552
  83.3 5.0 %up_kernel.1 = (f32[512,768]{1,0:T(8,128)S(1)}, bf16[768,512]{1,0:T(8,128)(2,1)S(1)}, bf16[2,512,768]{2,1,0:T(8,128)(2,1)S(1)}, bf16[2,512,768]{2,1,0:T(8,128)(2...) custom-call(f32[8,128]{1,0:T(8,128)S(1)} %gate_kernel.1.refs_0_, ...), custom_call_target="tpu_custom_call" | custom-call | flops 8999999488 | tf_op jit(solution)/shard_map/up_kernel/pallas_call | solution.py:76
  88.4 1.6 collective-permute-start.22
  90.5 3.2 %collective-permute-done.21.refs_11_ = bf16[384,768]{1,0:T(8,128)(2,1)S(1)} collective-permute-done((bf16[384,768]{1,0:T(8,128)(2,1)S(1)}, bf16[384,768]{1,0:T(8,128)(2,1)S(1)}, u32[]{:S(2)}, u32[]{:S(2)}) %collective-permute-start.21) | collective-permute-done | bytes 589856 | tf_op jit(solution)/shard_map/ppermute | solution.py:552
  93.7 12.7 %collective-permute-done.20.refs_10_ = bf16[384,768]{1,0:T(8,128)(2,1)S(1)} collective-permute-done((bf16[384,768]{1,0:T(8,128)(2,1)S(1)}, bf16[384,768]{1,0:T(8,128)(2,1)S(1)}, u32[]{:S(2)}, u32[]{:S(2)}) %collective-permute-start.20) | collective-permute-done | bytes 589856 | tf_op jit(solution)/shard_map/ppermute | solution.py:552
  106.4 5.1 %down_kernel.1 = (bf16[256,768]{1,0:T(8,128)(2,1)S(1)}, bf16[3,256,768]{2,1,0:T(8,128)(2,1)S(1)}, f32[2,768]{1,0:T(2,128)S(1)}, bf16[384,768]{1,0:T(8,128)(2,1)S...) custom-call(bf16[384,768]{1,0:T(8,128)(2,1)S(1)} %get-tuple-element., ...), custom_call_target="tpu_custom_call" | custom-call | flops 8999999488 | tf_op jit(solution)/shard_map/down_kernel/pallas_call | solution.py:76
  111.5 1.6 collective-permute-start.25
  113.8 1.6 collective-permute-start.27
  116.4 15.2 %attend_back_kernel.1 = (f32[256,768]{1,0:T(8,128)S(1)}, bf16[768,512]{1,0:T(8,128)(2,1)S(1)}, bf16[2,2,512,640]{3,2,1,0:T(8,128)(2,1)S(1)}, f32[512,768]{1,0:T(...) custom-call(bf16[384,768]{1,0:T(8,128)(2,1)S(1)} %get-tuple-element.113.refs_0_, ...), custom_call_target="tpu_custom_call" | custom-call | flops 19000000512 | tf_op jit(solution)/shard_map/attend_back_kernel/pallas_call | solution.py:76
  134.2 1.5 collective-permute-start.31
  136.2 3.4 %weight_kernel.1 = (bf16[384,768]{1,0:T(8,128)(2,1)S(1)}, bf16[416,768]{1,0:T(8,128)(2,1)S(1)}, bf16[416,768]{1,0:T(8,128)(2,1)S(1)}, bf16[416,768]{1,0:T(8,128)(2,1)S(1)}, f32[16,768]{1,0:T(8,128)S(1)}) custom-call(bf16[384,768]{1,0:T(8,128)(2,1)S(1)} %get-tuple-element.127.refs_0_, bf16[768,1024]{1,0:T(8,128)(2,1)S(1)} %get-tuple-element.128.refs_1_, ...), custom_call_target="tpu_custom_call" | custom-call | flops 6000000000 | tf_op jit(solution)/shard_map/weight_kernel/pallas_call | solution.py:76
  139.6 3.4 %last_kernel.1 = (bf16[256,768]{1,0:T(8,128)(2,1)}, f32[256,768]{1,0:T(8,128)}, f32[196,768]{1,0:T(8,128)}) custom-call(bf16[384,768]{1,0:T(8,128)(2,1)S(1)} %get-tuple-element.134.refs_0_.refs_2_, f32[512,768]{1,0:T(8,128)S(1)} %get-tuple-element.135.refs_1_, bf16[544,768]{1,0:T(8,128)(2,1)S(1)} %collective-permute-done.29.refs_6_.refs_2_, ...), custom_call_target="tpu_custom_call" | custom-call | flops 6000000000 | tf_op jit(solution)/shard_map/last_kernel/pallas_call | solution.py:76
  143.0 5.7 %collective-permute-done.30.refs_2_ = bf16[192,768]{1,0:T(8,128)(2,1)S(1)} collective-permute-done((bf16[192,768]{1,0:T(8,128)(2,1)S(1)}, bf16[192,768]{1,0:T(8,128)(2,1)S(1)}, u32[]{:S(2)}, u32[]{:S(2)}) %collective-permute-start.30) | collective-permute-done | bytes 294944 | tf_op jit(solution)/shard_map/ppermute | solution.py:552
  150.6 2.2 %collective-permute-start.41 = (bf16[96,768]{1,0:T(8,128)(2,1)}, bf16[96,768]{1,0:T(8,128)(2,1)}, u32[]{:S(2)}, u32[]{:S(2)}) collective-permute-start(bf16[96,768]{1,0:T(8,128)(2,1)} %get-tuple-element.164), channel_id=1, source_target_pairs={{0,24},{1,25},{2,26},{3,27},{4,28},{5,29},{6,30},{7,31},{8,0},{9,1... | collective-permute-start | bytes 442376 | tf_op jit(solution)/shard_map/ppermute | solution.py:552
  158.0 1.6 add_bitcast_fusion
  159.6 13.0 %collective-permute-done.33.refs_1_ = bf16[192,768]{1,0:T(8,128)(2,1)} collective-permute-done((bf16[192,768]{1,0:T(8,128)(2,1)}, bf16[192,768]{1,0:T(8,128)(2,1)}, u32[]{:S(2)}, u32[]{:S(2)}) %collective-permute-start.33) | collective-permute-done | bytes 294944 | tf_op jit(solution)/shard_map/ppermute | solution.py:552
  175.8 7.6 %collective-permute-done.35.refs_4_ = bf16[416,768]{1,0:T(8,128)(2,1)S(1)} collective-permute-done((bf16[416,768]{1,0:T(8,128)(2,1)S(1)}, bf16[416,768]{1,0:T(8,128)(2,1)S(1)}, u32[]{:S(2)}, u32[]{:S(2)}) %collective-permute-start.35) | collective-permute-done | bytes 639008 | tf_op jit(solution)/shard_map/ppermute | solution.py:552
  187.8 4.2 %collective-permute-done.37.refs_2_ = bf16[128,768]{1,0:T(8,128)(2,1)S(1)} collective-permute-done((bf16[128,768]{1,0:T(8,128)(2,1)S(1)}, bf16[128,768]{1,0:T(8,128)(2,1)S(1)}, u32[]{:S(2)}, u32[]{:S(2)}) %collective-permute-start.37) | collective-permute-done | bytes 196640 | tf_op jit(solution)/shard_map/ppermute | solution.py:552
  192.0 11.7 %collective-permute-done.38.refs_3_ = bf16[128,768]{1,0:T(8,128)(2,1)S(1)} collective-permute-done((bf16[128,768]{1,0:T(8,128)(2,1)S(1)}, bf16[128,768]{1,0:T(8,128)(2,1)S(1)}, u32[]{:S(2)}, u32[]{:S(2)}) %collective-permute-start.38) | collective-permute-done | bytes 196640 | tf_op jit(solution)/shard_map/ppermute | solution.py:552
  (150 shorter events, 39.2 us)
Async XLA Ops:
  0.7 10.7 %collective-permute-start = (bf16[256,768]{1,0:T(8,128)(2,1)}, bf16[256,768]{1,0:T(8,128)(2,1)S(1)}, u32[]{:S(2)}, u32[]{:S(2)}) collective-permute-start(bf16[256,768]{1,0:T(8,128)(2,1)} %refs_2_.4), channel_id=1, source_target_pairs={{0,1},{1,0},{2,3},{3,2},{4,5},{5,4},{6,7},{7,6},{8,9},{9,8},{10,11... | collective-permute-start | bytes 1179656 | tf_op jit(solution)/shard_map/ppermute | solution.py:552
  5.2 13.7 %collective-permute-start.5 = (bf16[96,768]{1,0:T(8,128)(2,1)S(1)}, bf16[96,768]{1,0:T(8,128)(2,1)S(1)}, u32[]{:S(2)}, u32[]{:S(2)}) collective-permute-start(bf16[96,768]{1,0:T(8,128)(2,1)S(1)} %pack_kernel.1.refs_0_.refs_1_), channel_id=1, source_target_pairs={{0,24},{1,25},{2,26},{3,27},{4,28},{5,29},{6,30},{7,31},{8,0},{9,1... | collective-permute-start | bytes 442376 | tf_op jit(solution)/shard_map/ppermute | solution.py:552
  9.9 13.1 %collective-permute-start.4 = (bf16[96,768]{1,0:T(8,128)(2,1)S(1)}, bf16[96,768]{1,0:T(8,128)(2,1)S(1)}, u32[]{:S(2)}, u32[]{:S(2)}) collective-permute-start(bf16[96,768]{1,0:T(8,128)(2,1)S(1)} %pack_kernel.1.refs_0_.refs_1_), channel_id=1, source_target_pairs={{0,16},{1,17},{2,18},{3,19},{4,20},{5,21},{6,22},{7,23},{8,24},{9,... | collective-permute-start | bytes 442376 | tf_op jit(solution)/shard_map/ppermute | solution.py:552
  10.3 12.7 %collective-permute-start.3 = (bf16[96,768]{1,0:T(8,128)(2,1)S(1)}, bf16[96,768]{1,0:T(8,128)(2,1)S(1)}, u32[]{:S(2)}, u32[]{:S(2)}) collective-permute-start(bf16[96,768]{1,0:T(8,128)(2,1)S(1)} %pack_kernel.1.refs_0_.refs_1_), channel_id=1, source_target_pairs={{0,8},{1,9},{2,10},{3,11},{4,12},{5,13},{6,14},{7,15},{8,16},{9,17... | collective-permute-start | bytes 442376 | tf_op jit(solution)/shard_map/ppermute | solution.py:552
  24.4 26.7 %collective-permute-start.14 = (bf16[400,768]{1,0:T(8,128)(2,1)S(1)}, bf16[400,768]{1,0:T(8,128)(2,1)S(1)}, u32[]{:S(2)}, u32[]{:S(2)}) collective-permute-start(bf16[400,768]{1,0:T(8,128)(2,1)S(1)} %get-tuple-element.93.refs_0_.refs_4_), channel_id=1, source_target_pairs={{0,6},{1,7},{2,4},{3,5},{4,2},{5,3},{6,0},{7,1},{8,14},{9,15},{10,... | collective-permute-start | bytes 1843208 | tf_op jit(solution)/shard_map/ppermute | solution.py:552
  26.9 28.5 %collective-permute-start.13 = (bf16[400,768]{1,0:T(8,128)(2,1)S(1)}, bf16[400,768]{1,0:T(8,128)(2,1)S(1)}, u32[]{:S(2)}, u32[]{:S(2)}) collective-permute-start(bf16[400,768]{1,0:T(8,128)(2,1)S(1)} %get-tuple-element.93.refs_0_.refs_4_), channel_id=1, source_target_pairs={{0,2},{1,3},{2,0},{3,1},{4,6},{5,7},{6,4},{7,5},{8,10},{9,11},{10,... | collective-permute-start | bytes 1843208 | tf_op jit(solution)/shard_map/ppermute | solution.py:552
  27.4 29.4 %collective-permute-start.12 = (bf16[400,768]{1,0:T(8,128)(2,1)S(1)}, bf16[400,768]{1,0:T(8,128)(2,1)S(1)}, u32[]{:S(2)}, u32[]{:S(2)}) collective-permute-start(bf16[400,768]{1,0:T(8,128)(2,1)S(1)} %get-tuple-element.93.refs_0_.refs_4_), channel_id=1, source_target_pairs={{0,4},{1,5},{2,6},{3,7},{4,0},{5,1},{6,2},{7,3},{8,12},{9,13},{10,... | collective-permute-start | bytes 1843208 | tf_op jit(solution)/shard_map/ppermute | solution.py:552
  27.9 10.8 %collective-permute-start.7 = (bf16[96,768]{1,0:T(8,128)(2,1)S(1)}, bf16[96,768]{1,0:T(8,128)(2,1)S(1)}, u32[]{:S(2)}, u32[]{:S(2)}) collective-permute-start(bf16[96,768]{1,0:T(8,128)(2,1)S(1)} %get-tuple-element.94.refs_1_), channel_id=1, source_target_pairs={{0,16},{1,17},{2,18},{3,19},{4,20},{5,21},{6,22},{7,23},{8,24},{9,... | collective-permute-start | bytes 442376 | tf_op jit(solution)/shard_map/ppermute | solution.py:552
  40.0 30.8 %collective-permute-start.16 = (bf16[96,768]{1,0:T(8,128)(2,1)S(1)}, bf16[96,768]{1,0:T(8,128)(2,1)S(1)}, u32[]{:S(2)}, u32[]{:S(2)}) collective-permute-start(bf16[96,768]{1,0:T(8,128)(2,1)S(1)} %get-tuple-element.98.refs_1_), channel_id=1, source_target_pairs={{0,16},{1,17},{2,18},{3,19},{4,20},{5,21},{6,22},{7,23},{8,24},{9,... | collective-permute-start | bytes 442376 | tf_op jit(solution)/shard_map/ppermute | solution.py:552
  44.9 26.0 %collective-permute-start.15 = (bf16[96,768]{1,0:T(8,128)(2,1)S(1)}, bf16[96,768]{1,0:T(8,128)(2,1)S(1)}, u32[]{:S(2)}, u32[]{:S(2)}) collective-permute-start(bf16[96,768]{1,0:T(8,128)(2,1)S(1)} %get-tuple-element.98.refs_1_), channel_id=1, source_target_pairs={{0,8},{1,9},{2,10},{3,11},{4,12},{5,13},{6,14},{7,15},{8,16},{9,17... | collective-permute-start | bytes 442376 | tf_op jit(solution)/shard_map/ppermute | solution.py:552
  51.1 23.2 %collective-permute-start.11 = (bf16[384,768]{1,0:T(8,128)(2,1)S(1)}, bf16[384,768]{1,0:T(8,128)(2,1)S(1)}, u32[]{:S(2)}, u32[]{:S(2)}) collective-permute-start(bf16[384,768]{1,0:T(8,128)(2,1)S(1)} %get-tuple-element.95.refs_0_.refs_8_), channel_id=1, source_target_pairs={{0,6},{1,7},{2,4},{3,5},{4,2},{5,3},{6,0},{7,1},{8,14},{9,15},{10,... | collective-permute-start | bytes 1769480 | tf_op jit(solution)/shard_map/ppermute | solution.py:552
  55.3 25.7 %collective-permute-start.10 = (bf16[384,768]{1,0:T(8,128)(2,1)S(1)}, bf16[384,768]{1,0:T(8,128)(2,1)S(1)}, u32[]{:S(2)}, u32[]{:S(2)}) collective-permute-start(bf16[384,768]{1,0:T(8,128)(2,1)S(1)} %get-tuple-element.95.refs_0_.refs_8_), channel_id=1, source_target_pairs={{0,2},{1,3},{2,0},{3,1},{4,6},{5,7},{6,4},{7,5},{8,10},{9,11},{10,... | collective-permute-start | bytes 1769480 | tf_op jit(solution)/shard_map/ppermute | solution.py:552
  56.8 24.2 %collective-permute-start.9 = (bf16[384,768]{1,0:T(8,128)(2,1)S(1)}, bf16[384,768]{1,0:T(8,128)(2,1)S(1)}, u32[]{:S(2)}, u32[]{:S(2)}) collective-permute-start(bf16[384,768]{1,0:T(8,128)(2,1)S(1)} %get-tuple-element.95.refs_0_.refs_8_), channel_id=1, source_target_pairs={{0,4},{1,5},{2,6},{3,7},{4,0},{5,1},{6,2},{7,3},{8,12},{9,13},{10,... | collective-permute-start | bytes 1769480 | tf_op jit(solution)/shard_map/ppermute | solution.py:552
  71.4 22.2 %collective-permute-start.21 = (bf16[384,768]{1,0:T(8,128)(2,1)S(1)}, bf16[384,768]{1,0:T(8,128)(2,1)S(1)}, u32[]{:S(2)}, u32[]{:S(2)}) collective-permute-start(bf16[384,768]{1,0:T(8,128)(2,1)S(1)} %get-tuple-element.99.refs_1_.refs_8_), channel_id=1, source_target_pairs={{0,6},{1,7},{2,4},{3,5},{4,2},{5,3},{6,0},{7,1},{8,14},{9,15},{10,... | collective-permute-start | bytes 1769480 | tf_op jit(solution)/shard_map/ppermute | solution.py:552
  72.9 33.5 %collective-permute-start.20 = (bf16[384,768]{1,0:T(8,128)(2,1)S(1)}, bf16[384,768]{1,0:T(8,128)(2,1)S(1)}, u32[]{:S(2)}, u32[]{:S(2)}) collective-permute-start(bf16[384,768]{1,0:T(8,128)(2,1)S(1)} %get-tuple-element.99.refs_1_.refs_8_), channel_id=1, source_target_pairs={{0,2},{1,3},{2,0},{3,1},{4,6},{5,7},{6,4},{7,5},{8,10},{9,11},{10,... | collective-permute-start | bytes 1769480 | tf_op jit(solution)/shard_map/ppermute | solution.py:552
  74.4 32.0 %collective-permute-start.19 = (bf16[384,768]{1,0:T(8,128)(2,1)S(1)}, bf16[384,768]{1,0:T(8,128)(2,1)S(1)}, u32[]{:S(2)}, u32[]{:S(2)}) collective-permute-start(bf16[384,768]{1,0:T(8,128)(2,1)S(1)} %get-tuple-element.99.refs_1_.refs_8_), channel_id=1, source_target_pairs={{0,4},{1,5},{2,6},{3,7},{4,0},{5,1},{6,2},{7,3},{8,12},{9,13},{10,... | collective-permute-start | bytes 1769480 | tf_op jit(solution)/shard_map/ppermute | solution.py:552
  88.4 25.2 %collective-permute-start.22 = (bf16[192,768]{1,0:T(8,128)(2,1)S(1)}, bf16[192,768]{1,0:T(8,128)(2,1)S(1)}, u32[]{:S(2)}, u32[]{:S(2)}) collective-permute-start(bf16[192,768]{1,0:T(8,128)(2,1)S(1)} %get-tuple-element.110), channel_id=1, source_target_pairs={{0,2},{1,3},{2,0},{3,1},{4,6},{5,7},{6,4},{7,5},{8,10},{9,11},{10,... | collective-permute-start | bytes 884744 | tf_op jit(solution)/shard_map/ppermute | solution.py:552
  89.9 23.7 %collective-permute-start.23 = (bf16[192,768]{1,0:T(8,128)(2,1)S(1)}, bf16[192,768]{1,0:T(8,128)(2,1)S(1)}, u32[]{:S(2)}, u32[]{:S(2)}) collective-permute-start(bf16[192,768]{1,0:T(8,128)(2,1)S(1)} %get-tuple-element.112), channel_id=1, source_target_pairs={{0,4},{1,5},{2,6},{3,7},{4,0},{5,1},{6,2},{7,3},{8,12},{9,13},{10,... | collective-permute-start | bytes 884744 | tf_op jit(solution)/shard_map/ppermute | solution.py:552
  111.5 20.3 %collective-permute-start.25 = (bf16[192,768]{1,0:T(8,128)(2,1)S(1)}, bf16[192,768]{1,0:T(8,128)(2,1)S(1)}, u32[]{:S(2)}, u32[]{:S(2)}) collective-permute-start(bf16[192,768]{1,0:T(8,128)(2,1)S(1)} %get-tuple-element.122), channel_id=1, source_target_pairs={{0,2},{1,3},{2,0},{3,1},{4,6},{5,7},{6,4},{7,5},{8,10},{9,11},{10,... | collective-permute-start | bytes 884744 | tf_op jit(solution)/shard_map/ppermute | solution.py:552
  113.1 18.8 %collective-permute-start.26 = (bf16[192,768]{1,0:T(8,128)(2,1)S(1)}, bf16[192,768]{1,0:T(8,128)(2,1)S(1)}, u32[]{:S(2)}, u32[]{:S(2)}) collective-permute-start(bf16[192,768]{1,0:T(8,128)(2,1)S(1)} %get-tuple-element.124), channel_id=1, source_target_pairs={{0,4},{1,5},{2,6},{3,7},{4,0},{5,1},{6,2},{7,3},{8,12},{9,13},{10,... | collective-permute-start | bytes 884744 | tf_op jit(solution)/shard_map/ppermute | solution.py:552
  113.8 18.7 %collective-permute-start.27 = (bf16[384,768]{1,0:T(8,128)(2,1)S(1)}, bf16[384,768]{1,0:T(8,128)(2,1)S(1)}, u32[]{:S(2)}, u32[]{:S(2)}) collective-permute-start(bf16[384,768]{1,0:T(8,128)(2,1)S(1)} %get-tuple-element.126), channel_id=1, source_target_pairs={{0,4},{1,5},{2,6},{3,7},{4,0},{5,1},{6,2},{7,3},{8,12},{9,13},{10,... | collective-permute-start | bytes 1769480 | tf_op jit(solution)/shard_map/ppermute | solution.py:552
  115.4 17.1 %collective-permute-start.28 = (bf16[384,768]{1,0:T(8,128)(2,1)S(1)}, bf16[384,768]{1,0:T(8,128)(2,1)S(1)}, u32[]{:S(2)}, u32[]{:S(2)}) collective-permute-start(bf16[384,768]{1,0:T(8,128)(2,1)S(1)} %get-tuple-element.113.refs_0_), channel_id=1, source_target_pairs={{0,2},{1,3},{2,0},{3,1},{4,6},{5,7},{6,4},{7,5},{8,10},{9,11},{10,... | collective-permute-start | bytes 1769480 | tf_op jit(solution)/shard_map/ppermute | solution.py:552
  132.8 16.0 %collective-permute-start.30 = (bf16[192,768]{1,0:T(8,128)(2,1)S(1)}, bf16[192,768]{1,0:T(8,128)(2,1)S(1)}, u32[]{:S(2)}, u32[]{:S(2)}) collective-permute-start(bf16[192,768]{1,0:T(8,128)(2,1)S(1)} %get-tuple-element.143), channel_id=1, source_target_pairs={{0,16},{1,17},{2,18},{3,19},{4,20},{5,21},{6,22},{7,23},{8,24},{9,... | collective-permute-start | bytes 884744 | tf_op jit(solution)/shard_map/ppermute | solution.py:552
  134.2 21.0 %collective-permute-start.31 = (bf16[384,768]{1,0:T(8,128)(2,1)S(1)}, bf16[384,768]{1,0:T(8,128)(2,1)S(1)}, u32[]{:S(2)}, u32[]{:S(2)}) collective-permute-start(bf16[384,768]{1,0:T(8,128)(2,1)S(1)} %get-tuple-element.146), channel_id=1, source_target_pairs={{0,4},{1,5},{2,6},{3,7},{4,0},{5,1},{6,2},{7,3},{8,12},{9,13},{10,... | collective-permute-start | bytes 1769480 | tf_op jit(solution)/shard_map/ppermute | solution.py:552
  135.7 20.6 %collective-permute-start.32 = (bf16[384,768]{1,0:T(8,128)(2,1)S(1)}, bf16[384,768]{1,0:T(8,128)(2,1)S(1)}, u32[]{:S(2)}, u32[]{:S(2)}) collective-permute-start(bf16[384,768]{1,0:T(8,128)(2,1)S(1)} %get-tuple-element.127.refs_0_), channel_id=1, source_target_pairs={{0,2},{1,3},{2,0},{3,1},{4,6},{5,7},{6,4},{7,5},{8,10},{9,11},{10,... | collective-permute-start | bytes 1769480 | tf_op jit(solution)/shard_map/ppermute | solution.py:552
  152.8 23.0 %collective-permute-start.34 = (bf16[416,768]{1,0:T(8,128)(2,1)S(1)}, bf16[416,768]{1,0:T(8,128)(2,1)S(1)}, u32[]{:S(2)}, u32[]{:S(2)}) collective-permute-start(bf16[416,768]{1,0:T(8,128)(2,1)S(1)} %get-tuple-element.151), channel_id=1, source_target_pairs={{0,6},{1,7},{2,4},{3,5},{4,2},{5,3},{6,0},{7,1},{8,14},{9,15},{10,... | collective-permute-start | bytes 1916936 | tf_op jit(solution)/shard_map/ppermute | solution.py:552
  154.2 29.1 %collective-permute-start.35 = (bf16[416,768]{1,0:T(8,128)(2,1)S(1)}, bf16[416,768]{1,0:T(8,128)(2,1)S(1)}, u32[]{:S(2)}, u32[]{:S(2)}) collective-permute-start(bf16[416,768]{1,0:T(8,128)(2,1)S(1)} %get-tuple-element.152), channel_id=1, source_target_pairs={{0,4},{1,5},{2,6},{3,7},{4,0},{5,1},{6,2},{7,3},{8,12},{9,13},{10,... | collective-permute-start | bytes 1916936 | tf_op jit(solution)/shard_map/ppermute | solution.py:552
  155.2 28.4 %collective-permute-start.36 = (bf16[416,768]{1,0:T(8,128)(2,1)S(1)}, bf16[416,768]{1,0:T(8,128)(2,1)}, u32[]{:S(2)}, u32[]{:S(2)}) collective-permute-start(bf16[416,768]{1,0:T(8,128)(2,1)S(1)} %get-tuple-element.153), channel_id=1, source_target_pairs={{0,2},{1,3},{2,0},{3,1},{4,6},{5,7},{6,4},{7,5},{8,10},{9,11},{10,... | collective-permute-start | bytes 1916936 | tf_op jit(solution)/shard_map/ppermute | solution.py:552
  158.0 14.7 %collective-permute-start.33 = (bf16[192,768]{1,0:T(8,128)(2,1)}, bf16[192,768]{1,0:T(8,128)(2,1)}, u32[]{:S(2)}, u32[]{:S(2)}) collective-permute-start(bf16[192,768]{1,0:T(8,128)(2,1)} %get-tuple-element.148), channel_id=1, source_target_pairs={{0,16},{1,17},{2,18},{3,19},{4,20},{5,21},{6,22},{7,23},{8,24},{9,... | collective-permute-start | bytes 884744 | tf_op jit(solution)/shard_map/ppermute | solution.py:552
  174.8 12.3 %collective-permute-start.40 = (bf16[96,768]{1,0:T(8,128)(2,1)S(1)}, bf16[96,768]{1,0:T(8,128)(2,1)S(1)}, u32[]{:S(2)}, u32[]{:S(2)}) collective-permute-start(bf16[96,768]{1,0:T(8,128)(2,1)S(1)} %get-tuple-element.163), channel_id=1, source_target_pairs={{0,24},{1,25},{2,26},{3,27},{4,28},{5,29},{6,30},{7,31},{8,0},{9,1... | collective-permute-start | bytes 442376 | tf_op jit(solution)/shard_map/ppermute | solution.py:552
  185.3 18.4 %collective-permute-start.38 = (bf16[128,768]{1,0:T(8,128)(2,1)S(1)}, bf16[128,768]{1,0:T(8,128)(2,1)S(1)}, u32[]{:S(2)}, u32[]{:S(2)}) collective-permute-start(bf16[128,768]{1,0:T(8,128)(2,1)S(1)} %get-tuple-element.157), channel_id=1, source_target_pairs={{0,16},{1,17},{2,18},{3,19},{4,20},{5,21},{6,22},{7,23},{8,24},{9,... | collective-permute-start | bytes 589832 | tf_op jit(solution)/shard_map/ppermute | solution.py:552
  186.4 17.3 %collective-permute-start.39 = (bf16[128,768]{1,0:T(8,128)(2,1)S(1)}, bf16[128,768]{1,0:T(8,128)(2,1)S(1)}, u32[]{:S(2)}, u32[]{:S(2)}) collective-permute-start(bf16[128,768]{1,0:T(8,128)(2,1)S(1)} %get-tuple-element.158), channel_id=1, source_target_pairs={{0,8},{1,9},{2,10},{3,11},{4,12},{5,13},{6,14},{7,15},{8,16},{9,17... | collective-permute-start | bytes 589832 | tf_op jit(solution)/shard_map/ppermute | solution.py:552
  (36 other events, 199.6 us)
